TPU v7x, 512 devices: a whole 4x4x16 slice. The times are simulated.
512 devices in a mesh: member: 32 (over z_hi, x, y), domain: 16 (over z_lo, core).
Axes of the slice: x: 4, y: 4, z: 16 (z_hi: 2, z_lo: 8; z = z_hi * 8 + z_lo), core: 2. Of those that a mesh axis runs over, the one named last changes fastest.
Arguments:
- ensemble: bfloat16 [1024, 2, 64, 2048], P('member', None, None, 'domain'), may hold values from -4 to 4
- obs_value: float32 [32, 4096], P('member', 'domain'), may hold values from -6 to 6
- obs_prec: float32 [32, 4096], P('member', 'domain'), may hold values from 1 to 10
- obs_row: int32 [32, 4096], P('member', 'domain'), may hold values from 0 to 1
- obs_col: int32 [32, 4096], P('member', 'domain'), may hold values from 0 to 127
- loc_mask: int32 [32, 64], P('member', 'domain'), may hold values 0 or 1
Outputs:
- analysis: bfloat16 [1024, 2, 64, 2048], P('member', None, None, 'domain')
All inputs are finite; a program needn't handle non-finite values. No bound on the sum of `loc_mask` on one device may be relied on, other than what follows from the above.
Results may differ from a plain program's by a relative error of at most 0.0075.
Values may be sent and summed in bfloat16 or wider, within the bound.
No kernel may reach another device: no remote copies, remote signals or barrier semaphores. Data moves between devices by JAX's collectives and lax.ppermute only.
A program may use at most 64 MiB of HBM per device.

v0:
```python
import jax
import jax.numpy as jnp
from jax import lax
from jax.sharding import PartitionSpec as P

ADVECT = 0.4
DIFFUSE = 0.15
OBS_WIND = 0.5


def padded(cells, sides, width):
    for axis, dim in sides:
        count = lax.axis_size(axis)
        head = lax.slice_in_dim(cells, 0, width, axis=dim)
        tail = lax.slice_in_dim(cells, cells.shape[dim] - width, cells.shape[dim], axis=dim)
        cells = jnp.concatenate(
            [
                lax.ppermute(tail, axis, [(i, (i + 1) % count) for i in range(count)]),
                cells,
                lax.ppermute(head, axis, [((i + 1) % count, i) for i in range(count)]),
            ],
            axis=dim,
        )
    return cells


def step_forward(central_cell, east_cells, west_cells, north_cells, south_cells):
    middle = central_cell.astype(jnp.float32)
    east_side = east_cells.astype(jnp.float32)
    west_side = west_cells.astype(jnp.float32)
    laplace = (
        east_side
        + west_side
        + north_cells.astype(jnp.float32)
        + south_cells.astype(jnp.float32)
        - 4.0 * middle
    )
    wind_field = middle[:, 0:1]
    return (
        middle - ADVECT * 0.5 * wind_field * (east_side - west_side) + DIFFUSE * laplace
    ).astype(jnp.bfloat16)


def observe(local_region, obs_index, observed, precision):
    member_states = local_region.shape[0]
    wind_field = local_region[:, 0].reshape(member_states, -1)
    tracer = local_region[:, 1].reshape(member_states, -1)
    equivalent = jnp.take(tracer, obs_index, axis=1).astype(jnp.float32) + OBS_WIND * jnp.take(
        wind_field, obs_index, axis=1
    ).astype(jnp.float32)
    central_cell = jnp.mean(equivalent, axis=0)
    scaled = (equivalent - central_cell) * (member_states - 1) ** (-0.5)
    return jnp.concatenate(
        [scaled, (observed - central_cell)[None], precision[None]], axis=0
    ).astype(jnp.bfloat16)


def block_weights(local_rows, block_mask, parts):
    member_states = local_rows.shape[0] - 2
    tapering = jnp.array([0.5, 1.0, 1.0, 0.5], jnp.float32) * block_mask.astype(jnp.float32)
    block_cols = local_rows.shape[1] // len(parts)
    factor = jnp.repeat(tapering[jnp.array(parts)], block_cols)
    return local_rows[member_states + 1].astype(jnp.float32) * factor


def contributions(local_rows, weight):
    member_states = local_rows.shape[0] - 2
    anomaly_obs = local_rows[:member_states]
    innovation = local_rows[member_states].astype(jnp.float32)
    weighted = (anomaly_obs.astype(jnp.float32) * weight).astype(jnp.bfloat16)
    cross_term = lax.dot_general(
        weighted, anomaly_obs, (((1,), (1,)), ((), ())), preferred_element_type=jnp.float32
    )
    forcing = jnp.dot(weighted.astype(jnp.float32), innovation, precision=lax.Precision.HIGHEST)
    return (cross_term, forcing)


def analyse(local_region, cross_term, forcing):
    member_states = local_region.shape[0]
    cells = local_region.reshape(member_states, -1)
    ens_mean = jnp.mean(cells.astype(jnp.float32), axis=0)
    anomalies = (cells.astype(jnp.float32) - ens_mean).astype(jnp.bfloat16)
    identity = jnp.eye(member_states, dtype=jnp.float32)
    cross_half = cross_term.astype(jnp.bfloat16)
    squared = jnp.dot(cross_half, cross_half, preferred_element_type=jnp.float32)
    row_bound = jnp.sqrt(jnp.max(jnp.sum(jnp.abs(squared), axis=1)))
    half_width = (row_bound + 1.0) / 2.0
    theta = 1.0 + half_width
    ratio_sigma = theta / half_width
    rho_first = 1.0 / ratio_sigma
    first_resid = (1.0 - 1.0 / theta) * identity - cross_term / theta
    first_step = first_resid / theta
    applied = first_step + ((theta - 1.0) * cross_term - squared) / (theta * theta)
    second_resid = first_resid - applied
    rho_second = 1.0 / (2.0 * ratio_sigma - rho_first)
    second_step = rho_second * rho_first * first_step + 2.0 * rho_second / half_width * second_resid
    inverse = identity / theta + first_step + second_step
    mean_weights = jnp.dot(inverse, forcing, precision=lax.Precision.HIGHEST)
    transform = (
        0.5 * (identity + inverse) + mean_weights[:, None] * (member_states - 1) ** (-0.5)
    ).astype(jnp.bfloat16)
    increment = lax.dot_general(
        transform, anomalies, (((0,), (0,)), ((), ())), preferred_element_type=jnp.float32
    )
    return (ens_mean + increment).astype(jnp.bfloat16).reshape(local_region.shape)


def on_device(ensemble, obs_value, obs_prec, obs_row, obs_col, loc_mask):
    padded_region = padded(ensemble, (("domain", 3),), 1)
    central_cell = padded_region[..., 1:-1]
    predicted_state = step_forward(
        central_cell,
        padded_region[..., 2:],
        padded_region[..., :-2],
        jnp.roll(central_cell, -1, axis=2),
        jnp.roll(central_cell, 1, axis=2),
    )
    local_region = lax.all_to_all(
        predicted_state, "member", split_axis=2, concat_axis=0, tiled=True
    )
    obs_index = obs_row[0] * local_region.shape[3] + obs_col[0]
    stacked = observe(local_region, obs_index, obs_value[0], obs_prec[0])
    half_cols = stacked.shape[1] // 2
    own_weight = block_weights(stacked, loc_mask[0], [1, 2])
    own_cross, own_forcing = contributions(stacked, own_weight)
    local_rows = padded(stacked, (("domain", 1),), half_cols)
    rim_rows = jnp.concatenate([local_rows[:, :half_cols], local_rows[:, -half_cols:]], axis=1)
    rim_weight = block_weights(rim_rows, loc_mask[0], [0, 3])
    rim_cross, rim_forcing = contributions(rim_rows, rim_weight)
    cross_term = own_cross + rim_cross
    forcing = own_forcing + rim_forcing
    analysis = analyse(local_region, cross_term, forcing)
    return lax.all_to_all(analysis, "member", split_axis=0, concat_axis=2, tiled=True)


def solution(mesh):
    in_specs = (
        P("member", None, None, "domain"),
        P("member", "domain"),
        P("member", "domain"),
        P("member", "domain"),
        P("member", "domain"),
        P("member", "domain"),
    )
    out_specs = P("member", None, None, "domain")
    return jax.shard_map(
        on_device, mesh=mesh, in_specs=in_specs, out_specs=out_specs, check_vma=False
    )
```

profile of v0, /device:TPU:40, one launch (start us, length us, event | category | flops | bytes accessed | tf_op | source)
XLA Modules:
  0.0 203.2 jit_solution(1559509797896157785)
XLA Ops:
  0.0 2.1 %fusion.30 = (bf16[32,2,64,1]{3,2,1,0:T(8,128)(2,1)S(1)}, bf16[32,2,64,1]{3,2,1,0:T(8,128)(2,1)S(1)}) fusion(bf16[32,2,64,128]{3,2,1,0:T(8,128)(2,1)} %param.12), kind=kLoop, calls=%fused_computation.71 | loop fusion | bytes 32768 | tf_op jit(solution)/shard_map/slice | solution.py:14
  2.6 1.9 collective-permute-start
  5.0 2.4 %collective-permute-start.1 = (bf16[32,2,64,1]{2,0,3,1:T(8,128)(2,1)S(1)}, bf16[32,2,64,1]{2,0,3,1:T(8,128)(2,1)S(1)}, u32[]{:S(2)}, u32[]{:S(2)}) collective-permute-start(bf16[32,2,64,1]{2,0,3,1:T(8,128)(2,1)S(1)} %copy.108), channel_id=1, source_target_pairs={{0,1},{1,2},{2,3},{3,4},{4,5},{5,6},{6,7},{7,8},{8,9},{9,10},{10,1... | collective-permute-start | bytes 24584 | tf_op jit(solution)/shard_map/ppermute | solution.py:18
  7.4 0.7 copy_convert_fusion
  8.1 1.8 fusion.29
  10.1 1.7 copy.84
  11.8 2.6 %copy.86 = bf16[32,2,64,1]{3,0,1,2:T(8,128)(2,1)} copy(bf16[32,2,64,1]{2,0,3,1:T(8,128)(2,1)S(1)} %collective-permute-done.1) | data formatting | bytes 16384 | tf_op jit(solution)/shard_map/ppermute | solution.py:18
  14.4 4.3 %fusion.3 = bf16[32,2,64,128]{3,0,1,2:T(8,128)(2,1)} fusion(bf16[32,2,64,128]{3,0,1,2:T(8,128)(2,1)S(1)} %get-tuple-element.9, bf16[32,2,64,1]{3,0,1,2:T(8,128)(2,1)} %copy.86, bf16[32,2,64,1]{3,0,1,2:T(8,128)(2,1)S(1)} %copy.84, bf16[32,2,1,128]{3,0,1,2:T(8,128)(2,1)S(1)} %get-tuple-element.11, bf16[32,2,63,128]{3,0,1,2:T(8,128)(2,1)} %get-tuple-element.13, ...), kind=kLoop, calls=%fused_computation.14 | loop fusion | flops 14680064 | bytes 5259264 | tf_op jit(solution)/shard_map/convert_element_type | solution.py:41
  18.8 19.9 %all-to-all-start = ((bf16[32,2,64,128]{3,0,1,2:T(8,128)(2,1)}), bf16[32,2,64,128]{3,0,1,2:T(8,128)(2,1)S(1)}, u32[]{:S(2)}, u32[]{:S(2)}) async-start(bf16[32,2,64,128]{3,0,1,2:T(8,128)(2,1)} %fusion.3), calls=%async_computation | async-start | bytes 2097152 | tf_op jit(solution)/shard_map/all_to_all | solution.py:118
  38.7 0.6 gather_fusion
  39.6 0.6 gather_fusion.1
  40.5 57.5 %all-to-all-done = bf16[32,2,64,128]{3,0,1,2:T(8,128)(2,1)S(1)} async-done(((bf16[32,2,64,128]{3,0,1,2:T(8,128)(2,1)}), bf16[32,2,64,128]{3,0,1,2:T(8,128)(2,1)S(1)}, u32[]{:S(2)}, u32[]{:S(2)}) %all-to-all-start) | async-done | bytes 1048608 | tf_op jit(solution)/shard_map/all_to_all | solution.py:118
  98.6 1.2 gather_fusion.2
  99.8 1.2 gather_fusion.3
  102.2 2.8 %fusion.17 = f32[1024,1024]{1,0:T(8,128)} fusion(bf16[1024,256]{0,1:T(8,128)(2,1)S(1)} %multiply_convert_fusion.2, f32[256]{0:T(256)S(1)} %bitcast.51), kind=kOutput, calls=%fused_computation.37 | convolution fusion | flops 537657344 | bytes 4719616 | tf_op jit(solution)/shard_map/dot_general | solution.py:71
  105.3 0.9 fusion.31
  106.1 1.9 collective-permute-start.2
  108.0 3.8 %collective-permute-start.3 = (bf16[1026,128]{0,1:T(8,128)(2,1)}, bf16[1026,128]{0,1:T(8,128)(2,1)S(1)}, u32[]{:S(2)}, u32[]{:S(2)}) collective-permute-start(bf16[1026,128]{0,1:T(8,128)(2,1)} %get-tuple-element.16), channel_id=1, source_target_pairs={{1,0},{2,1},{3,2},{4,3},{5,4},{6,5},{7,6},{8,7},{9,8},{10,9},{11,1... | collective-permute-start | bytes 787976 | tf_op jit(solution)/shard_map/ppermute | solution.py:20
  112.1 0.8 copy.100
  112.9 2.7 %reshape.50 = f32[1024,512]{1,0:T(8,128)} reshape(f32[32,32,2,2,128]{4,3,2,1,0:T(2,128)S(1)} %copy.100) | data formatting | bytes 4194304 | tf_op jit(solution)/shard_map/convert_element_type | solution.py:81
  115.7 1.9 copy.101
  117.6 1.0 constant_dynamic-update-slice_fusion.1
  118.9 3.0 %convolution_add_fusion = f32[1024,1024]{1,0:T(8,128)S(1)} fusion(f32[1024,1024]{1,0:T(8,128)} %fusion.17, f32[256]{0:T(256)S(1)} %multiply_reduce_fusion, bf16[1026,256]{0,1:T(8,128)(2,1)S(1)} %constant_dynamic-update-slice_fusion), kind=kOutput, calls=%fused_computation.10 | convolution fusion | flops 538705920 | bytes 9438208 | tf_op jit(solution)/shard_map/dot_general | solution.py:71
  122.0 4.4 %abs_reduce_fusion = (f32[1024]{0:T(1024)S(1)}, f32[1024,1024]{0,1:T(8,128)}) fusion(f32[1024,1024]{1,0:T(8,128)S(1)} %convolution_add_fusion), kind=kOutput, calls=%fused_computation.6 | convolution fusion | flops 2150628352 | bytes 8392704 | tf_op jit(solution)/shard_map/dot_general | solution.py:85
  126.4 0.6 reduce_max.9
  128.2 5.4 %copy.99 = f32[1024,1024]{1,0:T(8,128)} copy(f32[1024,1024]{0,1:T(8,128)} %get-tuple-element.21) | data formatting | bytes 8388608 | tf_op jit(solution)/shard_map/dot_general | solution.py:85
  133.6 4.6 %add_add_fusion = f32[1024,1024]{1,0:T(8,128)S(1)} fusion(f32[1024,1024]{1,0:T(8,128)} %copy.99, f32[1024,1024]{1,0:T(8,128)} %copy-done, f32[]{:T(128)S(6)} %mul.165, f32[]{:T(128)S(6)} %div.60, f32[]{:T(128)S(6)} %div.69, f32[]{:T(128)S(6)} %mul.158, f32[]{:T(128)S(6)} %add.91, f32[]{:T(128)S(6)} %sub.49, f32[]{:T(128)S(6)} %divide.4), kind=kLoop, calls=%fused_computation.5 | loop fusion | flops 16777216 | bytes 12582940 | tf_op jit(solution)/shard_map/add | solution.py:97
  138.2 3.6 %fusion.33 = f32[1,1024]{1,0:T(1,128)S(1)} fusion(f32[1024,1024]{1,0:T(8,128)S(1)} %add_add_fusion, f32[1024,1]{0,1:T(1,128)S(1)} %bitcast.48), kind=kOutput, calls=%fused_computation.74 | convolution fusion | flops 12582912 | bytes 4202496 | tf_op jit(solution)/shard_map/dot_general | solution.py:98
  141.9 2.4 %add_convert_fusion.2 = bf16[1024,512]{0,1:T(8,128)(2,1)} fusion(f32[1024,1024]{1,0:T(8,128)S(1)} %add_add_fusion, f32[1024]{0:T(1024)S(1)} %broadcast_multiply_fusion, f32[1024,512]{0,1:T(8,128)S(1)} %copy.101, f32[512]{0:T(512)S(1)} %bitcast.57), kind=kOutput, calls=%fused_computation.20 | convolution fusion | flops 1082130432 | bytes 7346176 | tf_op jit(solution)/shard_map/dot_general | solution.py:102
  144.3 2.4 %copy.102 = bf16[1024,2,2,128]{3,2,1,0:T(2,128)(2,1)S(1)} copy(bf16[1024,2,2,128]{0,3,2,1:T(8,128)(2,1)} %bitcast.47) | data formatting | bytes 2097152 | tf_op jit(solution)/shard_map/reshape | solution.py:105
  146.7 54.8 %all_to_all.36 = bf16[1024,2,2,128]{3,2,1,0:T(2,128)(2,1)S(1)} all-to-all(bf16[1024,2,2,128]{3,2,1,0:T(2,128)(2,1)S(1)} %copy.102), channel_id=1, replica_groups=mesh['member'=32,'domain'=16] {'member'}, dimensions={0} | all-to-all | bytes 2097152 | tf_op jit(solution)/shard_map/all_to_all | solution.py:133
  201.9 1.4 copy.105
  (61 shorter events, 4.7 us)
Async XLA Ops:
  0.0 7.4 %copy-start.1 = (bf16[32,2,64,128]{3,2,1,0:T(8,128)(2,1)S(1)}, bf16[32,2,64,128]{3,2,1,0:T(8,128)(2,1)}, u32[]{:S(2)}) copy-start(bf16[32,2,64,128]{3,2,1,0:T(8,128)(2,1)} %param.12) | copy-start | bytes 3145732
  2.6 7.5 %collective-permute-start = (bf16[32,2,64,1]{2,0,3,1:T(8,128)(2,1)S(1)}, bf16[32,2,64,1]{2,0,3,1:T(8,128)(2,1)S(1)}, u32[]{:S(2)}, u32[]{:S(2)}) collective-permute-start(bf16[32,2,64,1]{2,0,3,1:T(8,128)(2,1)S(1)} %copy.107), channel_id=1, source_target_pairs={{1,0},{2,1},{3,2},{4,3},{5,4},{6,5},{7,6},{8,7},{9,8},{10,9},{11,1... | collective-permute-start | bytes 24584 | tf_op jit(solution)/shard_map/ppermute | solution.py:20
  5.0 6.9 %collective-permute-start.1 = (bf16[32,2,64,1]{2,0,3,1:T(8,128)(2,1)S(1)}, bf16[32,2,64,1]{2,0,3,1:T(8,128)(2,1)S(1)}, u32[]{:S(2)}, u32[]{:S(2)}) collective-permute-start(bf16[32,2,64,1]{2,0,3,1:T(8,128)(2,1)S(1)} %copy.108), channel_id=1, source_target_pairs={{0,1},{1,2},{2,3},{3,4},{4,5},{5,6},{6,7},{7,8},{8,9},{9,10},{10,1... | collective-permute-start | bytes 24584 | tf_op jit(solution)/shard_map/ppermute | solution.py:18
  14.4 24.3 %copy-start.6 = (s32[2]{0:T(128)S(1)}, s32[2]{0:T(128)}, u32[]{:S(2)}) copy-start(s32[2]{0:T(128)} %constant.67) | copy-start | bytes 28
  14.4 24.3 %copy-start.7 = (s32[1,4]{1,0:T(1,128)S(1)}, s32[1,4]{1,0:T(1,128)}, u32[]{:S(2)}) copy-start(s32[1,4]{1,0:T(1,128)} %param.17) | copy-start | bytes 52
  14.4 24.3 %copy-start.8 = (f32[1,4]{1,0:T(1,128)S(1)}, f32[1,4]{1,0:T(1,128)}, u32[]{:S(2)}) copy-start(f32[1,4]{1,0:T(1,128)} %constant.66) | copy-start | bytes 52
  14.4 25.0 %copy-start.5 = (f32[1,256]{1,0:T(1,128)S(1)}, f32[1,256]{1,0:T(1,128)}, u32[]{:S(2)}) copy-start(f32[1,256]{1,0:T(1,128)} %param.14) | copy-start | bytes 3076
  14.4 26.0 %copy-start.2 = (s32[1,256]{1,0:T(1,128)S(1)}, s32[1,256]{1,0:T(1,128)}, u32[]{:S(2)}) copy-start(s32[1,256]{1,0:T(1,128)} %param.16) | copy-start | bytes 3076
  14.4 26.0 %copy-start.3 = (s32[1,256]{1,0:T(1,128)S(1)}, s32[1,256]{1,0:T(1,128)}, u32[]{:S(2)}) copy-start(s32[1,256]{1,0:T(1,128)} %param.15) | copy-start | bytes 3076
  18.8 79.3 %all-to-all-start = ((bf16[32,2,64,128]{3,0,1,2:T(8,128)(2,1)}), bf16[32,2,64,128]{3,0,1,2:T(8,128)(2,1)S(1)}, u32[]{:S(2)}, u32[]{:S(2)}) async-start(bf16[32,2,64,128]{3,0,1,2:T(8,128)(2,1)} %fusion.3), calls=%async_computation | async-start | bytes 2097152 | tf_op jit(solution)/shard_map/all_to_all | solution.py:118
  99.8 2.0 copy-start.4
  106.1 11.5 %collective-permute-start.2 = (bf16[1026,128]{0,1:T(8,128)(2,1)}, bf16[1026,128]{0,1:T(8,128)(2,1)}, u32[]{:S(2)}, u32[]{:S(2)}) collective-permute-start(bf16[1026,128]{0,1:T(8,128)(2,1)} %get-tuple-element.17), channel_id=1, source_target_pairs={{0,1},{1,2},{2,3},{3,4},{4,5},{5,6},{6,7},{7,8},{8,9},{9,10},{10,1... | collective-permute-start | bytes 787976 | tf_op jit(solution)/shard_map/ppermute | solution.py:18
  108.0 10.5 %collective-permute-start.3 = (bf16[1026,128]{0,1:T(8,128)(2,1)}, bf16[1026,128]{0,1:T(8,128)(2,1)S(1)}, u32[]{:S(2)}, u32[]{:S(2)}) collective-permute-start(bf16[1026,128]{0,1:T(8,128)(2,1)} %get-tuple-element.16), channel_id=1, source_target_pairs={{1,0},{2,1},{3,2},{4,3},{5,4},{6,5},{7,6},{8,7},{9,8},{10,9},{11,1... | collective-permute-start | bytes 787976 | tf_op jit(solution)/shard_map/ppermute | solution.py:20
  122.0 4.4 %copy-start = (f32[1024,1024]{1,0:T(8,128)}, f32[1024,1024]{1,0:T(8,128)S(1)}, u32[]{:S(2)}) copy-start(f32[1024,1024]{1,0:T(8,128)S(1)} %convolution_add_fusion) | copy-start | bytes 12582916
where the time goes:
time: 204 us; the launch traced here: 203 us
  waiting for transfers between devices  57.5 us (28%)
  blocking collectives  54.8 us (27%)
  local copies, waits for them, and re-layouts  31.3 us (15%)
  starting transfers between devices  29.9 us (15%)
  matrix products  16.9 us (8%)
  other arithmetic  11.5 us (6%)
    all_to_all x1, waiting for transfers between devices, on_device(): lax.all_to_all(predicted_state, 'member', split_axis=2, concat_axis=0, ti...  57.5 us
    all_to_all x1, blocking collectives, on_device(): lax.all_to_all(analysis, 'member', split_axis=0, concat_axis=2, tiled=True)  54.8 us
    all_to_all x1, starting transfers between devices, on_device(): lax.all_to_all(predicted_state, 'member', split_axis=2, concat_axis=0, ti...  19.9 us
    dot_general x2, matrix products, contributions(): lax.dot_general(weighted, anomaly_obs, (((1,), (1,)), ((), ())), preferre...  5.8 us
    ppermute x2, starting transfers between devices, padded(): lax.ppermute(head, axis, [((i + 1) % count, i) for i in range(count)])  5.74 us
    convert_element_type x3, local copies, waits for them, and re-layouts, analyse(): ens_mean = jnp.mean(cells.astype(jnp.float32), axis=0)  5.44 us
    dot_general x1, local copies, waits for them, and re-layouts, analyse(): jnp.dot(cross_half, cross_half, preferred_element_type=jnp.float32)  5.39 us
    add x1, other arithmetic, analyse(): inverse = identity / theta + first_step + second_step  4.61 us
  transfers between devices with their start and end apart: 5, of which 1 were waited for; matrix products, arithmetic and copies ran while one was open for 7% of the time, Pallas kernels for 0%

commit v1 on v0

v1 whole, which is shorter than its diff:
```python
import jax
import jax.numpy as jnp
from jax import lax
from jax.experimental import pallas as pl
from jax.experimental.pallas import tpu as pltpu
from jax.sharding import PartitionSpec as P

ADVECT = 0.4
DIFFUSE = 0.15
OBS_WIND = 0.5
F32 = jnp.float32
BF16 = jnp.bfloat16
VMEM = pl.BlockSpec(memory_space=pltpu.VMEM)
SMEM = pl.BlockSpec(memory_space=pltpu.SMEM)
PARAMS = pltpu.CompilerParams(vmem_limit_bytes=40 * 1024 * 1024)


def call(kernel, shapes, args, scratch=(), specs=None, flops=0):
    nbytes = sum(a.size * a.dtype.itemsize for a in args)
    return pl.pallas_call(
        kernel,
        out_shape=shapes,
        in_specs=specs or [VMEM] * len(args),
        out_specs=jax.tree.map(lambda _: VMEM, shapes),
        scratch_shapes=list(scratch),
        compiler_params=PARAMS,
        cost_estimate=pl.CostEstimate(flops=flops, bytes_accessed=nbytes, transcendentals=0),
    )(*args)


def iota(shape, dim):
    return lax.broadcasted_iota(jnp.int32, shape, dim)


def to_col(row):
    n = row.shape[1]
    return jnp.sum(jnp.where(iota((n, n), 0) == iota((n, n), 1), row, 0.0), axis=1, keepdims=True)


def to_row(col):
    n = col.shape[0]
    return jnp.sum(jnp.where(iota((n, n), 0) == iota((n, n), 1), col, 0.0), axis=0, keepdims=True)


def edge_kernel(ens_ref, head_ref, tail_ref):
    pick = jnp.where(
        (iota((8, 128), 0) == 0) & (iota((8, 128), 1) == 0)
        | (iota((8, 128), 0) == 1) & (iota((8, 128), 1) == 127),
        1.0,
        0.0,
    ).astype(BF16)
    members = ens_ref.shape[0] // 8
    for k in range(8):
        rows = ens_ref[k * members : (k + 1) * members].reshape(-1, 128)
        edges = lax.dot_general(pick, rows, (((1,), (1,)), ((), ())), preferred_element_type=F32)
        head_ref[k : k + 1, :] = edges[0:1]
        tail_ref[k : k + 1, :] = edges[1:2]


def forecast_kernel(ens_ref, west_ref, east_ref, out_ref, store):
    members, _, rows, cols = ens_ref.shape
    group = members // 8
    spot = iota((8, cols), 0)
    lane8 = iota((8, cols), 1)
    pick = jnp.where((spot == 0) & (lane8 == 0) | (spot == 1) & (lane8 == cols - 1), 1.0, 0.0).astype(BF16)

    for k in range(8):
        n = group * 2 * rows
        which = iota((8, n), 0)
        edges = jnp.where(which == 0, west_ref[k : k + 1, :], jnp.where(which == 1, east_ref[k : k + 1, :], 0.0))
        rim = lax.dot_general(
            edges.astype(BF16), pick, (((0,), (0,)), ((), ())), preferred_element_type=F32
        ).reshape(group * 2, rows, cols)
        for i in range(group):
            m = k * group + i
            wind = None
            for f in range(2):
                x = ens_ref[m, f].astype(F32)
                edge = rim[i * 2 + f]
                lane = iota((rows, cols), 1)
                east = jnp.where(lane == cols - 1, edge, pltpu.roll(x, cols - 1, 1))
                west = jnp.where(lane == 0, edge, pltpu.roll(x, 1, 1))
                north = pltpu.roll(x, rows - 1, 0)
                south = pltpu.roll(x, 1, 0)
                if f == 0:
                    wind = x
                laplace = east + west + north + south - 4.0 * x
                new = x - ADVECT * 0.5 * wind * (east - west) + DIFFUSE * laplace
                store[f, m * rows : (m + 1) * rows, :] = new
    for f in range(2):
        for r in range(rows):
            part = store[f, pl.ds(r, members, stride=rows), :]
            at = (f * 2 + r % 2) * cols
            out_ref[r // 2, :, at : at + cols] = part.astype(BF16)


def restore_kernel(in_ref, out_ref, store):
    members, _, rows, cols = out_ref.shape
    for f in range(2):
        for r in range(rows):
            at = (f * 2 + r % 2) * cols
            store[f, pl.ds(r, members, stride=rows), :] = in_ref[r // 2, :, at : at + cols].astype(F32)
    for f in range(2):
        for m in range(members):
            out_ref[m, f] = store[f, m * rows : (m + 1) * rows, :].astype(BF16)


def observe_kernel(local_ref, index_ref, value_ref, prec_ref, y_ref, head_ref, tail_ref):
    members, cells = local_ref.shape
    half = cells // 2
    equivalent = local_ref[:, half:].astype(F32) + OBS_WIND * local_ref[:, :half].astype(F32)
    mean = jnp.sum(equivalent, axis=0, keepdims=True) * (1.0 / members)
    y = ((equivalent - mean) * (members - 1) ** (-0.5)).astype(BF16)
    y_ref[...] = y
    n = index_ref.shape[1]
    hit = iota((half, n), 0) == index_ref[...]
    rows = jnp.dot(y, hit.astype(BF16), preferred_element_type=F32).astype(BF16)
    observed_mean = jnp.sum(jnp.where(hit, to_col(mean), 0.0), axis=0, keepdims=True)
    innovation = value_ref[...] - observed_mean
    which = iota((16, n), 0)
    last = jnp.where(which == 0, innovation, jnp.where(which == 1, prec_ref[...], 0.0)).astype(BF16)
    for ref, at in ((head_ref, 0), (tail_ref, n // 2)):
        ref[:members, :] = rows[:, at : at + n // 2]
        ref[members:, :] = last[:, at : at + n // 2]


def own_kernel(local_ref, y_ref, anomaly_ref, yt_ref, mean_ref, gram_ref, cover_ref):
    members, cells = local_ref.shape
    local = local_ref[...].astype(F32)
    mean = jnp.sum(local, axis=0, keepdims=True) * (1.0 / members)
    mean_ref[...] = jnp.broadcast_to(mean, mean_ref.shape)
    anomaly_ref[...] = (local - mean).astype(BF16)
    yt_ref[...] = y_ref[...].T
    gram_ref[...] = jnp.dot(yt_ref[...], y_ref[...], preferred_element_type=F32)
    cover_ref[...] = jnp.dot(yt_ref[...], anomaly_ref[...], preferred_element_type=F32)


def analyse_kernel(
    mask_ref, anomaly_ref, y_ref, yt_ref, mean_ref, gram_ref, cover_ref, left_ref, right_ref,
    index_ref, value_ref, prec_ref, out_ref, z, zt, gram, cover, u,
):
    members, cells = anomaly_ref.shape
    half = cells // 2
    quarter = half // 2
    n = index_ref.shape[1]

    z[:, :half] = y_ref[...]
    z[:, half : half + quarter] = left_ref[:members, :]
    z[:, half + quarter :] = right_ref[:members, :]
    zt[:half, :] = yt_ref[...]
    zt[half:, :] = z[:, half:].T
    rim = jnp.dot(zt[half:, :], z[...], preferred_element_type=F32)
    cross = jnp.dot(yt_ref[...], z[:, half:], preferred_element_type=F32)
    gram[:half, :half] = gram_ref[...]
    gram[:half, half:] = cross
    gram[half:, :] = rim
    cover[:half, :] = cover_ref[...]
    cover[half:, :] = jnp.dot(zt[half:, :], anomaly_ref[...], preferred_element_type=F32)

    mask = [mask_ref[0, b].astype(F32) for b in range(4)]
    hit = iota((half, n), 0) == index_ref[...]
    mean = mean_ref[0:1, :]
    cell_mean = to_col(mean[:, half:] + OBS_WIND * mean[:, :half])
    observed_mean = jnp.sum(jnp.where(hit, cell_mean, 0.0), axis=0, keepdims=True)
    innovation = (value_ref[...] - observed_mean).astype(BF16).astype(F32)
    weight = prec_ref[...].astype(BF16).astype(F32) * jnp.where(iota((1, n), 1) < n // 2, mask[1], mask[2])
    own_d = jnp.sum(jnp.where(hit, weight, 0.0), axis=1, keepdims=True)
    own_g = jnp.sum(jnp.where(hit, weight * innovation, 0.0), axis=1, keepdims=True)
    left_tail = left_ref[members : members + 16, :].astype(F32)
    right_tail = right_ref[members : members + 16, :].astype(F32)
    left_d = left_tail[1:2, :] * (0.5 * mask[0])
    right_d = right_tail[1:2, :] * (0.5 * mask[3])
    left_g = left_d * left_tail[0:1, :]
    right_g = right_d * right_tail[0:1, :]
    d_row = jnp.concatenate([to_row(own_d), left_d, right_d], axis=1)
    g_row = jnp.concatenate([to_row(own_g), left_g, right_g], axis=1)
    d_col = jnp.concatenate([own_d, to_col(left_d), to_col(right_d)], axis=0)
    g_col = jnp.concatenate([own_g, to_col(left_g), to_col(right_g)], axis=0)

    k = gram[...]
    m = cover[...]
    inner = (k * d_col * d_row).astype(BF16)
    u[...] = jnp.dot(z[...], inner, preferred_element_type=F32).astype(BF16)
    most = jnp.zeros((1, 1), F32)
    step = 256
    for i in range(members // step):
        squared = jnp.dot(u[i * step : (i + 1) * step, :], zt[...], preferred_element_type=F32)
        total = jnp.sum(jnp.abs(squared), axis=1, keepdims=True)
        most = jnp.maximum(most, jnp.max(total, axis=0, keepdims=True))
    row_bound = jnp.sqrt(most)
    half_width = (row_bound + 1.0) / 2.0
    theta = 1.0 + half_width
    ratio_sigma = theta / half_width
    rho_first = 1.0 / ratio_sigma
    rho_second = 1.0 / (2.0 * ratio_sigma - rho_first)
    resid_one = 1.0 - 1.0 / theta
    step_one = resid_one / theta
    step_cross = -1.0 / (theta * theta)
    second_one = resid_one - step_one
    second_cross = -1.0 / theta - step_cross - (theta - 1.0) / (theta * theta)
    first_rate = rho_second * rho_first
    second_rate = 2.0 * rho_second / half_width
    to_one = 1.0 / theta + step_one + first_rate * step_one + second_rate * second_one
    to_cross = step_cross + first_rate * step_cross + second_rate * second_cross
    to_square = second_rate / (theta * theta)

    dm = m * d_col
    kdm = jnp.dot(k.astype(BF16), dm.astype(BF16), preferred_element_type=F32)
    gain = (0.5 * to_cross * dm + (0.5 * to_square * d_col) * kdm).astype(BF16)
    once_row = d_row * jnp.sum(k * g_col, axis=0, keepdims=True)
    once_col = d_col * jnp.sum(k * g_row, axis=1, keepdims=True)
    twice_col = d_col * jnp.sum(k * once_row, axis=1, keepdims=True)
    force = to_one * g_col + to_cross * once_col + to_square * twice_col
    shift = mean + jnp.sum(force * m, axis=0, keepdims=True) * (members - 1) ** (-0.5)
    keep = 0.5 * (1.0 + to_one)
    for i in range(members // step):
        at = pl.ds(i * step, step)
        out_ref[at, :] = (
            shift
            + keep * anomaly_ref[at, :].astype(F32)
            + jnp.dot(z[at, :], gain, preferred_element_type=F32)
        ).astype(BF16)


def on_device(ensemble, obs_value, obs_prec, obs_row, obs_col, loc_mask):
    members, fields, rows, cols = ensemble.shape
    bands = lax.axis_size("member")
    domains = lax.axis_size("domain")
    total = members * bands
    cells = fields * (rows // bands) * cols
    n = obs_value.shape[1]
    to_right = [(i, (i + 1) % domains) for i in range(domains)]
    to_left = [((i + 1) % domains, i) for i in range(domains)]
    struct = jax.ShapeDtypeStruct

    edge = struct((8, members // 8 * fields * rows), F32)
    head, tail = call(edge_kernel, [edge, edge], [ensemble])
    west = lax.ppermute(tail, "domain", to_right)
    east = lax.ppermute(head, "domain", to_left)
    predicted = call(
        forecast_kernel,
        struct((bands, members, cells), BF16),
        [ensemble, west, east],
        scratch=[pltpu.VMEM((fields, members * rows, cols), F32)],
    )
    local = lax.all_to_all(predicted, "member", split_axis=0, concat_axis=0, tiled=True).reshape(total, cells)

    index = obs_row * cols + obs_col
    rim = struct((total + 16, n // 2), BF16)
    y, head_rows, tail_rows = call(
        observe_kernel,
        [struct((total, cells // 2), BF16), rim, rim],
        [local, index, obs_value, obs_prec],
    )
    left = lax.ppermute(tail_rows, "domain", to_right)
    right = lax.ppermute(head_rows, "domain", to_left)
    anomalies, yt, mean, gram, cover = call(
        own_kernel,
        [
            struct((total, cells), BF16),
            struct((cells // 2, total), BF16),
            struct((8, cells), F32),
            struct((cells // 2, cells // 2), F32),
            struct((cells // 2, cells), F32),
        ],
        [local, y],
        flops=2 * total * cells * cells * 3 // 4,
    )
    analysis = call(
        analyse_kernel,
        struct((total, cells), BF16),
        [loc_mask, anomalies, y, yt, mean, gram, cover, left, right, index, obs_value, obs_prec],
        scratch=[
            pltpu.VMEM((total, cells), BF16),
            pltpu.VMEM((cells, total), BF16),
            pltpu.VMEM((cells, cells), F32),
            pltpu.VMEM((cells, cells), F32),
            pltpu.VMEM((total, cells), BF16),
        ],
        specs=[SMEM] + [VMEM] * 11,
        flops=2 * total * total * cells * 2,
    )
    back = lax.all_to_all(
        analysis.reshape(bands, members, cells), "member", split_axis=0, concat_axis=0, tiled=True
    )
    return call(
        restore_kernel,
        struct(ensemble.shape, BF16),
        [back],
        scratch=[pltpu.VMEM((fields, members * rows, cols), F32)],
    )


def solution(mesh):
    in_specs = (
        P("member", None, None, "domain"),
        P("member", "domain"),
        P("member", "domain"),
        P("member", "domain"),
        P("member", "domain"),
        P("member", "domain"),
    )
    out_specs = P("member", None, None, "domain")
    return jax.shard_map(
        on_device, mesh=mesh, in_specs=in_specs, out_specs=out_specs, check_vma=False
    )
```

time: 204 us -> 172 us (0.84)
  the two profiles are of different devices: /device:TPU:40 before, /device:TPU:32 now
where the time goes in v1:
time: 172 us
  waiting for transfers between devices  64.7 us (38%)
  blocking collectives  60.9 us (35%)
  starting transfers between devices  30.9 us (18%)
  Pallas kernels  13.5 us (8%)
  local copies, waits for them, and re-layouts  1.9 us (1%)
    all_to_all x1, blocking collectives, on_device(): lax.all_to_all(analysis.reshape(bands, members, cells), 'member', split_a...  60.9 us
    all_to_all x1, waiting for transfers between devices, on_device(): lax.all_to_all(predicted, 'member', split_axis=0, concat_axis=0, tiled=True)  59.7 us
    all_to_all x1, starting transfers between devices, on_device(): lax.all_to_all(predicted, 'member', split_axis=0, concat_axis=0, tiled=True)  19.8 us
    pallas_call x6, Pallas kernels, call(): pl.pallas_call(kernel, out_shape=shapes, in_specs=specs or [VMEM] * len(a...  13.5 us
    ppermute x1, starting transfers between devices, on_device(): right = lax.ppermute(head_rows, 'domain', to_left)  3.64 us
    ppermute x1, starting transfers between devices, on_device(): east = lax.ppermute(head, 'domain', to_left)  3.64 us
    ppermute x1, waiting for transfers between devices, on_device(): left = lax.ppermute(tail_rows, 'domain', to_right)  3.58 us
  transfers between devices with their start and end apart: 5, of which 3 were waited for; matrix products, arithmetic and copies ran while one was open for 0% of the time, Pallas kernels for 0%

profile of v1, /device:TPU:32, one launch (start us, length us, event | category | flops | bytes accessed | tf_op | source)
XLA Modules:
  0.0 172.0 jit_solution(15502773384058327738)
XLA Ops:
  0.0 0.0 copy-start
  0.0 1.2 copy-done
  1.2 0.4 shard_map.64
  1.6 1.9 %collective-permute-start = (f32[8,512]{1,0:T(8,128)S(1)}, f32[8,512]{1,0:T(8,128)S(1)}, u32[]{:S(2)}, u32[]{:S(2)}) collective-permute-start(f32[8,512]{1,0:T(8,128)S(1)} %get-tuple-element.15), channel_id=1, source_target_pairs={{0,1},{1,2},{2,3},{3,4},{4,5},{5,6},{6,7},{7,8},{8,9},{9,10},{10,1... | collective-permute-start | bytes 49160 | tf_op jit(solution)/shard_map/ppermute | solution.py:238
  3.5 3.6 %collective-permute-start.1 = (f32[8,512]{1,0:T(8,128)S(1)}, f32[8,512]{1,0:T(8,128)S(1)}, u32[]{:S(2)}, u32[]{:S(2)}) collective-permute-start(f32[8,512]{1,0:T(8,128)S(1)} %get-tuple-element.16), channel_id=1, source_target_pairs={{1,0},{2,1},{3,2},{4,3},{5,4},{6,5},{7,6},{8,7},{9,8},{10,9},{11,1... | collective-permute-start | bytes 49160 | tf_op jit(solution)/shard_map/ppermute | solution.py:239
  7.2 0.0 collective-permute-done.west_ref
  7.2 1.4 collective-permute-done.1.east_ref
  8.6 4.0 %shard_map.65 = bf16[32,32,512]{2,1,0:T(8,128)(2,1)} custom-call(bf16[32,2,64,128]{3,2,1,0:T(8,128)(2,1)S(1)} %copy-done, f32[8,512]{1,0:T(8,128)S(1)} %collective-permute-done.west_ref, f32[8,512]{1,0:T(8,128)S(1)} %collective-permute-done.1.east_ref), custom_call_target="tpu_custom_call" | custom-call | bytes 1081344 | tf_op jit(solution)/shard_map/pallas_call | solution.py:20
  12.6 0.0 copy-start.4
  12.6 0.0 copy-start.5
  12.6 19.8 %all-to-all-start = ((bf16[32,32,512]{2,1,0:T(8,128)(2,1)}), bf16[32,32,512]{2,1,0:T(8,128)(2,1)S(1)}, u32[]{:S(2)}, u32[]{:S(2)}) async-start(bf16[32,32,512]{2,1,0:T(8,128)(2,1)} %shard_map.65), calls=%async_computation | async-start | bytes 2097152 | tf_op jit(solution)/shard_map/all_to_all | solution.py:246
  32.4 0.0 copy-done.4
  32.4 0.0 copy-done.5
  32.4 0.0 copy-start.2
  32.4 0.0 copy-start.1
  32.4 59.7 %all-to-all-done = bf16[32,32,512]{2,1,0:T(8,128)(2,1)S(1)} async-done(((bf16[32,32,512]{2,1,0:T(8,128)(2,1)}), bf16[32,32,512]{2,1,0:T(8,128)(2,1)S(1)}, u32[]{:S(2)}, u32[]{:S(2)}) %all-to-all-start) | async-done | bytes 1048608 | tf_op jit(solution)/shard_map/all_to_all | solution.py:246
  92.1 0.0 copy-done.2
  92.1 0.0 copy-done.1
  92.2 0.5 shard_map.66
  92.7 1.9 %collective-permute-start.2 = (bf16[1040,128]{1,0:T(8,128)(2,1)S(1)}, bf16[1040,128]{1,0:T(8,128)(2,1)S(1)}, u32[]{:S(2)}, u32[]{:S(2)}) collective-permute-start(bf16[1040,128]{1,0:T(8,128)(2,1)S(1)} %get-tuple-element.23), channel_id=1, source_target_pairs={{0,1},{1,2},{2,3},{3,4},{4,5},{5,6},{6,7},{7,8},{8,9},{9,10},{10,1... | collective-permute-start | bytes 798728 | tf_op jit(solution)/shard_map/ppermute | solution.py:255
  94.6 3.6 %collective-permute-start.3 = (bf16[1040,128]{1,0:T(8,128)(2,1)S(1)}, bf16[1040,128]{1,0:T(8,128)(2,1)S(1)}, u32[]{:S(2)}, u32[]{:S(2)}) collective-permute-start(bf16[1040,128]{1,0:T(8,128)(2,1)S(1)} %get-tuple-element.24), channel_id=1, source_target_pairs={{1,0},{2,1},{3,2},{4,3},{5,4},{6,5},{7,6},{8,7},{9,8},{10,9},{11,1... | collective-permute-start | bytes 798728 | tf_op jit(solution)/shard_map/ppermute | solution.py:256
  98.3 0.9 shard_map.67
  99.1 3.6 %collective-permute-done.2.left_ref = bf16[1040,128]{1,0:T(8,128)(2,1)S(1)} collective-permute-done((bf16[1040,128]{1,0:T(8,128)(2,1)S(1)}, bf16[1040,128]{1,0:T(8,128)(2,1)S(1)}, u32[]{:S(2)}, u32[]{:S(2)}) %collective-permute-start.2) | collective-permute-done | bytes 266272 | tf_op jit(solution)/shard_map/ppermute | solution.py:255
  102.7 0.0 collective-permute-done.3.right_ref
  102.7 0.0 copy-start.3
  102.7 0.7 copy-done.3
  103.4 4.8 %shard_map.68 = bf16[1024,512]{1,0:T(8,128)(2,1)S(1)} custom-call(s32[1,4]{1,0:T(1,128)S(1)} %copy-done.3, bf16[1024,512]{1,0:T(8,128)(2,1)S(1)} %get-tuple-element.18.anomaly_ref, bf16[1024,256]{1,0:T(8,128)(2,1)S(1)} %get-tuple-element.17.y_ref, bf16[256,1024]{1,0:T(8,128)(2,1)S(1)} %get-tuple-element.19.yt_ref, f32[8,512]{1,0:T(8,128)S(1)} %get-tuple-element.20.mean_ref, ...), custom_call_target="tpu_custom_call" | custom-call | flops 2147483648 | bytes 3435536 | tf_op jit(solution)/shard_map/pallas_call | solution.py:20
  108.2 60.9 %all_to_all.10.in_ref = bf16[32,32,512]{2,1,0:T(8,128)(2,1)S(1)} all-to-all(bf16[32,32,512]{2,1,0:T(8,128)(2,1)S(1)} %bitcast.4), channel_id=1, replica_groups=mesh['member'=32,'domain'=16] {'member'}, dimensions={0} | all-to-all | bytes 2097152 | tf_op jit(solution)/shard_map/all_to_all | solution.py:283
  169.0 3.0 %shard_map.69 = bf16[32,2,64,128]{3,2,1,0:T(8,128)(2,1)} custom-call(bf16[32,32,512]{2,1,0:T(8,128)(2,1)S(1)} %all_to_all.10.in_ref), custom_call_target="tpu_custom_call" | custom-call | bytes 1048576 | tf_op jit(solution)/shard_map/pallas_call | solution.py:20
  (1 shorter events, 0.0 us)
Async XLA Ops:
  0.0 1.2 copy-start
  1.6 5.6 %collective-permute-start = (f32[8,512]{1,0:T(8,128)S(1)}, f32[8,512]{1,0:T(8,128)S(1)}, u32[]{:S(2)}, u32[]{:S(2)}) collective-permute-start(f32[8,512]{1,0:T(8,128)S(1)} %get-tuple-element.15), channel_id=1, source_target_pairs={{0,1},{1,2},{2,3},{3,4},{4,5},{5,6},{6,7},{7,8},{8,9},{9,10},{10,1... | collective-permute-start | bytes 49160 | tf_op jit(solution)/shard_map/ppermute | solution.py:238
  3.5 5.1 %collective-permute-start.1 = (f32[8,512]{1,0:T(8,128)S(1)}, f32[8,512]{1,0:T(8,128)S(1)}, u32[]{:S(2)}, u32[]{:S(2)}) collective-permute-start(f32[8,512]{1,0:T(8,128)S(1)} %get-tuple-element.16), channel_id=1, source_target_pairs={{1,0},{2,1},{3,2},{4,3},{5,4},{6,5},{7,6},{8,7},{9,8},{10,9},{11,1... | collective-permute-start | bytes 49160 | tf_op jit(solution)/shard_map/ppermute | solution.py:239
  12.6 19.8 %copy-start.4 = (s32[1,256]{1,0:T(1,128)S(1)}, s32[1,256]{1,0:T(1,128)}, u32[]{:S(2)}) copy-start(s32[1,256]{1,0:T(1,128)} %param.10) | copy-start | bytes 3076
  12.6 19.8 %copy-start.5 = (s32[1,256]{1,0:T(1,128)S(1)}, s32[1,256]{1,0:T(1,128)}, u32[]{:S(2)}) copy-start(s32[1,256]{1,0:T(1,128)} %param.9) | copy-start | bytes 3076
  12.6 79.6 %all-to-all-start = ((bf16[32,32,512]{2,1,0:T(8,128)(2,1)}), bf16[32,32,512]{2,1,0:T(8,128)(2,1)S(1)}, u32[]{:S(2)}, u32[]{:S(2)}) async-start(bf16[32,32,512]{2,1,0:T(8,128)(2,1)} %shard_map.65), calls=%async_computation | async-start | bytes 2097152 | tf_op jit(solution)/shard_map/all_to_all | solution.py:246
  32.4 59.8 %copy-start.2 = (f32[1,256]{1,0:T(1,128)S(1)}, f32[1,256]{1,0:T(1,128)}, u32[]{:S(2)}) copy-start(f32[1,256]{1,0:T(1,128)} %prec_ref.3) | copy-start | bytes 3076
  32.4 59.7 %copy-start.1 = (f32[1,256]{1,0:T(1,128)S(1)}, f32[1,256]{1,0:T(1,128)}, u32[]{:S(2)}) copy-start(f32[1,256]{1,0:T(1,128)} %value_ref.3) | copy-start | bytes 3076
  92.7 10.0 %collective-permute-start.2 = (bf16[1040,128]{1,0:T(8,128)(2,1)S(1)}, bf16[1040,128]{1,0:T(8,128)(2,1)S(1)}, u32[]{:S(2)}, u32[]{:S(2)}) collective-permute-start(bf16[1040,128]{1,0:T(8,128)(2,1)S(1)} %get-tuple-element.23), channel_id=1, source_target_pairs={{0,1},{1,2},{2,3},{3,4},{4,5},{5,6},{6,7},{7,8},{8,9},{9,10},{10,1... | collective-permute-start | bytes 798728 | tf_op jit(solution)/shard_map/ppermute | solution.py:255
  94.6 8.1 %collective-permute-start.3 = (bf16[1040,128]{1,0:T(8,128)(2,1)S(1)}, bf16[1040,128]{1,0:T(8,128)(2,1)S(1)}, u32[]{:S(2)}, u32[]{:S(2)}) collective-permute-start(bf16[1040,128]{1,0:T(8,128)(2,1)S(1)} %get-tuple-element.24), channel_id=1, source_target_pairs={{1,0},{2,1},{3,2},{4,3},{5,4},{6,5},{7,6},{8,7},{9,8},{10,9},{11,1... | collective-permute-start | bytes 798728 | tf_op jit(solution)/shard_map/ppermute | solution.py:256
  102.7 0.7 copy-start.3

commit v2 on v1

--- a/solution.py
+++ b/solution.py
@@ -42,27 +42,44 @@
     return jnp.sum(jnp.where(iota((n, n), 0) == iota((n, n), 1), col, 0.0), axis=0, keepdims=True)
 
 
-def edge_kernel(ens_ref, head_ref, tail_ref):
-    pick = jnp.where(
-        (iota((8, 128), 0) == 0) & (iota((8, 128), 1) == 0)
-        | (iota((8, 128), 0) == 1) & (iota((8, 128), 1) == 127),
-        1.0,
-        0.0,
-    ).astype(BF16)
-    members = ens_ref.shape[0] // 8
+def split_kernel(half_ref, ens_ref, near_ref, far_ref, head_ref, tail_ref, store):
+    members, fields, rows, cols = ens_ref.shape
+    slabs = members * fields
+    part = rows // 2
+    half = half_ref[0, 0]
+    for ref, at in ((far_ref, 1 - half), (near_ref, half)):
+        start = pl.multiple_of(at * part, part)
+        ref[: slabs * part, :] = ens_ref[:, :, pl.ds(start, part), :].reshape(slabs * part, cols)
+    store[...] = ens_ref[...].reshape(slabs * rows, cols).astype(F32)
+    lines = [store[pl.ds(r, slabs, stride=rows), :].astype(BF16) for r in (part, rows - 1, 0, part - 1)]
+    top, bottom = slabs * part, slabs * part + slabs
+    low = [jnp.where(half == 0, lines[0], lines[2]), jnp.where(half == 0, lines[1], lines[3])]
+    high = [jnp.where(half == 0, lines[2], lines[0]), jnp.where(half == 0, lines[3], lines[1])]
+    for ref, (north, south) in ((far_ref, high), (near_ref, low)):
+        ref[top : top + slabs, :] = north
+        ref[bottom : bottom + slabs, :] = south
+    spot, lane = iota((8, cols), 0), iota((8, cols), 1)
+    pick = jnp.where((spot == 0) & (lane == 0) | (spot == 1) & (lane == cols - 1), 1.0, 0.0).astype(BF16)
+    group = members // 8
     for k in range(8):
-        rows = ens_ref[k * members : (k + 1) * members].reshape(-1, 128)
-        edges = lax.dot_general(pick, rows, (((1,), (1,)), ((), ())), preferred_element_type=F32)
+        lines = ens_ref[k * group : (k + 1) * group].reshape(-1, cols)
+        edges = lax.dot_general(pick, lines, (((1,), (1,)), ((), ())), preferred_element_type=F32)
         head_ref[k : k + 1, :] = edges[0:1]
         tail_ref[k : k + 1, :] = edges[1:2]
 
 
-def forecast_kernel(ens_ref, west_ref, east_ref, out_ref, store):
-    members, _, rows, cols = ens_ref.shape
+def forecast_kernel(half_ref, block_ref, west_ref, east_ref, out_ref, halo, store):
+    bands, members, _ = out_ref.shape
+    cols = block_ref.shape[1]
+    slabs = members * 2
+    part = bands * 2
+    rows = part * 2
     group = members // 8
-    spot = iota((8, cols), 0)
-    lane8 = iota((8, cols), 1)
+    half = half_ref[0, 0]
+    halo[...] = block_ref[slabs * part :, :].astype(F32)
+    spot, lane8 = iota((8, cols), 0), iota((8, cols), 1)
     pick = jnp.where((spot == 0) & (lane8 == 0) | (spot == 1) & (lane8 == cols - 1), 1.0, 0.0).astype(BF16)
+    lane, line = iota((part, cols), 1), iota((part, cols), 0)
 
     for k in range(8):
         n = group * 2 * rows
@@ -71,27 +88,28 @@
         rim = lax.dot_general(
             edges.astype(BF16), pick, (((0,), (0,)), ((), ())), preferred_element_type=F32
         ).reshape(group * 2, rows, cols)
+        rim = jnp.where(half == 0, rim[:, :part], rim[:, part:])
         for i in range(group):
             m = k * group + i
             wind = None
             for f in range(2):
-                x = ens_ref[m, f].astype(F32)
+                s = m * 2 + f
+                x = block_ref[s * part : (s + 1) * part, :].astype(F32)
                 edge = rim[i * 2 + f]
-                lane = iota((rows, cols), 1)
                 east = jnp.where(lane == cols - 1, edge, pltpu.roll(x, cols - 1, 1))
                 west = jnp.where(lane == 0, edge, pltpu.roll(x, 1, 1))
-                north = pltpu.roll(x, rows - 1, 0)
-                south = pltpu.roll(x, 1, 0)
+                north = jnp.where(line == part - 1, halo[s : s + 1, :], pltpu.roll(x, part - 1, 0))
+                south = jnp.where(line == 0, halo[slabs + s : slabs + s + 1, :], pltpu.roll(x, 1, 0))
                 if f == 0:
                     wind = x
                 laplace = east + west + north + south - 4.0 * x
                 new = x - ADVECT * 0.5 * wind * (east - west) + DIFFUSE * laplace
-                store[f, m * rows : (m + 1) * rows, :] = new
+                store[f, m * part : (m + 1) * part, :] = new
     for f in range(2):
-        for r in range(rows):
-            part = store[f, pl.ds(r, members, stride=rows), :]
+        for r in range(part):
+            line_r = store[f, pl.ds(r, members, stride=part), :]
             at = (f * 2 + r % 2) * cols
-            out_ref[r // 2, :, at : at + cols] = part.astype(BF16)
+            out_ref[r // 2, :, at : at + cols] = line_r.astype(BF16)
 
 
 def restore_kernel(in_ref, out_ref, store):
@@ -105,10 +123,11 @@
             out_ref[m, f] = store[f, m * rows : (m + 1) * rows, :].astype(BF16)
 
 
-def observe_kernel(local_ref, index_ref, value_ref, prec_ref, y_ref, head_ref, tail_ref):
-    members, cells = local_ref.shape
+def observe_kernel(near_ref, far_ref, index_ref, value_ref, prec_ref, y_ref, head_ref, tail_ref):
+    local = jnp.concatenate([near_ref[...], far_ref[...]], axis=0).astype(F32)
+    members, cells = local.shape
     half = cells // 2
-    equivalent = local_ref[:, half:].astype(F32) + OBS_WIND * local_ref[:, :half].astype(F32)
+    equivalent = local[:, half:] + OBS_WIND * local[:, :half]
     mean = jnp.sum(equivalent, axis=0, keepdims=True) * (1.0 / members)
     y = ((equivalent - mean) * (members - 1) ** (-0.5)).astype(BF16)
     y_ref[...] = y
@@ -124,9 +143,9 @@
         ref[members:, :] = last[:, at : at + n // 2]
 
 
-def own_kernel(local_ref, y_ref, anomaly_ref, yt_ref, mean_ref, gram_ref, cover_ref):
-    members, cells = local_ref.shape
-    local = local_ref[...].astype(F32)
+def own_kernel(near_ref, far_ref, y_ref, anomaly_ref, yt_ref, mean_ref, gram_ref, cover_ref):
+    local = jnp.concatenate([near_ref[...], far_ref[...]], axis=0).astype(F32)
+    members, cells = local.shape
     mean = jnp.sum(local, axis=0, keepdims=True) * (1.0 / members)
     mean_ref[...] = jnp.broadcast_to(mean, mean_ref.shape)
     anomaly_ref[...] = (local - mean).astype(BF16)
@@ -136,7 +155,7 @@
 
 
 def analyse_kernel(
-    mask_ref, anomaly_ref, y_ref, yt_ref, mean_ref, gram_ref, cover_ref, left_ref, right_ref,
+    mask_ref, half_ref, anomaly_ref, y_ref, yt_ref, mean_ref, gram_ref, cover_ref, left_ref, right_ref,
     index_ref, value_ref, prec_ref, out_ref, z, zt, gram, cover, u,
 ):
     members, cells = anomaly_ref.shape
@@ -157,7 +176,7 @@
     cover[:half, :] = cover_ref[...]
     cover[half:, :] = jnp.dot(zt[half:, :], anomaly_ref[...], preferred_element_type=F32)
 
-    mask = [mask_ref[0, b].astype(F32) for b in range(4)]
+    mask = [mask_ref[0:1, b : b + 1].astype(F32) for b in range(4)]
     hit = iota((half, n), 0) == index_ref[...]
     mean = mean_ref[0:1, :]
     cell_mean = to_col(mean[:, half:] + OBS_WIND * mean[:, :half])
@@ -215,7 +234,9 @@
     keep = 0.5 * (1.0 + to_one)
     for i in range(members // step):
         at = pl.ds(i * step, step)
-        out_ref[at, :] = (
+        side = i * step // (members // 2)
+        side = side + half_ref[0, 0] * (1 - 2 * side)
+        out_ref[side, pl.ds(i * step % (members // 2), step), :] = (
             shift
             + keep * anomaly_ref[at, :].astype(F32)
             + jnp.dot(z[at, :], gain, preferred_element_type=F32)
@@ -233,24 +254,50 @@
     to_left = [((i + 1) % domains, i) for i in range(domains)]
     struct = jax.ShapeDtypeStruct
 
+    part = bands // 2
+    half = (lax.axis_index("member") // part).astype(jnp.int32).reshape(1, 1)
+    groups = [[g * part + i for i in range(part)] for g in range(2)]
+    swap = [(i, (i + part) % bands) for i in range(bands)]
+    lines = members * fields * (rows // 2 + 2)
+
     edge = struct((8, members // 8 * fields * rows), F32)
-    head, tail = call(edge_kernel, [edge, edge], [ensemble])
+    block = struct((lines, cols), BF16)
+    near, far, head, tail = call(
+        split_kernel,
+        [block, block, edge, edge],
+        [half, ensemble],
+        scratch=[pltpu.VMEM((members * fields * rows, cols), F32)],
+        specs=[SMEM, VMEM],
+    )
+    far = lax.ppermute(far, "member", swap)
     west = lax.ppermute(tail, "domain", to_right)
     east = lax.ppermute(head, "domain", to_left)
-    predicted = call(
-        forecast_kernel,
-        struct((bands, members, cells), BF16),
-        [ensemble, west, east],
-        scratch=[pltpu.VMEM((fields, members * rows, cols), F32)],
-    )
-    local = lax.all_to_all(predicted, "member", split_axis=0, concat_axis=0, tiled=True).reshape(total, cells)
+    far_edges = lax.ppermute(jnp.concatenate([west, east], axis=0), "member", swap)
+
+    def forecast(rows_of, west_of, east_of):
+        predicted = call(
+            forecast_kernel,
+            struct((part, members, cells), BF16),
+            [half, rows_of, west_of, east_of],
+            scratch=[
+                pltpu.VMEM((2 * members * fields, cols), F32),
+                pltpu.VMEM((fields, members * rows // 2, cols), F32),
+            ],
+            specs=[SMEM, VMEM, VMEM, VMEM],
+        )
+        return lax.all_to_all(
+            predicted, "member", split_axis=0, concat_axis=0, axis_index_groups=groups, tiled=True
+        ).reshape(total // 2, cells)
+
+    near_local = forecast(near, west, east)
+    far_local = forecast(far, far_edges[:8], far_edges[8:])
 
     index = obs_row * cols + obs_col
     rim = struct((total + 16, n // 2), BF16)
     y, head_rows, tail_rows = call(
         observe_kernel,
         [struct((total, cells // 2), BF16), rim, rim],
-        [local, index, obs_value, obs_prec],
+        [near_local, far_local, index, obs_value, obs_prec],
     )
     left = lax.ppermute(tail_rows, "domain", to_right)
     right = lax.ppermute(head_rows, "domain", to_left)
@@ -263,13 +310,13 @@
             struct((cells // 2, cells // 2), F32),
             struct((cells // 2, cells), F32),
         ],
-        [local, y],
+        [near_local, far_local, y],
         flops=2 * total * cells * cells * 3 // 4,
     )
     analysis = call(
         analyse_kernel,
-        struct((total, cells), BF16),
-        [loc_mask, anomalies, y, yt, mean, gram, cover, left, right, index, obs_value, obs_prec],
+        struct((2, total // 2, cells), BF16),
+        [loc_mask, half, anomalies, y, yt, mean, gram, cover, left, right, index, obs_value, obs_prec],
         scratch=[
             pltpu.VMEM((total, cells), BF16),
             pltpu.VMEM((cells, total), BF16),
@@ -277,7 +324,7 @@
             pltpu.VMEM((cells, cells), F32),
             pltpu.VMEM((total, cells), BF16),
         ],
-        specs=[SMEM] + [VMEM] * 11,
+        specs=[VMEM, SMEM] + [VMEM] * 11,
         flops=2 * total * total * cells * 2,
     )
     back = lax.all_to_all(

time: 172 us -> 187 us (1.087)
  the two profiles are of different devices: /device:TPU:32 before, /device:TPU:8 now
where the time goes in v2:
time: 187 us; the launch traced here: 186 us
  starting transfers between devices  62 us (33%)
  waiting for transfers between devices  57.5 us (31%)
  blocking collectives  49.6 us (27%)
  Pallas kernels  14.4 us (8%)
  local copies, waits for them, and re-layouts  2.57 us (1%)
    all_to_all x1, blocking collectives, on_device(): lax.all_to_all(analysis.reshape(bands, members, cells), 'member', split_a...  49.6 us
    ppermute x1, waiting for transfers between devices, on_device(): west = lax.ppermute(tail, 'domain', to_right)  36.4 us
    ppermute x1, starting transfers between devices, on_device(): far = lax.ppermute(far, 'member', swap)  15.7 us
    all_to_all x2, starting transfers between devices, forecast(): lax.all_to_all(predicted, 'member', split_axis=0, concat_axis=0, axis_ind...  14.8 us
    pallas_call x7, Pallas kernels, call(): pl.pallas_call(kernel, out_shape=shapes, in_specs=specs or [VMEM] * len(a...  14.4 us
    ppermute x1, starting transfers between devices, on_device(): right = lax.ppermute(head_rows, 'domain', to_left)  10.2 us
    ppermute x1, starting transfers between devices, on_device(): east = lax.ppermute(head, 'domain', to_left)  10.2 us
    all_to_all x2, waiting for transfers between devices, forecast(): lax.all_to_all(predicted, 'member', split_axis=0, concat_axis=0, axis_ind...  9.7 us
  transfers between devices with their start and end apart: 8, of which 4 were waited for; matrix products, arithmetic and copies ran while one was open for 0% of the time, Pallas kernels for 3%

profile of v2, /device:TPU:8, one launch (start us, length us, event | category | flops | bytes accessed | tf_op | source)
XLA Modules:
  0.0 186.2 jit_solution(3723685584357430843)
XLA Ops:
  0.0 0.0 copy-start
  0.0 1.2 copy-done
  1.2 0.6 shard_map.64
  1.8 15.7 %collective-permute-start.2 = (bf16[2176,128]{1,0:T(8,128)(2,1)S(1)}, bf16[2176,128]{1,0:T(8,128)(2,1)S(1)}, u32[]{:S(2)}, u32[]{:S(2)}) collective-permute-start(bf16[2176,128]{1,0:T(8,128)(2,1)S(1)} %get-tuple-element.20), channel_id=1, source_target_pairs={{0,256},{16,272},{32,288},{48,304},{64,320},{80,336},{96,352},{112... | collective-permute-start | bytes 1671176 | tf_op jit(solution)/shard_map/ppermute | solution.py:272
  17.6 1.9 %collective-permute-start = (f32[8,512]{1,0:T(8,128)S(1)}, f32[8,512]{1,0:T(8,128)S(1)}, u32[]{:S(2)}, u32[]{:S(2)}) collective-permute-start(f32[8,512]{1,0:T(8,128)S(1)} %get-tuple-element.18), channel_id=1, source_target_pairs={{0,1},{1,2},{2,3},{3,4},{4,5},{5,6},{6,7},{7,8},{8,9},{9,10},{10,1... | collective-permute-start | bytes 49160 | tf_op jit(solution)/shard_map/ppermute | solution.py:273
  19.5 10.2 %collective-permute-start.1 = (f32[8,512]{1,0:T(8,128)S(1)}, f32[8,512]{1,0:T(8,128)S(1)}, u32[]{:S(2)}, u32[]{:S(2)}) collective-permute-start(f32[8,512]{1,0:T(8,128)S(1)} %get-tuple-element.19), channel_id=1, source_target_pairs={{1,0},{2,1},{3,2},{4,3},{5,4},{6,5},{7,6},{8,7},{9,8},{10,9},{11,1... | collective-permute-start | bytes 49160 | tf_op jit(solution)/shard_map/ppermute | solution.py:274
  29.7 36.4 %collective-permute-done.west_ref = f32[8,512]{1,0:T(8,128)S(1)} collective-permute-done((f32[8,512]{1,0:T(8,128)S(1)}, f32[8,512]{1,0:T(8,128)S(1)}, u32[]{:S(2)}, u32[]{:S(2)}) %collective-permute-start) | collective-permute-done | bytes 16416 | tf_op jit(solution)/shard_map/ppermute | solution.py:273
  66.1 0.0 collective-permute-done.1.east_ref
  66.1 2.6 %shard_map.65 = bf16[16,32,512]{2,1,0:T(8,128)(2,1)} custom-call(s32[1,1]{1,0:T(1,128)} %bitcast.half_ref, bf16[2176,128]{1,0:T(8,128)(2,1)S(1)} %get-tuple-element.17.block_ref, f32[8,512]{1,0:T(8,128)S(1)} %collective-permute-done.west_ref, f32[8,512]{1,0:T(8,128)S(1)} %collective-permute-done.1.east_ref), custom_call_target="tpu_custom_call" | custom-call | bytes 589828 | tf_op jit(solution)/shard_map/pallas_call | solution.py:20
  68.7 7.4 %all-to-all-start = ((bf16[16,32,512]{2,1,0:T(8,128)(2,1)}), bf16[16,32,512]{2,1,0:T(8,128)(2,1)S(1)}, u32[]{:S(2)}, u32[]{:S(2)}) async-start(bf16[16,32,512]{2,1,0:T(8,128)(2,1)} %shard_map.65), calls=%async_computation | async-start | bytes 1048576 | tf_op jit(solution)/shard_map/all_to_all | solution.py:288
  76.1 7.2 %collective-permute-start.3 = (f32[16,512]{1,0:T(8,128)S(1)}, f32[16,512]{1,0:T(8,128)S(1)}, u32[]{:S(2)}, u32[]{:S(2)}) collective-permute-start(f32[16,512]{1,0:T(8,128)S(1)} %pad_maximum_fusion), channel_id=1, source_target_pairs={{0,256},{16,272},{32,288},{48,304},{64,320},{80,336},{96,352},{112... | collective-permute-start | bytes 98312 | tf_op jit(solution)/shard_map/ppermute | solution.py:275
  83.2 7.4 %collective-permute-done.3 = f32[16,512]{1,0:T(8,128)S(1)} collective-permute-done((f32[16,512]{1,0:T(8,128)S(1)}, f32[16,512]{1,0:T(8,128)S(1)}, u32[]{:S(2)}, u32[]{:S(2)}) %collective-permute-start.3) | collective-permute-done | bytes 32800 | tf_op jit(solution)/shard_map/ppermute | solution.py:275
  90.6 0.0 collective-permute-done.2.block_ref
  90.6 2.6 %shard_map.66 = bf16[16,32,512]{2,1,0:T(8,128)(2,1)} custom-call(s32[1,1]{1,0:T(1,128)} %bitcast.half_ref, bf16[2176,128]{1,0:T(8,128)(2,1)S(1)} %collective-permute-done.2.block_ref, f32[8,512]{1,0:T(8,128)S(1)} %get-tuple-element.30.west_ref, f32[8,512]{1,0:T(8,128)S(1)} %get-tuple-element.29.east_ref), custom_call_target="tpu_custom_call" | custom-call | bytes 589828 | tf_op jit(solution)/shard_map/pallas_call | solution.py:20
  93.2 0.0 copy-start.4
  93.2 0.0 all-to-all-done
  93.2 7.4 %all-to-all-start.1 = ((bf16[16,32,512]{2,1,0:T(8,128)(2,1)}), bf16[16,32,512]{2,1,0:T(8,128)(2,1)S(1)}, u32[]{:S(2)}, u32[]{:S(2)}) async-start(bf16[16,32,512]{2,1,0:T(8,128)(2,1)} %shard_map.66), calls=%async_computation.1 | async-start | bytes 1048576 | tf_op jit(solution)/shard_map/all_to_all | solution.py:288
  100.6 0.0 copy-done.4
  100.6 0.0 copy-done.5
  100.6 9.7 %all-to-all-done.1 = bf16[16,32,512]{2,1,0:T(8,128)(2,1)S(1)} async-done(((bf16[16,32,512]{2,1,0:T(8,128)(2,1)}), bf16[16,32,512]{2,1,0:T(8,128)(2,1)S(1)}, u32[]{:S(2)}, u32[]{:S(2)}) %all-to-all-start.1) | async-done | bytes 524320 | tf_op jit(solution)/shard_map/all_to_all | solution.py:288
  110.3 0.0 copy-done.2
  110.3 0.7 copy-done.1
  111.0 0.6 shard_map.67
  111.5 1.9 %collective-permute-start.4 = (bf16[1040,128]{1,0:T(8,128)(2,1)S(1)}, bf16[1040,128]{1,0:T(8,128)(2,1)S(1)}, u32[]{:S(2)}, u32[]{:S(2)}) collective-permute-start(bf16[1040,128]{1,0:T(8,128)(2,1)S(1)} %get-tuple-element.27), channel_id=1, source_target_pairs={{0,1},{1,2},{2,3},{3,4},{4,5},{5,6},{6,7},{7,8},{8,9},{9,10},{10,1... | collective-permute-start | bytes 798728 | tf_op jit(solution)/shard_map/ppermute | solution.py:302
  113.4 10.2 %collective-permute-start.5 = (bf16[1040,128]{1,0:T(8,128)(2,1)S(1)}, bf16[1040,128]{1,0:T(8,128)(2,1)S(1)}, u32[]{:S(2)}, u32[]{:S(2)}) collective-permute-start(bf16[1040,128]{1,0:T(8,128)(2,1)S(1)} %get-tuple-element.28), channel_id=1, source_target_pairs={{1,0},{2,1},{3,2},{4,3},{5,4},{6,5},{7,6},{8,7},{9,8},{10,9},{11,1... | collective-permute-start | bytes 798728 | tf_op jit(solution)/shard_map/ppermute | solution.py:303
  123.7 0.9 shard_map.68
  124.6 4.1 %collective-permute-done.4.left_ref = bf16[1040,128]{1,0:T(8,128)(2,1)S(1)} collective-permute-done((bf16[1040,128]{1,0:T(8,128)(2,1)S(1)}, bf16[1040,128]{1,0:T(8,128)(2,1)S(1)}, u32[]{:S(2)}, u32[]{:S(2)}) %collective-permute-start.4) | collective-permute-done | bytes 266272 | tf_op jit(solution)/shard_map/ppermute | solution.py:302
  128.7 0.0 collective-permute-done.5.right_ref
  128.7 0.7 copy-done.3
  129.4 4.2 %shard_map.69 = bf16[2,512,512]{2,1,0:T(8,128)(2,1)S(1)} custom-call(s32[1,4]{1,0:T(1,128)S(1)} %copy-done.3, s32[1,1]{1,0:T(1,128)} %bitcast.half_ref, bf16[1024,512]{1,0:T(8,128)(2,1)S(1)} %get-tuple-element.22.anomaly_ref, bf16[1024,256]{1,0:T(8,128)(2,1)S(1)} %get-tuple-element.21.y_ref, bf16[256,1024]{1,0:T(8,128)(2,1)S(1)} %get-tuple-element.23.yt_ref, ...), custom_call_target="tpu_custom_call" | custom-call | flops 2147483648 | bytes 3435540 | tf_op jit(solution)/shard_map/pallas_call | solution.py:20
  133.6 49.6 %all_to_all.15.in_ref = bf16[32,32,512]{2,1,0:T(8,128)(2,1)S(1)} all-to-all(bf16[32,32,512]{2,1,0:T(8,128)(2,1)S(1)} %bitcast.8), channel_id=1, replica_groups=mesh['member'=32,'domain'=16] {'member'}, dimensions={0} | all-to-all | bytes 2097152 | tf_op jit(solution)/shard_map/all_to_all | solution.py:330
  183.2 3.0 %shard_map.70 = bf16[32,2,64,128]{3,2,1,0:T(8,128)(2,1)} custom-call(bf16[32,32,512]{2,1,0:T(8,128)(2,1)S(1)} %all_to_all.15.in_ref), custom_call_target="tpu_custom_call" | custom-call | bytes 1048576 | tf_op jit(solution)/shard_map/pallas_call | solution.py:20
  (7 shorter events, 0.0 us)
Async XLA Ops:
  0.0 1.2 copy-start
  1.8 88.8 %collective-permute-start.2 = (bf16[2176,128]{1,0:T(8,128)(2,1)S(1)}, bf16[2176,128]{1,0:T(8,128)(2,1)S(1)}, u32[]{:S(2)}, u32[]{:S(2)}) collective-permute-start(bf16[2176,128]{1,0:T(8,128)(2,1)S(1)} %get-tuple-element.20), channel_id=1, source_target_pairs={{0,256},{16,272},{32,288},{48,304},{64,320},{80,336},{96,352},{112... | collective-permute-start | bytes 1671176 | tf_op jit(solution)/shard_map/ppermute | solution.py:272
  17.6 48.5 %collective-permute-start = (f32[8,512]{1,0:T(8,128)S(1)}, f32[8,512]{1,0:T(8,128)S(1)}, u32[]{:S(2)}, u32[]{:S(2)}) collective-permute-start(f32[8,512]{1,0:T(8,128)S(1)} %get-tuple-element.18), channel_id=1, source_target_pairs={{0,1},{1,2},{2,3},{3,4},{4,5},{5,6},{6,7},{7,8},{8,9},{9,10},{10,1... | collective-permute-start | bytes 49160 | tf_op jit(solution)/shard_map/ppermute | solution.py:273
  19.5 46.6 %collective-permute-start.1 = (f32[8,512]{1,0:T(8,128)S(1)}, f32[8,512]{1,0:T(8,128)S(1)}, u32[]{:S(2)}, u32[]{:S(2)}) collective-permute-start(f32[8,512]{1,0:T(8,128)S(1)} %get-tuple-element.19), channel_id=1, source_target_pairs={{1,0},{2,1},{3,2},{4,3},{5,4},{6,5},{7,6},{8,7},{9,8},{10,9},{11,1... | collective-permute-start | bytes 49160 | tf_op jit(solution)/shard_map/ppermute | solution.py:274
  68.7 24.5 %all-to-all-start = ((bf16[16,32,512]{2,1,0:T(8,128)(2,1)}), bf16[16,32,512]{2,1,0:T(8,128)(2,1)S(1)}, u32[]{:S(2)}, u32[]{:S(2)}) async-start(bf16[16,32,512]{2,1,0:T(8,128)(2,1)} %shard_map.65), calls=%async_computation | async-start | bytes 1048576 | tf_op jit(solution)/shard_map/all_to_all | solution.py:288
  76.1 14.5 %collective-permute-start.3 = (f32[16,512]{1,0:T(8,128)S(1)}, f32[16,512]{1,0:T(8,128)S(1)}, u32[]{:S(2)}, u32[]{:S(2)}) collective-permute-start(f32[16,512]{1,0:T(8,128)S(1)} %pad_maximum_fusion), channel_id=1, source_target_pairs={{0,256},{16,272},{32,288},{48,304},{64,320},{80,336},{96,352},{112... | collective-permute-start | bytes 98312 | tf_op jit(solution)/shard_map/ppermute | solution.py:275
  93.2 7.4 %copy-start.4 = (s32[1,256]{1,0:T(1,128)S(1)}, s32[1,256]{1,0:T(1,128)}, u32[]{:S(2)}) copy-start(s32[1,256]{1,0:T(1,128)} %param.10) | copy-start | bytes 3076
  93.2 7.4 %copy-start.5 = (s32[1,256]{1,0:T(1,128)S(1)}, s32[1,256]{1,0:T(1,128)}, u32[]{:S(2)}) copy-start(s32[1,256]{1,0:T(1,128)} %param.9) | copy-start | bytes 3076
  93.2 17.1 %copy-start.2 = (f32[1,256]{1,0:T(1,128)S(1)}, f32[1,256]{1,0:T(1,128)}, u32[]{:S(2)}) copy-start(f32[1,256]{1,0:T(1,128)} %prec_ref.3) | copy-start | bytes 3076
  93.2 17.1 %all-to-all-start.1 = ((bf16[16,32,512]{2,1,0:T(8,128)(2,1)}), bf16[16,32,512]{2,1,0:T(8,128)(2,1)S(1)}, u32[]{:S(2)}, u32[]{:S(2)}) async-start(bf16[16,32,512]{2,1,0:T(8,128)(2,1)} %shard_map.66), calls=%async_computation.1 | async-start | bytes 1048576 | tf_op jit(solution)/shard_map/all_to_all | solution.py:288
  110.3 0.7 copy-start.1
  111.5 17.2 %collective-permute-start.4 = (bf16[1040,128]{1,0:T(8,128)(2,1)S(1)}, bf16[1040,128]{1,0:T(8,128)(2,1)S(1)}, u32[]{:S(2)}, u32[]{:S(2)}) collective-permute-start(bf16[1040,128]{1,0:T(8,128)(2,1)S(1)} %get-tuple-element.27), channel_id=1, source_target_pairs={{0,1},{1,2},{2,3},{3,4},{4,5},{5,6},{6,7},{7,8},{8,9},{9,10},{10,1... | collective-permute-start | bytes 798728 | tf_op jit(solution)/shard_map/ppermute | solution.py:302
  113.4 15.2 %collective-permute-start.5 = (bf16[1040,128]{1,0:T(8,128)(2,1)S(1)}, bf16[1040,128]{1,0:T(8,128)(2,1)S(1)}, u32[]{:S(2)}, u32[]{:S(2)}) collective-permute-start(bf16[1040,128]{1,0:T(8,128)(2,1)S(1)} %get-tuple-element.28), channel_id=1, source_target_pairs={{1,0},{2,1},{3,2},{4,3},{5,4},{6,5},{7,6},{8,7},{9,8},{10,9},{11,1... | collective-permute-start | bytes 798728 | tf_op jit(solution)/shard_map/ppermute | solution.py:303
  128.7 0.7 copy-start.3

commit v3 on v1

--- a/solution.py
+++ b/solution.py
@@ -42,51 +42,64 @@
     return jnp.sum(jnp.where(iota((n, n), 0) == iota((n, n), 1), col, 0.0), axis=0, keepdims=True)
 
 
-def edge_kernel(ens_ref, head_ref, tail_ref):
+def edge_kernel(even_ref, ens_ref, pair_ref, cross_ref):
     pick = jnp.where(
         (iota((8, 128), 0) == 0) & (iota((8, 128), 1) == 0)
         | (iota((8, 128), 0) == 1) & (iota((8, 128), 1) == 127),
         1.0,
         0.0,
     ).astype(BF16)
+    even = even_ref[0, 0] == 1
     members = ens_ref.shape[0] // 8
     for k in range(8):
         rows = ens_ref[k * members : (k + 1) * members].reshape(-1, 128)
         edges = lax.dot_general(pick, rows, (((1,), (1,)), ((), ())), preferred_element_type=F32)
-        head_ref[k : k + 1, :] = edges[0:1]
-        tail_ref[k : k + 1, :] = edges[1:2]
-
-
-def forecast_kernel(ens_ref, west_ref, east_ref, out_ref, store):
+        head, tail = edges[0:1], edges[1:2]
+        pair_ref[k : k + 1, :] = jnp.where(even, tail, head)
+        cross_ref[k : k + 1, :] = jnp.where(even, head, tail)
+
+
+def inside_kernel(ens_ref, new_ref):
+    members, _, rows, cols = ens_ref.shape
+    lane = iota((rows, cols), 1)
+    for m in range(members):
+        wind = None
+        for f in range(2):
+            x = ens_ref[m, f].astype(F32)
+            east = jnp.where(lane == cols - 1, 0.0, pltpu.roll(x, cols - 1, 1))
+            west = jnp.where(lane == 0, 0.0, pltpu.roll(x, 1, 1))
+            north = pltpu.roll(x, rows - 1, 0)
+            south = pltpu.roll(x, 1, 0)
+            if f == 0:
+                wind = x
+            laplace = east + west + north + south - 4.0 * x
+            new_ref[f, m * rows : (m + 1) * rows, :] = x - ADVECT * 0.5 * wind * (east - west) + DIFFUSE * laplace
+
+
+def forecast_kernel(even_ref, new_ref, ens_ref, pair_ref, cross_ref, out_ref, store):
     members, _, rows, cols = ens_ref.shape
     group = members // 8
+    even = even_ref[0, 0] == 1
     spot = iota((8, cols), 0)
     lane8 = iota((8, cols), 1)
     pick = jnp.where((spot == 0) & (lane8 == 0) | (spot == 1) & (lane8 == cols - 1), 1.0, 0.0).astype(BF16)
+    side = jnp.where(iota((rows, cols), 1) == 0, ADVECT * 0.5, -ADVECT * 0.5)
 
     for k in range(8):
         n = group * 2 * rows
         which = iota((8, n), 0)
-        edges = jnp.where(which == 0, west_ref[k : k + 1, :], jnp.where(which == 1, east_ref[k : k + 1, :], 0.0))
+        pair, cross = pair_ref[k : k + 1, :], cross_ref[k : k + 1, :]
+        west, east = jnp.where(even, cross, pair), jnp.where(even, pair, cross)
+        edges = jnp.where(which == 0, west, jnp.where(which == 1, east, 0.0))
         rim = lax.dot_general(
             edges.astype(BF16), pick, (((0,), (0,)), ((), ())), preferred_element_type=F32
         ).reshape(group * 2, rows, cols)
         for i in range(group):
             m = k * group + i
-            wind = None
+            rate = side * ens_ref[m, 0].astype(F32) + DIFFUSE
             for f in range(2):
-                x = ens_ref[m, f].astype(F32)
-                edge = rim[i * 2 + f]
-                lane = iota((rows, cols), 1)
-                east = jnp.where(lane == cols - 1, edge, pltpu.roll(x, cols - 1, 1))
-                west = jnp.where(lane == 0, edge, pltpu.roll(x, 1, 1))
-                north = pltpu.roll(x, rows - 1, 0)
-                south = pltpu.roll(x, 1, 0)
-                if f == 0:
-                    wind = x
-                laplace = east + west + north + south - 4.0 * x
-                new = x - ADVECT * 0.5 * wind * (east - west) + DIFFUSE * laplace
-                store[f, m * rows : (m + 1) * rows, :] = new
+                at = slice(m * rows, (m + 1) * rows)
+                store[f, at, :] = new_ref[f, at, :] + rate * rim[i * 2 + f]
     for f in range(2):
         for r in range(rows):
             part = store[f, pl.ds(r, members, stride=rows), :]
@@ -105,27 +118,31 @@
             out_ref[m, f] = store[f, m * rows : (m + 1) * rows, :].astype(BF16)
 
 
-def observe_kernel(local_ref, index_ref, value_ref, prec_ref, y_ref, head_ref, tail_ref):
+def observe_kernel(even_ref, local_ref, index_ref, value_ref, prec_ref, y_ref, mean_ref, pair_ref, cross_ref):
     members, cells = local_ref.shape
     half = cells // 2
     equivalent = local_ref[:, half:].astype(F32) + OBS_WIND * local_ref[:, :half].astype(F32)
     mean = jnp.sum(equivalent, axis=0, keepdims=True) * (1.0 / members)
-    y = ((equivalent - mean) * (members - 1) ** (-0.5)).astype(BF16)
-    y_ref[...] = y
-    n = index_ref.shape[1]
-    hit = iota((half, n), 0) == index_ref[...]
-    rows = jnp.dot(y, hit.astype(BF16), preferred_element_type=F32).astype(BF16)
-    observed_mean = jnp.sum(jnp.where(hit, to_col(mean), 0.0), axis=0, keepdims=True)
-    innovation = value_ref[...] - observed_mean
-    which = iota((16, n), 0)
-    last = jnp.where(which == 0, innovation, jnp.where(which == 1, prec_ref[...], 0.0)).astype(BF16)
-    for ref, at in ((head_ref, 0), (tail_ref, n // 2)):
-        ref[:members, :] = rows[:, at : at + n // 2]
-        ref[members:, :] = last[:, at : at + n // 2]
-
-
-def own_kernel(local_ref, y_ref, anomaly_ref, yt_ref, mean_ref, gram_ref, cover_ref):
+    mean_ref[...] = jnp.broadcast_to(mean, mean_ref.shape)
+    y_ref[...] = ((equivalent - mean) * (members - 1) ** (-0.5)).astype(BF16)
+    n = index_ref.shape[1] // 2
+    even = even_ref[0, 0]
+    for ref, side in ((cross_ref, 1 - even), (pair_ref, even)):
+        at = pl.ds(pl.multiple_of(side * n, n), n)
+        hit = iota((half, n), 0) == index_ref[:, at]
+        ref[:members, :] = jnp.dot(y_ref[...], hit.astype(BF16), preferred_element_type=F32).astype(BF16)
+        innovation = value_ref[:, at] - jnp.sum(jnp.where(hit, to_col(mean), 0.0), axis=0, keepdims=True)
+        which = iota((16, n), 0)
+        last = jnp.where(which == 0, innovation, jnp.where(which == 1, prec_ref[:, at], 0.0))
+        ref[members:, :] = last.astype(BF16)
+
+
+def own_kernel(
+    mask_ref, local_ref, y_ref, observed_ref, index_ref, value_ref, prec_ref,
+    anomaly_ref, yt_ref, mean_ref, gram_ref, cover_ref, row_ref, col_ref,
+):
     members, cells = local_ref.shape
+    half = cells // 2
     local = local_ref[...].astype(F32)
     mean = jnp.sum(local, axis=0, keepdims=True) * (1.0 / members)
     mean_ref[...] = jnp.broadcast_to(mean, mean_ref.shape)
@@ -134,19 +151,31 @@
     gram_ref[...] = jnp.dot(yt_ref[...], y_ref[...], preferred_element_type=F32)
     cover_ref[...] = jnp.dot(yt_ref[...], anomaly_ref[...], preferred_element_type=F32)
 
+    n = index_ref.shape[1]
+    hit = iota((half, n), 0) == index_ref[...]
+    observed_mean = jnp.sum(jnp.where(hit, to_col(observed_ref[0:1, :]), 0.0), axis=0, keepdims=True)
+    innovation = (value_ref[...] - observed_mean).astype(BF16).astype(F32)
+    mask = jnp.where(iota((1, n), 1) < n // 2, mask_ref[0:1, 1:2].astype(F32), mask_ref[0:1, 2:3].astype(F32))
+    weight = prec_ref[...].astype(BF16).astype(F32) * mask
+    own_d = jnp.sum(jnp.where(hit, weight, 0.0), axis=1, keepdims=True)
+    own_g = jnp.sum(jnp.where(hit, weight * innovation, 0.0), axis=1, keepdims=True)
+    which = iota((8, half), 0)
+    row_ref[...] = jnp.where(which == 0, to_row(own_d), to_row(own_g))
+    lane = iota((half, 128), 1)
+    col_ref[...] = jnp.where(lane == 0, own_d, own_g)
+
 
 def analyse_kernel(
-    mask_ref, anomaly_ref, y_ref, yt_ref, mean_ref, gram_ref, cover_ref, left_ref, right_ref,
-    index_ref, value_ref, prec_ref, out_ref, z, zt, gram, cover, u,
+    even_ref, mask_ref, anomaly_ref, y_ref, yt_ref, mean_ref, gram_ref, cover_ref, row_ref, col_ref,
+    pair_ref, cross_ref, out_ref, z, zt, gram, cover, u,
 ):
     members, cells = anomaly_ref.shape
     half = cells // 2
     quarter = half // 2
-    n = index_ref.shape[1]
 
     z[:, :half] = y_ref[...]
-    z[:, half : half + quarter] = left_ref[:members, :]
-    z[:, half + quarter :] = right_ref[:members, :]
+    z[:, half : half + quarter] = pair_ref[:members, :]
+    z[:, half + quarter :] = cross_ref[:members, :]
     zt[:half, :] = yt_ref[...]
     zt[half:, :] = z[:, half:].T
     rim = jnp.dot(zt[half:, :], z[...], preferred_element_type=F32)
@@ -157,25 +186,19 @@
     cover[:half, :] = cover_ref[...]
     cover[half:, :] = jnp.dot(zt[half:, :], anomaly_ref[...], preferred_element_type=F32)
 
-    mask = [mask_ref[0, b].astype(F32) for b in range(4)]
-    hit = iota((half, n), 0) == index_ref[...]
     mean = mean_ref[0:1, :]
-    cell_mean = to_col(mean[:, half:] + OBS_WIND * mean[:, :half])
-    observed_mean = jnp.sum(jnp.where(hit, cell_mean, 0.0), axis=0, keepdims=True)
-    innovation = (value_ref[...] - observed_mean).astype(BF16).astype(F32)
-    weight = prec_ref[...].astype(BF16).astype(F32) * jnp.where(iota((1, n), 1) < n // 2, mask[1], mask[2])
-    own_d = jnp.sum(jnp.where(hit, weight, 0.0), axis=1, keepdims=True)
-    own_g = jnp.sum(jnp.where(hit, weight * innovation, 0.0), axis=1, keepdims=True)
-    left_tail = left_ref[members : members + 16, :].astype(F32)
-    right_tail = right_ref[members : members + 16, :].astype(F32)
-    left_d = left_tail[1:2, :] * (0.5 * mask[0])
-    right_d = right_tail[1:2, :] * (0.5 * mask[3])
-    left_g = left_d * left_tail[0:1, :]
-    right_g = right_d * right_tail[0:1, :]
-    d_row = jnp.concatenate([to_row(own_d), left_d, right_d], axis=1)
-    g_row = jnp.concatenate([to_row(own_g), left_g, right_g], axis=1)
-    d_col = jnp.concatenate([own_d, to_col(left_d), to_col(right_d)], axis=0)
-    g_col = jnp.concatenate([own_g, to_col(left_g), to_col(right_g)], axis=0)
+    even = even_ref[0, 0] == 1
+    left_mask, right_mask = mask_ref[0:1, 0:1].astype(F32), mask_ref[0:1, 3:4].astype(F32)
+    pair_tail = pair_ref[members : members + 16, :].astype(F32)
+    cross_tail = cross_ref[members : members + 16, :].astype(F32)
+    pair_d = pair_tail[1:2, :] * (0.5 * jnp.where(even, right_mask, left_mask))
+    cross_d = cross_tail[1:2, :] * (0.5 * jnp.where(even, left_mask, right_mask))
+    pair_g = pair_d * pair_tail[0:1, :]
+    cross_g = cross_d * cross_tail[0:1, :]
+    d_row = jnp.concatenate([row_ref[0:1, :], pair_d, cross_d], axis=1)
+    g_row = jnp.concatenate([row_ref[1:2, :], pair_g, cross_g], axis=1)
+    d_col = jnp.concatenate([col_ref[:, 0:1], to_col(pair_d), to_col(cross_d)], axis=0)
+    g_col = jnp.concatenate([col_ref[:, 1:2], to_col(pair_g), to_col(cross_g)], axis=0)
 
     k = gram[...]
     m = cover[...]
@@ -229,32 +252,36 @@
     total = members * bands
     cells = fields * (rows // bands) * cols
     n = obs_value.shape[1]
-    to_right = [(i, (i + 1) % domains) for i in range(domains)]
-    to_left = [((i + 1) % domains, i) for i in range(domains)]
+    pairs = [(i, i ^ 1) for i in range(domains)]
+    crosses = [(i, (i - 1 + 2 * (i % 2)) % domains) for i in range(domains)]
     struct = jax.ShapeDtypeStruct
+    even = (1 - lax.axis_index("domain") % 2).astype(jnp.int32).reshape(1, 1)
 
     edge = struct((8, members // 8 * fields * rows), F32)
-    head, tail = call(edge_kernel, [edge, edge], [ensemble])
-    west = lax.ppermute(tail, "domain", to_right)
-    east = lax.ppermute(head, "domain", to_left)
+    pair_edge, cross_edge = call(edge_kernel, [edge, edge], [even, ensemble], specs=[SMEM, VMEM])
+    cross_edge = lax.ppermute(cross_edge, "domain", crosses)
+    pair_edge = lax.ppermute(pair_edge, "domain", pairs)
+    inside = call(inside_kernel, struct((fields, members * rows, cols), F32), [ensemble])
     predicted = call(
         forecast_kernel,
         struct((bands, members, cells), BF16),
-        [ensemble, west, east],
+        [even, inside, ensemble, pair_edge, cross_edge],
         scratch=[pltpu.VMEM((fields, members * rows, cols), F32)],
+        specs=[SMEM] + [VMEM] * 4,
     )
     local = lax.all_to_all(predicted, "member", split_axis=0, concat_axis=0, tiled=True).reshape(total, cells)
 
     index = obs_row * cols + obs_col
     rim = struct((total + 16, n // 2), BF16)
-    y, head_rows, tail_rows = call(
+    y, observed, pair_rows, cross_rows = call(
         observe_kernel,
-        [struct((total, cells // 2), BF16), rim, rim],
-        [local, index, obs_value, obs_prec],
-    )
-    left = lax.ppermute(tail_rows, "domain", to_right)
-    right = lax.ppermute(head_rows, "domain", to_left)
-    anomalies, yt, mean, gram, cover = call(
+        [struct((total, cells // 2), BF16), struct((8, cells // 2), F32), rim, rim],
+        [even, local, index, obs_value, obs_prec],
+        specs=[SMEM] + [VMEM] * 4,
+    )
+    cross_rows = lax.ppermute(cross_rows, "domain", crosses)
+    pair_rows = lax.ppermute(pair_rows, "domain", pairs)
+    own = call(
         own_kernel,
         [
             struct((total, cells), BF16),
@@ -262,14 +289,17 @@
             struct((8, cells), F32),
             struct((cells // 2, cells // 2), F32),
             struct((cells // 2, cells), F32),
+            struct((8, cells // 2), F32),
+            struct((cells // 2, 128), F32),
         ],
-        [local, y],
+        [loc_mask, local, y, observed, index, obs_value, obs_prec],
         flops=2 * total * cells * cells * 3 // 4,
     )
+    anomalies, yt, mean, gram, cover, row, col = own
     analysis = call(
         analyse_kernel,
         struct((total, cells), BF16),
-        [loc_mask, anomalies, y, yt, mean, gram, cover, left, right, index, obs_value, obs_prec],
+        [even, loc_mask, anomalies, y, yt, mean, gram, cover, row, col, pair_rows, cross_rows],
         scratch=[
             pltpu.VMEM((total, cells), BF16),
             pltpu.VMEM((cells, total), BF16),

time: 172 us -> 169 us (0.983)
    all_to_all x1, starting transfers between devices: 19.8 us -> 15.9 us  [on_device(): lax.all_to_all(predicted, 'member', split_axis=0, concat_axis=0, tiled=True)]
    ppermute x4, starting transfers between devices: 11.1 us -> 13.3 us  [the longest x1 7.49 us: on_device(): cross_edge = lax.ppermute(cross_edge, 'domain', crosses)]
    pallas_call x6 -> x7, Pallas kernels: 13.5 us -> 13.4 us  [call(): pl.pallas_call(kernel, out_shape=shapes, in_specs=specs or [VMEM] * len(a...]
  transfers between devices with their start and end apart: 5 -> 5, of which waited for: 3 -> 2; matrix products, arithmetic and copies ran while one was open for 0% -> 0% of each run, Pallas kernels for 0% -> 1%
where the time goes in v3:
time: 169 us
  waiting for transfers between devices  64.1 us (38%)
  blocking collectives  60.5 us (36%)
  starting transfers between devices  29.2 us (17%)
  Pallas kernels  13.4 us (8%)
    all_to_all x1, blocking collectives, on_device(): lax.all_to_all(analysis.reshape(bands, members, cells), 'member', split_a...  60.5 us
    all_to_all x1, waiting for transfers between devices, on_device(): lax.all_to_all(predicted, 'member', split_axis=0, concat_axis=0, tiled=True)  59.3 us
    all_to_all x1, starting transfers between devices, on_device(): lax.all_to_all(predicted, 'member', split_axis=0, concat_axis=0, tiled=True)  15.9 us
    pallas_call x7, Pallas kernels, call(): pl.pallas_call(kernel, out_shape=shapes, in_specs=specs or [VMEM] * len(a...  13.4 us
    ppermute x1, starting transfers between devices, on_device(): cross_edge = lax.ppermute(cross_edge, 'domain', crosses)  7.49 us
    ppermute x1, waiting for transfers between devices, on_device(): cross_rows = lax.ppermute(cross_rows, 'domain', crosses)  4.82 us
  transfers between devices with their start and end apart: 5, of which 2 were waited for; matrix products, arithmetic and copies ran while one was open for 0% of the time, Pallas kernels for 1%

profile of v3, /device:TPU:32, one launch (start us, length us, event | category | flops | bytes accessed | tf_op | source)
XLA Modules:
  0.0 168.6 jit_solution(17416643310285031098)
XLA Ops:
  0.0 0.0 copy-start
  0.0 1.2 copy-done
  1.2 0.4 shard_map.65
  1.6 1.9 %collective-permute-start = (f32[8,512]{1,0:T(8,128)S(1)}, f32[8,512]{1,0:T(8,128)S(1)}, u32[]{:S(2)}, u32[]{:S(2)}) collective-permute-start(f32[8,512]{1,0:T(8,128)S(1)} %get-tuple-element.18), channel_id=1, source_target_pairs={{0,1},{1,0},{2,3},{3,2},{4,5},{5,4},{6,7},{7,6},{8,9},{9,8},{10,11... | collective-permute-start | bytes 49160 | tf_op jit(solution)/shard_map/ppermute | solution.py:263
  3.5 7.5 %collective-permute-start.1 = (f32[8,512]{1,0:T(8,128)S(1)}, f32[8,512]{1,0:T(8,128)S(1)}, u32[]{:S(2)}, u32[]{:S(2)}) collective-permute-start(f32[8,512]{1,0:T(8,128)S(1)} %get-tuple-element.19), channel_id=1, source_target_pairs={{0,15},{1,2},{2,1},{3,4},{4,3},{5,6},{6,5},{7,8},{8,7},{9,10},{10,... | collective-permute-start | bytes 49160 | tf_op jit(solution)/shard_map/ppermute | solution.py:262
  11.0 1.4 shard_map.64.new_ref
  12.5 0.0 collective-permute-done.pair_ref
  12.5 0.0 collective-permute-done.1.cross_ref
  12.5 2.9 %shard_map.66 = bf16[32,32,512]{2,1,0:T(8,128)(2,1)} custom-call(s32[1,1]{1,0:T(1,128)} %bitcast.even_ref, f32[2,2048,128]{2,1,0:T(8,128)S(1)} %shard_map.64.new_ref, bf16[32,2,64,128]{3,2,1,0:T(8,128)(2,1)S(1)} %copy-done, f32[8,512]{1,0:T(8,128)S(1)} %collective-permute-done.pair_ref, f32[8,512]{1,0:T(8,128)S(1)} %collective-permute-done.1.cross_ref), custom_call_target="tpu_custom_call" | custom-call | bytes 3178500 | tf_op jit(solution)/shard_map/pallas_call | solution.py:20
  15.4 0.0 copy-start.4
  15.4 0.0 copy-start.5
  15.4 0.0 copy-start.1
  15.4 0.0 copy-start.2
  15.4 0.0 copy-start.3
  15.4 15.9 %all-to-all-start = ((bf16[32,32,512]{2,1,0:T(8,128)(2,1)}), bf16[32,32,512]{2,1,0:T(8,128)(2,1)S(1)}, u32[]{:S(2)}, u32[]{:S(2)}) async-start(bf16[32,32,512]{2,1,0:T(8,128)(2,1)} %shard_map.66), calls=%async_computation | async-start | bytes 2097152 | tf_op jit(solution)/shard_map/all_to_all | solution.py:272
  31.3 0.0 copy-done.4
  31.4 0.0 copy-done.5
  31.4 59.3 %all-to-all-done = bf16[32,32,512]{2,1,0:T(8,128)(2,1)S(1)} async-done(((bf16[32,32,512]{2,1,0:T(8,128)(2,1)}), bf16[32,32,512]{2,1,0:T(8,128)(2,1)S(1)}, u32[]{:S(2)}, u32[]{:S(2)}) %all-to-all-start) | async-done | bytes 1048608 | tf_op jit(solution)/shard_map/all_to_all | solution.py:272
  90.7 0.0 copy-done.1
  90.7 0.0 copy-done.2
  90.7 0.7 shard_map.67
  91.3 1.9 %collective-permute-start.2 = (bf16[1040,128]{1,0:T(8,128)(2,1)S(1)}, bf16[1040,128]{1,0:T(8,128)(2,1)S(1)}, u32[]{:S(2)}, u32[]{:S(2)}) collective-permute-start(bf16[1040,128]{1,0:T(8,128)(2,1)S(1)} %get-tuple-element.29), channel_id=1, source_target_pairs={{0,1},{1,0},{2,3},{3,2},{4,5},{5,4},{6,7},{7,6},{8,9},{9,8},{10,11... | collective-permute-start | bytes 798728 | tf_op jit(solution)/shard_map/ppermute | solution.py:283
  93.3 1.9 %collective-permute-start.3 = (bf16[1040,128]{1,0:T(8,128)(2,1)S(1)}, bf16[1040,128]{1,0:T(8,128)(2,1)S(1)}, u32[]{:S(2)}, u32[]{:S(2)}) collective-permute-start(bf16[1040,128]{1,0:T(8,128)(2,1)S(1)} %get-tuple-element.30), channel_id=1, source_target_pairs={{0,15},{1,2},{2,1},{3,4},{4,3},{5,6},{6,5},{7,8},{8,7},{9,10},{10,... | collective-permute-start | bytes 798728 | tf_op jit(solution)/shard_map/ppermute | solution.py:282
  95.2 0.0 copy-done.3
  95.2 1.0 shard_map.68
  96.2 0.0 collective-permute-done.2.pair_ref
  96.2 4.8 %collective-permute-done.3.cross_ref = bf16[1040,128]{1,0:T(8,128)(2,1)S(1)} collective-permute-done((bf16[1040,128]{1,0:T(8,128)(2,1)S(1)}, bf16[1040,128]{1,0:T(8,128)(2,1)S(1)}, u32[]{:S(2)}, u32[]{:S(2)}) %collective-permute-start.3) | collective-permute-done | bytes 266272 | tf_op jit(solution)/shard_map/ppermute | solution.py:282
  101.0 4.1 %shard_map.69 = bf16[1024,512]{1,0:T(8,128)(2,1)S(1)} custom-call(s32[1,1]{1,0:T(1,128)} %bitcast.even_ref, s32[1,4]{1,0:T(1,128)S(1)} %copy-done.3, bf16[1024,512]{1,0:T(8,128)(2,1)S(1)} %get-tuple-element.22.anomaly_ref, bf16[1024,256]{1,0:T(8,128)(2,1)S(1)} %get-tuple-element.20.y_ref, bf16[256,1024]{1,0:T(8,128)(2,1)S(1)} %get-tuple-element.23.yt_ref, ...), custom_call_target="tpu_custom_call" | custom-call | flops 2147483648 | bytes 3571732 | tf_op jit(solution)/shard_map/pallas_call | solution.py:20
  105.1 60.5 %all_to_all.10.in_ref = bf16[32,32,512]{2,1,0:T(8,128)(2,1)S(1)} all-to-all(bf16[32,32,512]{2,1,0:T(8,128)(2,1)S(1)} %bitcast.5), channel_id=1, replica_groups=mesh['member'=32,'domain'=16] {'member'}, dimensions={0} | all-to-all | bytes 2097152 | tf_op jit(solution)/shard_map/all_to_all | solution.py:313
  165.6 3.0 %shard_map.70 = bf16[32,2,64,128]{3,2,1,0:T(8,128)(2,1)} custom-call(bf16[32,32,512]{2,1,0:T(8,128)(2,1)S(1)} %all_to_all.10.in_ref), custom_call_target="tpu_custom_call" | custom-call | bytes 1048576 | tf_op jit(solution)/shard_map/pallas_call | solution.py:20
  (1 shorter events, 0.0 us)
Async XLA Ops:
  0.0 1.2 copy-start
  1.6 10.9 %collective-permute-start = (f32[8,512]{1,0:T(8,128)S(1)}, f32[8,512]{1,0:T(8,128)S(1)}, u32[]{:S(2)}, u32[]{:S(2)}) collective-permute-start(f32[8,512]{1,0:T(8,128)S(1)} %get-tuple-element.18), channel_id=1, source_target_pairs={{0,1},{1,0},{2,3},{3,2},{4,5},{5,4},{6,7},{7,6},{8,9},{9,8},{10,11... | collective-permute-start | bytes 49160 | tf_op jit(solution)/shard_map/ppermute | solution.py:263
  3.5 8.9 %collective-permute-start.1 = (f32[8,512]{1,0:T(8,128)S(1)}, f32[8,512]{1,0:T(8,128)S(1)}, u32[]{:S(2)}, u32[]{:S(2)}) collective-permute-start(f32[8,512]{1,0:T(8,128)S(1)} %get-tuple-element.19), channel_id=1, source_target_pairs={{0,15},{1,2},{2,1},{3,4},{4,3},{5,6},{6,5},{7,8},{8,7},{9,10},{10,... | collective-permute-start | bytes 49160 | tf_op jit(solution)/shard_map/ppermute | solution.py:262
  15.4 15.9 %copy-start.4 = (s32[1,256]{1,0:T(1,128)S(1)}, s32[1,256]{1,0:T(1,128)}, u32[]{:S(2)}) copy-start(s32[1,256]{1,0:T(1,128)} %param.10) | copy-start | bytes 3076
  15.4 16.0 %copy-start.5 = (s32[1,256]{1,0:T(1,128)S(1)}, s32[1,256]{1,0:T(1,128)}, u32[]{:S(2)}) copy-start(s32[1,256]{1,0:T(1,128)} %param.9) | copy-start | bytes 3076
  15.4 75.3 %copy-start.1 = (f32[1,256]{1,0:T(1,128)S(1)}, f32[1,256]{1,0:T(1,128)}, u32[]{:S(2)}) copy-start(f32[1,256]{1,0:T(1,128)} %value_ref.3) | copy-start | bytes 3076
  15.4 75.3 %copy-start.2 = (f32[1,256]{1,0:T(1,128)S(1)}, f32[1,256]{1,0:T(1,128)}, u32[]{:S(2)}) copy-start(f32[1,256]{1,0:T(1,128)} %prec_ref.3) | copy-start | bytes 3076
  15.4 79.8 %copy-start.3 = (s32[1,4]{1,0:T(1,128)S(1)}, s32[1,4]{1,0:T(1,128)}, u32[]{:S(2)}) copy-start(s32[1,4]{1,0:T(1,128)} %mask_ref.3) | copy-start | bytes 52
  15.4 75.3 %all-to-all-start = ((bf16[32,32,512]{2,1,0:T(8,128)(2,1)}), bf16[32,32,512]{2,1,0:T(8,128)(2,1)S(1)}, u32[]{:S(2)}, u32[]{:S(2)}) async-start(bf16[32,32,512]{2,1,0:T(8,128)(2,1)} %shard_map.66), calls=%async_computation | async-start | bytes 2097152 | tf_op jit(solution)/shard_map/all_to_all | solution.py:272
  91.3 4.8 %collective-permute-start.2 = (bf16[1040,128]{1,0:T(8,128)(2,1)S(1)}, bf16[1040,128]{1,0:T(8,128)(2,1)S(1)}, u32[]{:S(2)}, u32[]{:S(2)}) collective-permute-start(bf16[1040,128]{1,0:T(8,128)(2,1)S(1)} %get-tuple-element.29), channel_id=1, source_target_pairs={{0,1},{1,0},{2,3},{3,2},{4,5},{5,4},{6,7},{7,6},{8,9},{9,8},{10,11... | collective-permute-start | bytes 798728 | tf_op jit(solution)/shard_map/ppermute | solution.py:283
  93.3 7.7 %collective-permute-start.3 = (bf16[1040,128]{1,0:T(8,128)(2,1)S(1)}, bf16[1040,128]{1,0:T(8,128)(2,1)S(1)}, u32[]{:S(2)}, u32[]{:S(2)}) collective-permute-start(bf16[1040,128]{1,0:T(8,128)(2,1)S(1)} %get-tuple-element.30), channel_id=1, source_target_pairs={{0,15},{1,2},{2,1},{3,4},{4,3},{5,6},{6,5},{7,8},{8,7},{9,10},{10,... | collective-permute-start | bytes 798728 | tf_op jit(solution)/shard_map/ppermute | solution.py:282

commit v4 on v3

--- a/solution.py
+++ b/solution.py
@@ -8,6 +8,7 @@
 ADVECT = 0.4
 DIFFUSE = 0.15
 OBS_WIND = 0.5
+SKEW = 4
 F32 = jnp.float32
 BF16 = jnp.bfloat16
 VMEM = pl.BlockSpec(memory_space=pltpu.VMEM)
@@ -42,25 +43,23 @@
     return jnp.sum(jnp.where(iota((n, n), 0) == iota((n, n), 1), col, 0.0), axis=0, keepdims=True)
 
 
-def edge_kernel(even_ref, ens_ref, pair_ref, cross_ref):
-    pick = jnp.where(
-        (iota((8, 128), 0) == 0) & (iota((8, 128), 1) == 0)
-        | (iota((8, 128), 0) == 1) & (iota((8, 128), 1) == 127),
-        1.0,
-        0.0,
-    ).astype(BF16)
-    even = even_ref[0, 0] == 1
+def write_edges(ens_ref, tail, edge_ref):
+    rows, cols = ens_ref.shape[2:]
+    pick = (iota((8, cols), 1) == jnp.where(tail, cols - 1, 0)).astype(F32).astype(BF16)
     members = ens_ref.shape[0] // 8
     for k in range(8):
-        rows = ens_ref[k * members : (k + 1) * members].reshape(-1, 128)
-        edges = lax.dot_general(pick, rows, (((1,), (1,)), ((), ())), preferred_element_type=F32)
-        head, tail = edges[0:1], edges[1:2]
-        pair_ref[k : k + 1, :] = jnp.where(even, tail, head)
-        cross_ref[k : k + 1, :] = jnp.where(even, head, tail)
-
-
-def inside_kernel(ens_ref, new_ref):
+        lines = ens_ref[k * members : (k + 1) * members].reshape(-1, cols)
+        edges = lax.dot_general(pick, lines, (((1,), (1,)), ((), ())), preferred_element_type=F32)
+        edge_ref[k : k + 1, :] = edges[0:1]
+
+
+def edge_kernel(even_ref, ens_ref, cross_ref):
+    write_edges(ens_ref, even_ref[0, 0] == 0, cross_ref)
+
+
+def inside_kernel(even_ref, ens_ref, pair_ref, new_ref):
     members, _, rows, cols = ens_ref.shape
+    write_edges(ens_ref, even_ref[0, 0] == 1, pair_ref)
     lane = iota((rows, cols), 1)
     for m in range(members):
         wind = None
@@ -79,6 +78,7 @@
 def forecast_kernel(even_ref, new_ref, ens_ref, pair_ref, cross_ref, out_ref, store):
     members, _, rows, cols = ens_ref.shape
     group = members // 8
+    pitch = store.shape[1] // members
     even = even_ref[0, 0] == 1
     spot = iota((8, cols), 0)
     lane8 = iota((8, cols), 1)
@@ -99,48 +99,53 @@
             rate = side * ens_ref[m, 0].astype(F32) + DIFFUSE
             for f in range(2):
                 at = slice(m * rows, (m + 1) * rows)
-                store[f, at, :] = new_ref[f, at, :] + rate * rim[i * 2 + f]
+                store[f, m * pitch : m * pitch + rows, :] = new_ref[f, at, :] + rate * rim[i * 2 + f]
     for f in range(2):
         for r in range(rows):
-            part = store[f, pl.ds(r, members, stride=rows), :]
+            part = store[f, pl.ds(r, members, stride=pitch), :]
             at = (f * 2 + r % 2) * cols
             out_ref[r // 2, :, at : at + cols] = part.astype(BF16)
 
 
 def restore_kernel(in_ref, out_ref, store):
     members, _, rows, cols = out_ref.shape
+    pitch = store.shape[1] // members
     for f in range(2):
         for r in range(rows):
             at = (f * 2 + r % 2) * cols
-            store[f, pl.ds(r, members, stride=rows), :] = in_ref[r // 2, :, at : at + cols].astype(F32)
+            store[f, pl.ds(r, members, stride=pitch), :] = in_ref[r // 2, :, at : at + cols].astype(F32)
     for f in range(2):
         for m in range(members):
-            out_ref[m, f] = store[f, m * rows : (m + 1) * rows, :].astype(BF16)
-
-
-def observe_kernel(even_ref, local_ref, index_ref, value_ref, prec_ref, y_ref, mean_ref, pair_ref, cross_ref):
+            out_ref[m, f] = store[f, m * pitch : m * pitch + rows, :].astype(BF16)
+
+
+def write_rows(side, y_ref, mean, index_ref, value_ref, prec_ref, ref):
+    members, half = y_ref.shape
+    n = index_ref.shape[1] // 2
+    at = pl.ds(pl.multiple_of(side * n, n), n)
+    hit = iota((half, n), 0) == index_ref[:, at]
+    ref[:members, :] = jnp.dot(y_ref[...], hit.astype(BF16), preferred_element_type=F32).astype(BF16)
+    innovation = value_ref[:, at] - jnp.sum(jnp.where(hit, to_col(mean), 0.0), axis=0, keepdims=True)
+    which = iota((16, n), 0)
+    last = jnp.where(which == 0, innovation, jnp.where(which == 1, prec_ref[:, at], 0.0))
+    ref[members:, :] = last.astype(BF16)
+
+
+def observe_kernel(even_ref, local_ref, index_ref, value_ref, prec_ref, y_ref, mean_ref, cross_ref):
     members, cells = local_ref.shape
     half = cells // 2
     equivalent = local_ref[:, half:].astype(F32) + OBS_WIND * local_ref[:, :half].astype(F32)
     mean = jnp.sum(equivalent, axis=0, keepdims=True) * (1.0 / members)
     mean_ref[...] = jnp.broadcast_to(mean, mean_ref.shape)
     y_ref[...] = ((equivalent - mean) * (members - 1) ** (-0.5)).astype(BF16)
-    n = index_ref.shape[1] // 2
-    even = even_ref[0, 0]
-    for ref, side in ((cross_ref, 1 - even), (pair_ref, even)):
-        at = pl.ds(pl.multiple_of(side * n, n), n)
-        hit = iota((half, n), 0) == index_ref[:, at]
-        ref[:members, :] = jnp.dot(y_ref[...], hit.astype(BF16), preferred_element_type=F32).astype(BF16)
-        innovation = value_ref[:, at] - jnp.sum(jnp.where(hit, to_col(mean), 0.0), axis=0, keepdims=True)
-        which = iota((16, n), 0)
-        last = jnp.where(which == 0, innovation, jnp.where(which == 1, prec_ref[:, at], 0.0))
-        ref[members:, :] = last.astype(BF16)
+    write_rows(1 - even_ref[0, 0], y_ref, mean, index_ref, value_ref, prec_ref, cross_ref)
 
 
 def own_kernel(
-    mask_ref, local_ref, y_ref, observed_ref, index_ref, value_ref, prec_ref,
-    anomaly_ref, yt_ref, mean_ref, gram_ref, cover_ref, row_ref, col_ref,
+    even_ref, mask_ref, local_ref, y_ref, observed_ref, index_ref, value_ref, prec_ref,
+    pair_ref, anomaly_ref, yt_ref, mean_ref, gram_ref, cover_ref, row_ref, col_ref,
 ):
+    write_rows(even_ref[0, 0], y_ref, observed_ref[0:1, :], index_ref, value_ref, prec_ref, pair_ref)
     members, cells = local_ref.shape
     half = cells // 2
     local = local_ref[...].astype(F32)
@@ -258,32 +263,38 @@
     even = (1 - lax.axis_index("domain") % 2).astype(jnp.int32).reshape(1, 1)
 
     edge = struct((8, members // 8 * fields * rows), F32)
-    pair_edge, cross_edge = call(edge_kernel, [edge, edge], [even, ensemble], specs=[SMEM, VMEM])
+    cross_edge = call(edge_kernel, edge, [even, ensemble], specs=[SMEM, VMEM])
     cross_edge = lax.ppermute(cross_edge, "domain", crosses)
+    pair_edge, inside = call(
+        inside_kernel,
+        [edge, struct((fields, members * rows, cols), F32)],
+        [even, ensemble],
+        specs=[SMEM, VMEM],
+        flops=10**9,
+    )
     pair_edge = lax.ppermute(pair_edge, "domain", pairs)
-    inside = call(inside_kernel, struct((fields, members * rows, cols), F32), [ensemble])
     predicted = call(
         forecast_kernel,
         struct((bands, members, cells), BF16),
         [even, inside, ensemble, pair_edge, cross_edge],
-        scratch=[pltpu.VMEM((fields, members * rows, cols), F32)],
+        scratch=[pltpu.VMEM((fields, members * (rows + SKEW), cols), F32)],
         specs=[SMEM] + [VMEM] * 4,
     )
     local = lax.all_to_all(predicted, "member", split_axis=0, concat_axis=0, tiled=True).reshape(total, cells)
 
     index = obs_row * cols + obs_col
     rim = struct((total + 16, n // 2), BF16)
-    y, observed, pair_rows, cross_rows = call(
+    y, observed, cross_rows = call(
         observe_kernel,
-        [struct((total, cells // 2), BF16), struct((8, cells // 2), F32), rim, rim],
+        [struct((total, cells // 2), BF16), struct((8, cells // 2), F32), rim],
         [even, local, index, obs_value, obs_prec],
         specs=[SMEM] + [VMEM] * 4,
     )
     cross_rows = lax.ppermute(cross_rows, "domain", crosses)
-    pair_rows = lax.ppermute(pair_rows, "domain", pairs)
     own = call(
         own_kernel,
         [
+            rim,
             struct((total, cells), BF16),
             struct((cells // 2, total), BF16),
             struct((8, cells), F32),
@@ -292,10 +303,12 @@
             struct((8, cells // 2), F32),
             struct((cells // 2, 128), F32),
         ],
-        [loc_mask, local, y, observed, index, obs_value, obs_prec],
+        [even, loc_mask, local, y, observed, index, obs_value, obs_prec],
+        specs=[SMEM] + [VMEM] * 7,
         flops=2 * total * cells * cells * 3 // 4,
     )
-    anomalies, yt, mean, gram, cover, row, col = own
+    pair_rows, anomalies, yt, mean, gram, cover, row, col = own
+    pair_rows = lax.ppermute(pair_rows, "domain", pairs)
     analysis = call(
         analyse_kernel,
         struct((total, cells), BF16),
@@ -317,7 +330,7 @@
         restore_kernel,
         struct(ensemble.shape, BF16),
         [back],
-        scratch=[pltpu.VMEM((fields, members * rows, cols), F32)],
+        scratch=[pltpu.VMEM((fields, members * (rows + SKEW), cols), F32)],
     )
 
 

time: 169 us -> 165 us (0.976)
  Pallas kernels: 13.4 us -> 10.2 us
    ppermute x1, starting transfers between devices: 7.49 us -> 1.93 us  [on_device(): cross_edge = lax.ppermute(cross_edge, 'domain', crosses)]
    pallas_call x7, Pallas kernels: 13.4 us -> 10.2 us  [call(): pl.pallas_call(kernel, out_shape=shapes, in_specs=specs or [VMEM] * len(a...]
    all_to_all x1, starting transfers between devices: 15.9 us -> 18.9 us  [on_device(): lax.all_to_all(predicted, 'member', split_axis=0, concat_axis=0, tiled=True)]
    ppermute x1, starting transfers between devices: 1.93 us -> 3.93 us  [on_device(): pair_edge = lax.ppermute(pair_edge, 'domain', pairs)]
    ppermute x1, waiting for transfers between devices: 4.82 us -> 2.83 us  [on_device(): cross_rows = lax.ppermute(cross_rows, 'domain', crosses)]
  transfers between devices with their start and end apart: 5 -> 5, of which waited for: 2 -> 3; matrix products, arithmetic and copies ran while one was open for 0% -> 0% of each run, Pallas kernels for 1% -> 2%
where the time goes in v4:
time: 165 us
  waiting for transfers between devices  62.9 us (38%)
  blocking collectives  61.5 us (37%)
  starting transfers between devices  28.6 us (17%)
  Pallas kernels  10.2 us (6%)
    all_to_all x1, blocking collectives, on_device(): lax.all_to_all(analysis.reshape(bands, members, cells), 'member', split_a...  61.5 us
    all_to_all x1, waiting for transfers between devices, on_device(): lax.all_to_all(predicted, 'member', split_axis=0, concat_axis=0, tiled=True)  59.2 us
    all_to_all x1, starting transfers between devices, on_device(): lax.all_to_all(predicted, 'member', split_axis=0, concat_axis=0, tiled=True)  18.9 us
    pallas_call x7, Pallas kernels, call(): pl.pallas_call(kernel, out_shape=shapes, in_specs=specs or [VMEM] * len(a...  10.2 us
    ppermute x1, starting transfers between devices, on_device(): pair_edge = lax.ppermute(pair_edge, 'domain', pairs)  3.93 us
  transfers between devices with their start and end apart: 5, of which 3 were waited for; matrix products, arithmetic and copies ran while one was open for 0% of the time, Pallas kernels for 2%

profile of v4, /device:TPU:32, one launch (start us, length us, event | category | flops | bytes accessed | tf_op | source)
XLA Modules:
  0.0 164.6 jit_solution(6087454383076955228)
XLA Ops:
  0.0 0.0 copy-start
  0.0 1.2 copy-done
  1.2 0.4 shard_map.65
  1.6 1.9 %collective-permute-start.1 = (f32[8,512]{1,0:T(8,128)S(1)}, f32[8,512]{1,0:T(8,128)S(1)}, u32[]{:S(2)}, u32[]{:S(2)}) collective-permute-start(f32[8,512]{1,0:T(8,128)S(1)} %shard_map.65), channel_id=1, source_target_pairs={{0,15},{1,2},{2,1},{3,4},{4,3},{5,6},{6,5},{7,8},{8,7},{9,10},{10,... | collective-permute-start | bytes 49160 | tf_op jit(solution)/shard_map/ppermute | solution.py:267
  3.5 1.5 shard_map.64
  5.0 3.9 %collective-permute-start = (f32[8,512]{1,0:T(8,128)S(1)}, f32[8,512]{1,0:T(8,128)S(1)}, u32[]{:S(2)}, u32[]{:S(2)}) collective-permute-start(f32[8,512]{1,0:T(8,128)S(1)} %get-tuple-element.19), channel_id=1, source_target_pairs={{0,1},{1,0},{2,3},{3,2},{4,5},{5,4},{6,7},{7,6},{8,9},{9,8},{10,11... | collective-permute-start | bytes 49160 | tf_op jit(solution)/shard_map/ppermute | solution.py:275
  8.9 0.0 collective-permute-done.1.cross_ref
  8.9 0.8 collective-permute-done.pair_ref
  9.8 1.6 shard_map.66
  11.4 0.0 copy-start.4
  11.4 0.0 copy-start.5
  11.4 0.0 copy-start.1
  11.4 0.0 copy-start.2
  11.4 0.0 copy-start.3
  11.4 18.9 %all-to-all-start = ((bf16[32,32,512]{2,1,0:T(8,128)(2,1)}), bf16[32,32,512]{2,1,0:T(8,128)(2,1)S(1)}, u32[]{:S(2)}, u32[]{:S(2)}) async-start(bf16[32,32,512]{2,1,0:T(8,128)(2,1)} %shard_map.66), calls=%async_computation | async-start | bytes 2097152 | tf_op jit(solution)/shard_map/all_to_all | solution.py:283
  30.3 0.0 copy-done.4
  30.4 0.0 copy-done.5
  30.4 59.2 %all-to-all-done = bf16[32,32,512]{2,1,0:T(8,128)(2,1)S(1)} async-done(((bf16[32,32,512]{2,1,0:T(8,128)(2,1)}), bf16[32,32,512]{2,1,0:T(8,128)(2,1)S(1)}, u32[]{:S(2)}, u32[]{:S(2)}) %all-to-all-start) | async-done | bytes 1048608 | tf_op jit(solution)/shard_map/all_to_all | solution.py:283
  89.6 0.0 copy-done.1
  89.6 0.0 copy-done.2
  89.6 0.5 shard_map.67
  90.1 1.9 %collective-permute-start.3 = (bf16[1040,128]{1,0:T(8,128)(2,1)S(1)}, bf16[1040,128]{1,0:T(8,128)(2,1)S(1)}, u32[]{:S(2)}, u32[]{:S(2)}) collective-permute-start(bf16[1040,128]{1,0:T(8,128)(2,1)S(1)} %get-tuple-element.30), channel_id=1, source_target_pairs={{0,15},{1,2},{2,1},{3,4},{4,3},{5,6},{6,5},{7,8},{8,7},{9,10},{10,... | collective-permute-start | bytes 798728 | tf_op jit(solution)/shard_map/ppermute | solution.py:293
  92.0 0.0 copy-done.3
  92.0 1.0 shard_map.68
  93.1 1.9 %collective-permute-start.2 = (bf16[1040,128]{1,0:T(8,128)(2,1)S(1)}, bf16[1040,128]{1,0:T(8,128)(2,1)S(1)}, u32[]{:S(2)}, u32[]{:S(2)}) collective-permute-start(bf16[1040,128]{1,0:T(8,128)(2,1)S(1)} %get-tuple-element.29), channel_id=1, source_target_pairs={{0,1},{1,0},{2,3},{3,2},{4,5},{5,4},{6,7},{7,6},{8,9},{9,8},{10,11... | collective-permute-start | bytes 798728 | tf_op jit(solution)/shard_map/ppermute | solution.py:311
  95.0 2.8 %collective-permute-done.3.cross_ref = bf16[1040,128]{1,0:T(8,128)(2,1)S(1)} collective-permute-done((bf16[1040,128]{1,0:T(8,128)(2,1)S(1)}, bf16[1040,128]{1,0:T(8,128)(2,1)S(1)}, u32[]{:S(2)}, u32[]{:S(2)}) %collective-permute-start.3) | collective-permute-done | bytes 266272 | tf_op jit(solution)/shard_map/ppermute | solution.py:293
  97.8 0.0 collective-permute-done.2.pair_ref
  97.8 4.1 %shard_map.69 = bf16[1024,512]{1,0:T(8,128)(2,1)S(1)} custom-call(s32[1,1]{1,0:T(1,128)} %bitcast.even_ref, s32[1,4]{1,0:T(1,128)S(1)} %copy-done.3, bf16[1024,512]{1,0:T(8,128)(2,1)S(1)} %get-tuple-element.22.anomaly_ref, bf16[1024,256]{1,0:T(8,128)(2,1)S(1)} %get-tuple-element.20.y_ref, bf16[256,1024]{1,0:T(8,128)(2,1)S(1)} %get-tuple-element.23.yt_ref, ...), custom_call_target="tpu_custom_call" | custom-call | flops 2147483648 | bytes 3571732 | tf_op jit(solution)/shard_map/pallas_call | solution.py:21
  101.9 61.5 %all_to_all.10.in_ref = bf16[32,32,512]{2,1,0:T(8,128)(2,1)S(1)} all-to-all(bf16[32,32,512]{2,1,0:T(8,128)(2,1)S(1)} %bitcast.5), channel_id=1, replica_groups=mesh['member'=32,'domain'=16] {'member'}, dimensions={0} | all-to-all | bytes 2097152 | tf_op jit(solution)/shard_map/all_to_all | solution.py:326
  163.4 1.2 shard_map.70
  (1 shorter events, 0.0 us)
Async XLA Ops:
  0.0 1.2 copy-start
  1.6 7.3 %collective-permute-start.1 = (f32[8,512]{1,0:T(8,128)S(1)}, f32[8,512]{1,0:T(8,128)S(1)}, u32[]{:S(2)}, u32[]{:S(2)}) collective-permute-start(f32[8,512]{1,0:T(8,128)S(1)} %shard_map.65), channel_id=1, source_target_pairs={{0,15},{1,2},{2,1},{3,4},{4,3},{5,6},{6,5},{7,8},{8,7},{9,10},{10,... | collective-permute-start | bytes 49160 | tf_op jit(solution)/shard_map/ppermute | solution.py:267
  5.0 4.8 %collective-permute-start = (f32[8,512]{1,0:T(8,128)S(1)}, f32[8,512]{1,0:T(8,128)S(1)}, u32[]{:S(2)}, u32[]{:S(2)}) collective-permute-start(f32[8,512]{1,0:T(8,128)S(1)} %get-tuple-element.19), channel_id=1, source_target_pairs={{0,1},{1,0},{2,3},{3,2},{4,5},{5,4},{6,7},{7,6},{8,9},{9,8},{10,11... | collective-permute-start | bytes 49160 | tf_op jit(solution)/shard_map/ppermute | solution.py:275
  11.4 18.9 %copy-start.4 = (s32[1,256]{1,0:T(1,128)S(1)}, s32[1,256]{1,0:T(1,128)}, u32[]{:S(2)}) copy-start(s32[1,256]{1,0:T(1,128)} %param.10) | copy-start | bytes 3076
  11.4 19.0 %copy-start.5 = (s32[1,256]{1,0:T(1,128)S(1)}, s32[1,256]{1,0:T(1,128)}, u32[]{:S(2)}) copy-start(s32[1,256]{1,0:T(1,128)} %param.9) | copy-start | bytes 3076
  11.4 78.2 %copy-start.1 = (f32[1,256]{1,0:T(1,128)S(1)}, f32[1,256]{1,0:T(1,128)}, u32[]{:S(2)}) copy-start(f32[1,256]{1,0:T(1,128)} %value_ref.3) | copy-start | bytes 3076
  11.4 78.2 %copy-start.2 = (f32[1,256]{1,0:T(1,128)S(1)}, f32[1,256]{1,0:T(1,128)}, u32[]{:S(2)}) copy-start(f32[1,256]{1,0:T(1,128)} %prec_ref.3) | copy-start | bytes 3076
  11.4 80.6 %copy-start.3 = (s32[1,4]{1,0:T(1,128)S(1)}, s32[1,4]{1,0:T(1,128)}, u32[]{:S(2)}) copy-start(s32[1,4]{1,0:T(1,128)} %mask_ref.3) | copy-start | bytes 52
  11.4 78.2 %all-to-all-start = ((bf16[32,32,512]{2,1,0:T(8,128)(2,1)}), bf16[32,32,512]{2,1,0:T(8,128)(2,1)S(1)}, u32[]{:S(2)}, u32[]{:S(2)}) async-start(bf16[32,32,512]{2,1,0:T(8,128)(2,1)} %shard_map.66), calls=%async_computation | async-start | bytes 2097152 | tf_op jit(solution)/shard_map/all_to_all | solution.py:283
  90.1 7.7 %collective-permute-start.3 = (bf16[1040,128]{1,0:T(8,128)(2,1)S(1)}, bf16[1040,128]{1,0:T(8,128)(2,1)S(1)}, u32[]{:S(2)}, u32[]{:S(2)}) collective-permute-start(bf16[1040,128]{1,0:T(8,128)(2,1)S(1)} %get-tuple-element.30), channel_id=1, source_target_pairs={{0,15},{1,2},{2,1},{3,4},{4,3},{5,6},{6,5},{7,8},{8,7},{9,10},{10,... | collective-permute-start | bytes 798728 | tf_op jit(solution)/shard_map/ppermute | solution.py:293
  93.1 4.8 %collective-permute-start.2 = (bf16[1040,128]{1,0:T(8,128)(2,1)S(1)}, bf16[1040,128]{1,0:T(8,128)(2,1)S(1)}, u32[]{:S(2)}, u32[]{:S(2)}) collective-permute-start(bf16[1040,128]{1,0:T(8,128)(2,1)S(1)} %get-tuple-element.29), channel_id=1, source_target_pairs={{0,1},{1,0},{2,3},{3,2},{4,5},{5,4},{6,7},{7,6},{8,9},{9,8},{10,11... | collective-permute-start | bytes 798728 | tf_op jit(solution)/shard_map/ppermute | solution.py:311

commit v5 on v4

--- a/solution.py
+++ b/solution.py
@@ -13,16 +13,17 @@
 BF16 = jnp.bfloat16
 VMEM = pl.BlockSpec(memory_space=pltpu.VMEM)
 SMEM = pl.BlockSpec(memory_space=pltpu.SMEM)
+HBM = pl.BlockSpec(memory_space=pltpu.HBM)
 PARAMS = pltpu.CompilerParams(vmem_limit_bytes=40 * 1024 * 1024)
 
 
-def call(kernel, shapes, args, scratch=(), specs=None, flops=0):
+def call(kernel, shapes, args, scratch=(), specs=None, flops=0, out=VMEM):
     nbytes = sum(a.size * a.dtype.itemsize for a in args)
     return pl.pallas_call(
         kernel,
         out_shape=shapes,
         in_specs=specs or [VMEM] * len(args),
-        out_specs=jax.tree.map(lambda _: VMEM, shapes),
+        out_specs=jax.tree.map(lambda _: out, shapes),
         scratch_shapes=list(scratch),
         compiler_params=PARAMS,
         cost_estimate=pl.CostEstimate(flops=flops, bytes_accessed=nbytes, transcendentals=0),
@@ -107,23 +108,30 @@
             out_ref[r // 2, :, at : at + cols] = part.astype(BF16)
 
 
-def restore_kernel(in_ref, out_ref, store):
-    members, _, rows, cols = out_ref.shape
+def restore_kernel(in_ref, out_ref, store, done, sems):
+    members, _, rows, cols = done.shape
     pitch = store.shape[1] // members
+    half = members // 2
+    copies = []
     for f in range(2):
         for r in range(rows):
             at = (f * 2 + r % 2) * cols
             store[f, pl.ds(r, members, stride=pitch), :] = in_ref[r // 2, :, at : at + cols].astype(F32)
-    for f in range(2):
-        for m in range(members):
-            out_ref[m, f] = store[f, m * pitch : m * pitch + rows, :].astype(BF16)
-
-
-def write_rows(side, y_ref, mean, index_ref, value_ref, prec_ref, ref):
+        for p in range(2):
+            for m in range(p * half, (p + 1) * half):
+                done[m, f] = store[f, m * pitch : m * pitch + rows, :].astype(BF16)
+            part = (pl.ds(p * half, half), f)
+            copies.append(pltpu.make_async_copy(done.at[part], out_ref.at[part], sems.at[f * 2 + p]))
+            copies[-1].start()
+    for copy in copies:
+        copy.wait()
+
+
+def write_rows(side, y_ref, mean, row_ref, col_ref, value_ref, prec_ref, ref):
     members, half = y_ref.shape
-    n = index_ref.shape[1] // 2
+    n = row_ref.shape[1] // 2
     at = pl.ds(pl.multiple_of(side * n, n), n)
-    hit = iota((half, n), 0) == index_ref[:, at]
+    hit = iota((half, n), 0) == row_ref[:, at] * (half // 2) + col_ref[:, at]
     ref[:members, :] = jnp.dot(y_ref[...], hit.astype(BF16), preferred_element_type=F32).astype(BF16)
     innovation = value_ref[:, at] - jnp.sum(jnp.where(hit, to_col(mean), 0.0), axis=0, keepdims=True)
     which = iota((16, n), 0)
@@ -131,21 +139,21 @@
     ref[members:, :] = last.astype(BF16)
 
 
-def observe_kernel(even_ref, local_ref, index_ref, value_ref, prec_ref, y_ref, mean_ref, cross_ref):
+def observe_kernel(even_ref, local_ref, row_ref, col_ref, value_ref, prec_ref, y_ref, mean_ref, cross_ref):
     members, cells = local_ref.shape
     half = cells // 2
     equivalent = local_ref[:, half:].astype(F32) + OBS_WIND * local_ref[:, :half].astype(F32)
     mean = jnp.sum(equivalent, axis=0, keepdims=True) * (1.0 / members)
     mean_ref[...] = jnp.broadcast_to(mean, mean_ref.shape)
     y_ref[...] = ((equivalent - mean) * (members - 1) ** (-0.5)).astype(BF16)
-    write_rows(1 - even_ref[0, 0], y_ref, mean, index_ref, value_ref, prec_ref, cross_ref)
+    write_rows(1 - even_ref[0, 0], y_ref, mean, row_ref, col_ref, value_ref, prec_ref, cross_ref)
 
 
 def own_kernel(
-    even_ref, mask_ref, local_ref, y_ref, observed_ref, index_ref, value_ref, prec_ref,
-    pair_ref, anomaly_ref, yt_ref, mean_ref, gram_ref, cover_ref, row_ref, col_ref,
+    even_ref, mask_ref, local_ref, y_ref, observed_ref, row_ref, col_ref, value_ref, prec_ref,
+    pair_ref, anomaly_ref, yt_ref, mean_ref, gram_ref, cover_ref, across_ref, down_ref,
 ):
-    write_rows(even_ref[0, 0], y_ref, observed_ref[0:1, :], index_ref, value_ref, prec_ref, pair_ref)
+    write_rows(even_ref[0, 0], y_ref, observed_ref[0:1, :], row_ref, col_ref, value_ref, prec_ref, pair_ref)
     members, cells = local_ref.shape
     half = cells // 2
     local = local_ref[...].astype(F32)
@@ -156,8 +164,8 @@
     gram_ref[...] = jnp.dot(yt_ref[...], y_ref[...], preferred_element_type=F32)
     cover_ref[...] = jnp.dot(yt_ref[...], anomaly_ref[...], preferred_element_type=F32)
 
-    n = index_ref.shape[1]
-    hit = iota((half, n), 0) == index_ref[...]
+    n = row_ref.shape[1]
+    hit = iota((half, n), 0) == row_ref[...] * (half // 2) + col_ref[...]
     observed_mean = jnp.sum(jnp.where(hit, to_col(observed_ref[0:1, :]), 0.0), axis=0, keepdims=True)
     innovation = (value_ref[...] - observed_mean).astype(BF16).astype(F32)
     mask = jnp.where(iota((1, n), 1) < n // 2, mask_ref[0:1, 1:2].astype(F32), mask_ref[0:1, 2:3].astype(F32))
@@ -165,9 +173,9 @@
     own_d = jnp.sum(jnp.where(hit, weight, 0.0), axis=1, keepdims=True)
     own_g = jnp.sum(jnp.where(hit, weight * innovation, 0.0), axis=1, keepdims=True)
     which = iota((8, half), 0)
-    row_ref[...] = jnp.where(which == 0, to_row(own_d), to_row(own_g))
+    across_ref[...] = jnp.where(which == 0, to_row(own_d), to_row(own_g))
     lane = iota((half, 128), 1)
-    col_ref[...] = jnp.where(lane == 0, own_d, own_g)
+    down_ref[...] = jnp.where(lane == 0, own_d, own_g)
 
 
 def analyse_kernel(
@@ -184,9 +192,8 @@
     zt[:half, :] = yt_ref[...]
     zt[half:, :] = z[:, half:].T
     rim = jnp.dot(zt[half:, :], z[...], preferred_element_type=F32)
-    cross = jnp.dot(yt_ref[...], z[:, half:], preferred_element_type=F32)
     gram[:half, :half] = gram_ref[...]
-    gram[:half, half:] = cross
+    gram[:half, half:] = rim[:, :half].T
     gram[half:, :] = rim
     cover[:half, :] = cover_ref[...]
     cover[half:, :] = jnp.dot(zt[half:, :], anomaly_ref[...], preferred_element_type=F32)
@@ -209,12 +216,23 @@
     m = cover[...]
     inner = (k * d_col * d_row).astype(BF16)
     u[...] = jnp.dot(z[...], inner, preferred_element_type=F32).astype(BF16)
+    step = 256
+    blocks = members // step
     most = jnp.zeros((1, 1), F32)
-    step = 256
-    for i in range(members // step):
-        squared = jnp.dot(u[i * step : (i + 1) * step, :], zt[...], preferred_element_type=F32)
-        total = jnp.sum(jnp.abs(squared), axis=1, keepdims=True)
-        most = jnp.maximum(most, jnp.max(total, axis=0, keepdims=True))
+    mirrored = [jnp.zeros((1, step), F32) for _ in range(blocks)]
+    for i in range(blocks):
+        total = jnp.zeros((step, 1), F32)
+        for j in range(i, blocks):
+            squared = jnp.abs(
+                jnp.dot(
+                    u[i * step : (i + 1) * step, :], zt[:, j * step : (j + 1) * step], preferred_element_type=F32
+                )
+            )
+            total = total + jnp.sum(squared, axis=1, keepdims=True)
+            if j > i:
+                mirrored[j] = mirrored[j] + jnp.sum(squared, axis=0, keepdims=True)
+        sums = to_row(total) + mirrored[i]
+        most = jnp.maximum(most, jnp.max(sums, axis=1, keepdims=True))
     row_bound = jnp.sqrt(most)
     half_width = (row_bound + 1.0) / 2.0
     theta = 1.0 + half_width
@@ -282,13 +300,12 @@
     )
     local = lax.all_to_all(predicted, "member", split_axis=0, concat_axis=0, tiled=True).reshape(total, cells)
 
-    index = obs_row * cols + obs_col
     rim = struct((total + 16, n // 2), BF16)
     y, observed, cross_rows = call(
         observe_kernel,
         [struct((total, cells // 2), BF16), struct((8, cells // 2), F32), rim],
-        [even, local, index, obs_value, obs_prec],
-        specs=[SMEM] + [VMEM] * 4,
+        [even, local, obs_row, obs_col, obs_value, obs_prec],
+        specs=[SMEM] + [VMEM] * 5,
     )
     cross_rows = lax.ppermute(cross_rows, "domain", crosses)
     own = call(
@@ -303,8 +320,8 @@
             struct((8, cells // 2), F32),
             struct((cells // 2, 128), F32),
         ],
-        [even, loc_mask, local, y, observed, index, obs_value, obs_prec],
-        specs=[SMEM] + [VMEM] * 7,
+        [even, loc_mask, local, y, observed, obs_row, obs_col, obs_value, obs_prec],
+        specs=[SMEM] + [VMEM] * 8,
         flops=2 * total * cells * cells * 3 // 4,
     )
     pair_rows, anomalies, yt, mean, gram, cover, row, col = own
@@ -330,7 +347,12 @@
         restore_kernel,
         struct(ensemble.shape, BF16),
         [back],
-        scratch=[pltpu.VMEM((fields, members * (rows + SKEW), cols), F32)],
+        scratch=[
+            pltpu.VMEM((fields, members * (rows + SKEW), cols), F32),
+            pltpu.VMEM(ensemble.shape, BF16),
+            pltpu.SemaphoreType.DMA((4,)),
+        ],
+        out=HBM,
     )
 
 

time: 165 us -> 163 us (0.988)
  blocking collectives: 61.5 us -> 139 us
  waiting for transfers between devices: 62.9 us -> 3.67 us
  starting transfers between devices: 28.6 us -> 9.7 us
    all_to_all x0 -> x1, blocking collectives: none -> 78 us  [on_device(): lax.all_to_all(predicted, 'member', split_axis=0, concat_axis=0, tiled=True)]
    all_to_all x1 -> x0, waiting for transfers between devices: 59.2 us -> none  [on_device(): lax.all_to_all(predicted, 'member', split_axis=0, concat_axis=0, tiled=True)]
    all_to_all x1 -> x0, starting transfers between devices: 18.9 us -> none  [on_device(): lax.all_to_all(predicted, 'member', split_axis=0, concat_axis=0, tiled=True)]
  transfers between devices with their start and end apart: 5 -> 4, of which waited for: 3 -> 2; matrix products, arithmetic and copies ran while one was open for 0% -> 0% of each run, Pallas kernels for 2% -> 2%
where the time goes in v5:
time: 163 us
  blocking collectives  139 us (85%)
  starting transfers between devices  9.7 us (6%)
  Pallas kernels  8.66 us (5%)
  waiting for transfers between devices  3.67 us (2%)
    all_to_all x1, blocking collectives, on_device(): lax.all_to_all(predicted, 'member', split_axis=0, concat_axis=0, tiled=True)  78 us
    all_to_all x1, blocking collectives, on_device(): lax.all_to_all(analysis.reshape(bands, members, cells), 'member', split_a...  61.5 us
    pallas_call x7, Pallas kernels, call(): pl.pallas_call(kernel, out_shape=shapes, in_specs=specs or [VMEM] * len(a...  8.66 us
    ppermute x1, starting transfers between devices, on_device(): pair_edge = lax.ppermute(pair_edge, 'domain', pairs)  3.93 us
  transfers between devices with their start and end apart: 4, of which 2 were waited for; matrix products, arithmetic and copies ran while one was open for 0% of the time, Pallas kernels for 2%

profile of v5, /device:TPU:32, one launch (start us, length us, event | category | flops | bytes accessed | tf_op | source)
XLA Modules:
  0.0 162.9 jit_solution(10879242987331466523)
XLA Ops:
  0.0 0.0 copy-start
  0.0 1.2 copy-done
  1.2 0.4 shard_map.65
  1.6 1.9 %collective-permute-start.1 = (f32[8,512]{1,0:T(8,128)S(1)}, f32[8,512]{1,0:T(8,128)S(1)}, u32[]{:S(2)}, u32[]{:S(2)}) collective-permute-start(f32[8,512]{1,0:T(8,128)S(1)} %shard_map.65), channel_id=1, source_target_pairs={{0,15},{1,2},{2,1},{3,4},{4,3},{5,6},{6,5},{7,8},{8,7},{9,10},{10,... | collective-permute-start | bytes 49160 | tf_op jit(solution)/shard_map/ppermute | solution.py:285
  3.5 1.5 shard_map.64
  5.0 3.9 %collective-permute-start = (f32[8,512]{1,0:T(8,128)S(1)}, f32[8,512]{1,0:T(8,128)S(1)}, u32[]{:S(2)}, u32[]{:S(2)}) collective-permute-start(f32[8,512]{1,0:T(8,128)S(1)} %get-tuple-element.19), channel_id=1, source_target_pairs={{0,1},{1,0},{2,3},{3,2},{4,5},{5,4},{6,7},{7,6},{8,9},{9,8},{10,11... | collective-permute-start | bytes 49160 | tf_op jit(solution)/shard_map/ppermute | solution.py:293
  8.9 0.0 collective-permute-done.1.cross_ref
  8.9 0.8 collective-permute-done.pair_ref
  9.8 0.7 shard_map.66
  10.4 0.0 copy-start.1
  10.4 0.0 copy-start.2
  10.5 0.0 copy-start.3
  10.5 0.0 copy-start.4
  10.5 0.0 copy-start.5
  10.5 78.0 %all_to_all.10 = bf16[32,32,512]{2,1,0:T(8,128)(2,1)S(1)} all-to-all(bf16[32,32,512]{2,1,0:T(8,128)(2,1)S(1)} %shard_map.66), channel_id=1, replica_groups=mesh['member'=32,'domain'=16] {'member'}, dimensions={0} | all-to-all | bytes 2097152 | tf_op jit(solution)/shard_map/all_to_all | solution.py:301
  88.4 0.0 copy-done.1
  88.4 0.0 copy-done.2
  88.4 0.0 copy-done.3
  88.5 0.0 copy-done.4
  88.5 0.5 shard_map.67
  89.0 1.9 %collective-permute-start.3 = (bf16[1040,128]{1,0:T(8,128)(2,1)S(1)}, bf16[1040,128]{1,0:T(8,128)(2,1)S(1)}, u32[]{:S(2)}, u32[]{:S(2)}) collective-permute-start(bf16[1040,128]{1,0:T(8,128)(2,1)S(1)} %get-tuple-element.30), channel_id=1, source_target_pairs={{0,15},{1,2},{2,1},{3,4},{4,3},{5,6},{6,5},{7,8},{8,7},{9,10},{10,... | collective-permute-start | bytes 798728 | tf_op jit(solution)/shard_map/ppermute | solution.py:310
  90.9 0.0 copy-done.5
  90.9 1.0 shard_map.68
  91.9 1.9 %collective-permute-start.2 = (bf16[1040,128]{1,0:T(8,128)(2,1)S(1)}, bf16[1040,128]{1,0:T(8,128)(2,1)S(1)}, u32[]{:S(2)}, u32[]{:S(2)}) collective-permute-start(bf16[1040,128]{1,0:T(8,128)(2,1)S(1)} %get-tuple-element.29), channel_id=1, source_target_pairs={{0,1},{1,0},{2,3},{3,2},{4,5},{5,4},{6,7},{7,6},{8,9},{9,8},{10,11... | collective-permute-start | bytes 798728 | tf_op jit(solution)/shard_map/ppermute | solution.py:328
  93.8 2.9 %collective-permute-done.3.cross_ref = bf16[1040,128]{1,0:T(8,128)(2,1)S(1)} collective-permute-done((bf16[1040,128]{1,0:T(8,128)(2,1)S(1)}, bf16[1040,128]{1,0:T(8,128)(2,1)S(1)}, u32[]{:S(2)}, u32[]{:S(2)}) %collective-permute-start.3) | collective-permute-done | bytes 266272 | tf_op jit(solution)/shard_map/ppermute | solution.py:310
  96.7 0.0 collective-permute-done.2.pair_ref
  96.7 3.6 %shard_map.69 = bf16[1024,512]{1,0:T(8,128)(2,1)S(1)} custom-call(s32[1,1]{1,0:T(1,128)} %bitcast.even_ref, s32[1,4]{1,0:T(1,128)S(1)} %copy-done.5, bf16[1024,512]{1,0:T(8,128)(2,1)S(1)} %get-tuple-element.22.anomaly_ref, bf16[1024,256]{1,0:T(8,128)(2,1)S(1)} %get-tuple-element.20.y_ref, bf16[256,1024]{1,0:T(8,128)(2,1)S(1)} %get-tuple-element.23.yt_ref, ...), custom_call_target="tpu_custom_call" | custom-call | flops 2147483648 | bytes 3571732 | tf_op jit(solution)/shard_map/pallas_call | solution.py:22
  100.3 61.5 %all_to_all.11.in_ref = bf16[32,32,512]{2,1,0:T(8,128)(2,1)S(1)} all-to-all(bf16[32,32,512]{2,1,0:T(8,128)(2,1)S(1)} %bitcast.5), channel_id=1, replica_groups=mesh['member'=32,'domain'=16] {'member'}, dimensions={0} | all-to-all | bytes 2097152 | tf_op jit(solution)/shard_map/all_to_all | solution.py:343
  161.8 1.1 shard_map.70
Async XLA Ops:
  0.0 1.2 copy-start
  1.6 7.3 %collective-permute-start.1 = (f32[8,512]{1,0:T(8,128)S(1)}, f32[8,512]{1,0:T(8,128)S(1)}, u32[]{:S(2)}, u32[]{:S(2)}) collective-permute-start(f32[8,512]{1,0:T(8,128)S(1)} %shard_map.65), channel_id=1, source_target_pairs={{0,15},{1,2},{2,1},{3,4},{4,3},{5,6},{6,5},{7,8},{8,7},{9,10},{10,... | collective-permute-start | bytes 49160 | tf_op jit(solution)/shard_map/ppermute | solution.py:285
  5.0 4.8 %collective-permute-start = (f32[8,512]{1,0:T(8,128)S(1)}, f32[8,512]{1,0:T(8,128)S(1)}, u32[]{:S(2)}, u32[]{:S(2)}) collective-permute-start(f32[8,512]{1,0:T(8,128)S(1)} %get-tuple-element.19), channel_id=1, source_target_pairs={{0,1},{1,0},{2,3},{3,2},{4,5},{5,4},{6,7},{7,6},{8,9},{9,8},{10,11... | collective-permute-start | bytes 49160 | tf_op jit(solution)/shard_map/ppermute | solution.py:293
  10.4 78.0 %copy-start.1 = (s32[1,256]{1,0:T(1,128)S(1)}, s32[1,256]{1,0:T(1,128)}, u32[]{:S(2)}) copy-start(s32[1,256]{1,0:T(1,128)} %row_ref.3) | copy-start | bytes 3076
  10.4 78.0 %copy-start.2 = (s32[1,256]{1,0:T(1,128)S(1)}, s32[1,256]{1,0:T(1,128)}, u32[]{:S(2)}) copy-start(s32[1,256]{1,0:T(1,128)} %col_ref.3) | copy-start | bytes 3076
  10.5 78.0 %copy-start.3 = (f32[1,256]{1,0:T(1,128)S(1)}, f32[1,256]{1,0:T(1,128)}, u32[]{:S(2)}) copy-start(f32[1,256]{1,0:T(1,128)} %value_ref.3) | copy-start | bytes 3076
  10.5 78.0 %copy-start.4 = (f32[1,256]{1,0:T(1,128)S(1)}, f32[1,256]{1,0:T(1,128)}, u32[]{:S(2)}) copy-start(f32[1,256]{1,0:T(1,128)} %prec_ref.3) | copy-start | bytes 3076
  10.5 80.4 %copy-start.5 = (s32[1,4]{1,0:T(1,128)S(1)}, s32[1,4]{1,0:T(1,128)}, u32[]{:S(2)}) copy-start(s32[1,4]{1,0:T(1,128)} %mask_ref.3) | copy-start | bytes 52
  89.0 7.7 %collective-permute-start.3 = (bf16[1040,128]{1,0:T(8,128)(2,1)S(1)}, bf16[1040,128]{1,0:T(8,128)(2,1)S(1)}, u32[]{:S(2)}, u32[]{:S(2)}) collective-permute-start(bf16[1040,128]{1,0:T(8,128)(2,1)S(1)} %get-tuple-element.30), channel_id=1, source_target_pairs={{0,15},{1,2},{2,1},{3,4},{4,3},{5,6},{6,5},{7,8},{8,7},{9,10},{10,... | collective-permute-start | bytes 798728 | tf_op jit(solution)/shard_map/ppermute | solution.py:310
  91.9 4.8 %collective-permute-start.2 = (bf16[1040,128]{1,0:T(8,128)(2,1)S(1)}, bf16[1040,128]{1,0:T(8,128)(2,1)S(1)}, u32[]{:S(2)}, u32[]{:S(2)}) collective-permute-start(bf16[1040,128]{1,0:T(8,128)(2,1)S(1)} %get-tuple-element.29), channel_id=1, source_target_pairs={{0,1},{1,0},{2,3},{3,2},{4,5},{5,4},{6,7},{7,6},{8,9},{9,8},{10,11... | collective-permute-start | bytes 798728 | tf_op jit(solution)/shard_map/ppermute | solution.py:328

commit v6 on v5

--- a/solution.py
+++ b/solution.py
@@ -54,13 +54,13 @@
         edge_ref[k : k + 1, :] = edges[0:1]
 
 
-def edge_kernel(even_ref, ens_ref, cross_ref):
+def edge_kernel(even_ref, ens_ref, pair_ref, cross_ref):
     write_edges(ens_ref, even_ref[0, 0] == 0, cross_ref)
-
-
-def inside_kernel(even_ref, ens_ref, pair_ref, new_ref):
+    write_edges(ens_ref, even_ref[0, 0] == 1, pair_ref)
+
+
+def inside_kernel(ens_ref, new_ref):
     members, _, rows, cols = ens_ref.shape
-    write_edges(ens_ref, even_ref[0, 0] == 1, pair_ref)
     lane = iota((rows, cols), 1)
     for m in range(members):
         wind = None
@@ -281,16 +281,10 @@
     even = (1 - lax.axis_index("domain") % 2).astype(jnp.int32).reshape(1, 1)
 
     edge = struct((8, members // 8 * fields * rows), F32)
-    cross_edge = call(edge_kernel, edge, [even, ensemble], specs=[SMEM, VMEM])
+    pair_edge, cross_edge = call(edge_kernel, [edge, edge], [even, ensemble], specs=[SMEM, VMEM])
+    pair_edge = lax.ppermute(pair_edge, "domain", pairs)
     cross_edge = lax.ppermute(cross_edge, "domain", crosses)
-    pair_edge, inside = call(
-        inside_kernel,
-        [edge, struct((fields, members * rows, cols), F32)],
-        [even, ensemble],
-        specs=[SMEM, VMEM],
-        flops=10**9,
-    )
-    pair_edge = lax.ppermute(pair_edge, "domain", pairs)
+    inside = call(inside_kernel, struct((fields, members * rows, cols), F32), [ensemble], flops=10**9)
     predicted = call(
         forecast_kernel,
         struct((bands, members, cells), BF16),

time: 163 us -> 164 us (level)
  starting transfers between devices: 9.7 us -> 13.3 us
  blocking collectives: 139 us -> 137 us
    ppermute x1, starting transfers between devices: 1.93 us -> 7.49 us  [on_device(): cross_edge = lax.ppermute(cross_edge, 'domain', crosses)]
    all_to_all x1, blocking collectives: 78 us -> 75.1 us  [on_device(): lax.all_to_all(predicted, 'member', split_axis=0, concat_axis=0, tiled=True)]
    ppermute x1, starting transfers between devices: 3.93 us -> 1.93 us  [on_device(): pair_edge = lax.ppermute(pair_edge, 'domain', pairs)]
  transfers between devices with their start and end apart: 4 -> 4, of which waited for: 2 -> 1; matrix products, arithmetic and copies ran while one was open for 0% -> 0% of each run, Pallas kernels for 2% -> 1%
where the time goes in v6:
time: 164 us; the launch traced here: 163 us
  blocking collectives  137 us (84%)
  starting transfers between devices  13.3 us (8%)
  Pallas kernels  8.9 us (5%)
  waiting for transfers between devices  2.87 us (2%)
    all_to_all x1, blocking collectives, on_device(): lax.all_to_all(predicted, 'member', split_axis=0, concat_axis=0, tiled=True)  75.1 us
    all_to_all x1, blocking collectives, on_device(): lax.all_to_all(analysis.reshape(bands, members, cells), 'member', split_a...  61.9 us
    pallas_call x7, Pallas kernels, call(): pl.pallas_call(kernel, out_shape=shapes, in_specs=specs or [VMEM] * len(a...  8.9 us
    ppermute x1, starting transfers between devices, on_device(): cross_edge = lax.ppermute(cross_edge, 'domain', crosses)  7.49 us
  transfers between devices with their start and end apart: 4, of which 1 were waited for; matrix products, arithmetic and copies ran while one was open for 0% of the time, Pallas kernels for 1%

profile of v6, /device:TPU:32, one launch (start us, length us, event | category | flops | bytes accessed | tf_op | source)
XLA Modules:
  0.0 163.4 jit_solution(2711281396277935912)
XLA Ops:
  0.0 0.0 copy-start
  0.0 1.2 copy-done
  1.2 0.6 shard_map.65
  1.9 1.9 %collective-permute-start = (f32[8,512]{1,0:T(8,128)S(1)}, f32[8,512]{1,0:T(8,128)S(1)}, u32[]{:S(2)}, u32[]{:S(2)}) collective-permute-start(f32[8,512]{1,0:T(8,128)S(1)} %get-tuple-element.18), channel_id=1, source_target_pairs={{0,1},{1,0},{2,3},{3,2},{4,5},{5,4},{6,7},{7,6},{8,9},{9,8},{10,11... | collective-permute-start | bytes 49160 | tf_op jit(solution)/shard_map/ppermute | solution.py:285
  3.8 7.5 %collective-permute-start.1 = (f32[8,512]{1,0:T(8,128)S(1)}, f32[8,512]{1,0:T(8,128)S(1)}, u32[]{:S(2)}, u32[]{:S(2)}) collective-permute-start(f32[8,512]{1,0:T(8,128)S(1)} %get-tuple-element.19), channel_id=1, source_target_pairs={{0,15},{1,2},{2,1},{3,4},{4,3},{5,6},{6,5},{7,8},{8,7},{9,10},{10,... | collective-permute-start | bytes 49160 | tf_op jit(solution)/shard_map/ppermute | solution.py:286
  11.3 1.4 shard_map.64.new_ref
  12.7 0.0 collective-permute-done.pair_ref
  12.8 0.0 collective-permute-done.1.cross_ref
  12.8 0.7 shard_map.66
  13.4 0.0 copy-start.1
  13.4 0.0 copy-start.2
  13.5 0.0 copy-start.3
  13.5 0.0 copy-start.4
  13.5 0.0 copy-start.5
  13.5 75.1 %all_to_all.10 = bf16[32,32,512]{2,1,0:T(8,128)(2,1)S(1)} all-to-all(bf16[32,32,512]{2,1,0:T(8,128)(2,1)S(1)} %shard_map.66), channel_id=1, replica_groups=mesh['member'=32,'domain'=16] {'member'}, dimensions={0} | all-to-all | bytes 2097152 | tf_op jit(solution)/shard_map/all_to_all | solution.py:295
  88.6 0.0 copy-done.1
  88.6 0.0 copy-done.2
  88.6 0.0 copy-done.3
  88.6 0.0 copy-done.4
  88.6 0.5 shard_map.67
  89.1 1.9 %collective-permute-start.3 = (bf16[1040,128]{1,0:T(8,128)(2,1)S(1)}, bf16[1040,128]{1,0:T(8,128)(2,1)S(1)}, u32[]{:S(2)}, u32[]{:S(2)}) collective-permute-start(bf16[1040,128]{1,0:T(8,128)(2,1)S(1)} %get-tuple-element.30), channel_id=1, source_target_pairs={{0,15},{1,2},{2,1},{3,4},{4,3},{5,6},{6,5},{7,8},{8,7},{9,10},{10,... | collective-permute-start | bytes 798728 | tf_op jit(solution)/shard_map/ppermute | solution.py:304
  91.0 0.0 copy-done.5
  91.0 1.0 shard_map.68
  92.0 1.9 %collective-permute-start.2 = (bf16[1040,128]{1,0:T(8,128)(2,1)S(1)}, bf16[1040,128]{1,0:T(8,128)(2,1)S(1)}, u32[]{:S(2)}, u32[]{:S(2)}) collective-permute-start(bf16[1040,128]{1,0:T(8,128)(2,1)S(1)} %get-tuple-element.29), channel_id=1, source_target_pairs={{0,1},{1,0},{2,3},{3,2},{4,5},{5,4},{6,7},{7,6},{8,9},{9,8},{10,11... | collective-permute-start | bytes 798728 | tf_op jit(solution)/shard_map/ppermute | solution.py:322
  94.0 2.9 %collective-permute-done.3.cross_ref = bf16[1040,128]{1,0:T(8,128)(2,1)S(1)} collective-permute-done((bf16[1040,128]{1,0:T(8,128)(2,1)S(1)}, bf16[1040,128]{1,0:T(8,128)(2,1)S(1)}, u32[]{:S(2)}, u32[]{:S(2)}) %collective-permute-start.3) | collective-permute-done | bytes 266272 | tf_op jit(solution)/shard_map/ppermute | solution.py:304
  96.8 0.0 collective-permute-done.2.pair_ref
  96.8 3.6 %shard_map.69 = bf16[1024,512]{1,0:T(8,128)(2,1)S(1)} custom-call(s32[1,1]{1,0:T(1,128)} %bitcast.even_ref, s32[1,4]{1,0:T(1,128)S(1)} %copy-done.5, bf16[1024,512]{1,0:T(8,128)(2,1)S(1)} %get-tuple-element.22.anomaly_ref, bf16[1024,256]{1,0:T(8,128)(2,1)S(1)} %get-tuple-element.20.y_ref, bf16[256,1024]{1,0:T(8,128)(2,1)S(1)} %get-tuple-element.23.yt_ref, ...), custom_call_target="tpu_custom_call" | custom-call | flops 2147483648 | bytes 3571732 | tf_op jit(solution)/shard_map/pallas_call | solution.py:22
  100.4 61.9 %all_to_all.11.in_ref = bf16[32,32,512]{2,1,0:T(8,128)(2,1)S(1)} all-to-all(bf16[32,32,512]{2,1,0:T(8,128)(2,1)S(1)} %bitcast.5), channel_id=1, replica_groups=mesh['member'=32,'domain'=16] {'member'}, dimensions={0} | all-to-all | bytes 2097152 | tf_op jit(solution)/shard_map/all_to_all | solution.py:337
  162.3 1.1 shard_map.70
Async XLA Ops:
  0.0 1.2 copy-start
  1.9 10.9 %collective-permute-start = (f32[8,512]{1,0:T(8,128)S(1)}, f32[8,512]{1,0:T(8,128)S(1)}, u32[]{:S(2)}, u32[]{:S(2)}) collective-permute-start(f32[8,512]{1,0:T(8,128)S(1)} %get-tuple-element.18), channel_id=1, source_target_pairs={{0,1},{1,0},{2,3},{3,2},{4,5},{5,4},{6,7},{7,6},{8,9},{9,8},{10,11... | collective-permute-start | bytes 49160 | tf_op jit(solution)/shard_map/ppermute | solution.py:285
  3.8 8.9 %collective-permute-start.1 = (f32[8,512]{1,0:T(8,128)S(1)}, f32[8,512]{1,0:T(8,128)S(1)}, u32[]{:S(2)}, u32[]{:S(2)}) collective-permute-start(f32[8,512]{1,0:T(8,128)S(1)} %get-tuple-element.19), channel_id=1, source_target_pairs={{0,15},{1,2},{2,1},{3,4},{4,3},{5,6},{6,5},{7,8},{8,7},{9,10},{10,... | collective-permute-start | bytes 49160 | tf_op jit(solution)/shard_map/ppermute | solution.py:286
  13.4 75.1 %copy-start.1 = (s32[1,256]{1,0:T(1,128)S(1)}, s32[1,256]{1,0:T(1,128)}, u32[]{:S(2)}) copy-start(s32[1,256]{1,0:T(1,128)} %row_ref.3) | copy-start | bytes 3076
  13.4 75.1 %copy-start.2 = (s32[1,256]{1,0:T(1,128)S(1)}, s32[1,256]{1,0:T(1,128)}, u32[]{:S(2)}) copy-start(s32[1,256]{1,0:T(1,128)} %col_ref.3) | copy-start | bytes 3076
  13.5 75.1 %copy-start.3 = (f32[1,256]{1,0:T(1,128)S(1)}, f32[1,256]{1,0:T(1,128)}, u32[]{:S(2)}) copy-start(f32[1,256]{1,0:T(1,128)} %value_ref.3) | copy-start | bytes 3076
  13.5 75.1 %copy-start.4 = (f32[1,256]{1,0:T(1,128)S(1)}, f32[1,256]{1,0:T(1,128)}, u32[]{:S(2)}) copy-start(f32[1,256]{1,0:T(1,128)} %prec_ref.3) | copy-start | bytes 3076
  13.5 77.5 %copy-start.5 = (s32[1,4]{1,0:T(1,128)S(1)}, s32[1,4]{1,0:T(1,128)}, u32[]{:S(2)}) copy-start(s32[1,4]{1,0:T(1,128)} %mask_ref.3) | copy-start | bytes 52
  89.1 7.7 %collective-permute-start.3 = (bf16[1040,128]{1,0:T(8,128)(2,1)S(1)}, bf16[1040,128]{1,0:T(8,128)(2,1)S(1)}, u32[]{:S(2)}, u32[]{:S(2)}) collective-permute-start(bf16[1040,128]{1,0:T(8,128)(2,1)S(1)} %get-tuple-element.30), channel_id=1, source_target_pairs={{0,15},{1,2},{2,1},{3,4},{4,3},{5,6},{6,5},{7,8},{8,7},{9,10},{10,... | collective-permute-start | bytes 798728 | tf_op jit(solution)/shard_map/ppermute | solution.py:304
  92.0 4.8 %collective-permute-start.2 = (bf16[1040,128]{1,0:T(8,128)(2,1)S(1)}, bf16[1040,128]{1,0:T(8,128)(2,1)S(1)}, u32[]{:S(2)}, u32[]{:S(2)}) collective-permute-start(bf16[1040,128]{1,0:T(8,128)(2,1)S(1)} %get-tuple-element.29), channel_id=1, source_target_pairs={{0,1},{1,0},{2,3},{3,2},{4,5},{5,4},{6,7},{7,6},{8,9},{9,8},{10,11... | collective-permute-start | bytes 798728 | tf_op jit(solution)/shard_map/ppermute | solution.py:322

commit v7 on v6

--- a/solution.py
+++ b/solution.py
@@ -139,21 +139,23 @@
     ref[members:, :] = last.astype(BF16)
 
 
-def observe_kernel(even_ref, local_ref, row_ref, col_ref, value_ref, prec_ref, y_ref, mean_ref, cross_ref):
+def observe_kernel(
+    even_ref, local_ref, row_ref, col_ref, value_ref, prec_ref, y_ref, mean_ref, pair_ref, cross_ref
+):
     members, cells = local_ref.shape
     half = cells // 2
     equivalent = local_ref[:, half:].astype(F32) + OBS_WIND * local_ref[:, :half].astype(F32)
     mean = jnp.sum(equivalent, axis=0, keepdims=True) * (1.0 / members)
     mean_ref[...] = jnp.broadcast_to(mean, mean_ref.shape)
     y_ref[...] = ((equivalent - mean) * (members - 1) ** (-0.5)).astype(BF16)
+    write_rows(even_ref[0, 0], y_ref, mean, row_ref, col_ref, value_ref, prec_ref, pair_ref)
     write_rows(1 - even_ref[0, 0], y_ref, mean, row_ref, col_ref, value_ref, prec_ref, cross_ref)
 
 
 def own_kernel(
-    even_ref, mask_ref, local_ref, y_ref, observed_ref, row_ref, col_ref, value_ref, prec_ref,
-    pair_ref, anomaly_ref, yt_ref, mean_ref, gram_ref, cover_ref, across_ref, down_ref,
+    mask_ref, local_ref, y_ref, observed_ref, row_ref, col_ref, value_ref, prec_ref,
+    anomaly_ref, yt_ref, mean_ref, gram_ref, cover_ref, across_ref, down_ref,
 ):
-    write_rows(even_ref[0, 0], y_ref, observed_ref[0:1, :], row_ref, col_ref, value_ref, prec_ref, pair_ref)
     members, cells = local_ref.shape
     half = cells // 2
     local = local_ref[...].astype(F32)
@@ -295,17 +297,17 @@
     local = lax.all_to_all(predicted, "member", split_axis=0, concat_axis=0, tiled=True).reshape(total, cells)
 
     rim = struct((total + 16, n // 2), BF16)
-    y, observed, cross_rows = call(
+    y, observed, pair_rows, cross_rows = call(
         observe_kernel,
-        [struct((total, cells // 2), BF16), struct((8, cells // 2), F32), rim],
+        [struct((total, cells // 2), BF16), struct((8, cells // 2), F32), rim, rim],
         [even, local, obs_row, obs_col, obs_value, obs_prec],
         specs=[SMEM] + [VMEM] * 5,
     )
+    pair_rows = lax.ppermute(pair_rows, "domain", pairs)
     cross_rows = lax.ppermute(cross_rows, "domain", crosses)
     own = call(
         own_kernel,
         [
-            rim,
             struct((total, cells), BF16),
             struct((cells // 2, total), BF16),
             struct((8, cells), F32),
@@ -314,12 +316,10 @@
             struct((8, cells // 2), F32),
             struct((cells // 2, 128), F32),
         ],
-        [even, loc_mask, local, y, observed, obs_row, obs_col, obs_value, obs_prec],
-        specs=[SMEM] + [VMEM] * 8,
+        [loc_mask, local, y, observed, obs_row, obs_col, obs_value, obs_prec],
         flops=2 * total * cells * cells * 3 // 4,
     )
-    pair_rows, anomalies, yt, mean, gram, cover, row, col = own
-    pair_rows = lax.ppermute(pair_rows, "domain", pairs)
+    anomalies, yt, mean, gram, cover, row, col = own
     analysis = call(
         analyse_kernel,
         struct((total, cells), BF16),

time: 164 us -> 164 us (level)
  waiting for transfers between devices: 2.87 us -> 4.84 us
    ppermute x1, waiting for transfers between devices: 2.86 us -> 4.83 us  [on_device(): cross_rows = lax.ppermute(cross_rows, 'domain', crosses)]
where the time goes in v7:
time: 164 us
  blocking collectives  136 us (83%)
  starting transfers between devices  13.3 us (8%)
  Pallas kernels  9.03 us (6%)
  waiting for transfers between devices  4.84 us (3%)
    all_to_all x1, blocking collectives, on_device(): lax.all_to_all(predicted, 'member', split_axis=0, concat_axis=0, tiled=True)  75 us
    all_to_all x1, blocking collectives, on_device(): lax.all_to_all(analysis.reshape(bands, members, cells), 'member', split_a...  60.5 us
    pallas_call x7, Pallas kernels, call(): pl.pallas_call(kernel, out_shape=shapes, in_specs=specs or [VMEM] * len(a...  9.03 us
    ppermute x1, starting transfers between devices, on_device(): cross_edge = lax.ppermute(cross_edge, 'domain', crosses)  7.49 us
    ppermute x1, waiting for transfers between devices, on_device(): cross_rows = lax.ppermute(cross_rows, 'domain', crosses)  4.83 us
  transfers between devices with their start and end apart: 4, of which 1 were waited for; matrix products, arithmetic and copies ran while one was open for 0% of the time, Pallas kernels for 1%

profile of v7, /device:TPU:32, one launch (start us, length us, event | category | flops | bytes accessed | tf_op | source)
XLA Modules:
  0.0 164.1 jit_solution(6118105580719215637)
XLA Ops:
  0.0 0.0 copy-start
  0.0 1.2 copy-done
  1.2 0.6 shard_map.65
  1.9 1.9 %collective-permute-start = (f32[8,512]{1,0:T(8,128)S(1)}, f32[8,512]{1,0:T(8,128)S(1)}, u32[]{:S(2)}, u32[]{:S(2)}) collective-permute-start(f32[8,512]{1,0:T(8,128)S(1)} %get-tuple-element.18), channel_id=1, source_target_pairs={{0,1},{1,0},{2,3},{3,2},{4,5},{5,4},{6,7},{7,6},{8,9},{9,8},{10,11... | collective-permute-start | bytes 49160 | tf_op jit(solution)/shard_map/ppermute | solution.py:287
  3.8 7.5 %collective-permute-start.1 = (f32[8,512]{1,0:T(8,128)S(1)}, f32[8,512]{1,0:T(8,128)S(1)}, u32[]{:S(2)}, u32[]{:S(2)}) collective-permute-start(f32[8,512]{1,0:T(8,128)S(1)} %get-tuple-element.19), channel_id=1, source_target_pairs={{0,15},{1,2},{2,1},{3,4},{4,3},{5,6},{6,5},{7,8},{8,7},{9,10},{10,... | collective-permute-start | bytes 49160 | tf_op jit(solution)/shard_map/ppermute | solution.py:288
  11.3 1.4 shard_map.64.new_ref
  12.7 0.0 collective-permute-done.pair_ref
  12.8 0.0 collective-permute-done.1.cross_ref
  12.8 0.7 shard_map.66
  13.4 0.0 copy-start.1
  13.4 0.0 copy-start.2
  13.5 0.0 copy-start.3
  13.5 0.0 copy-start.4
  13.5 0.0 copy-start.5
  13.5 75.0 %all_to_all.10 = bf16[32,32,512]{2,1,0:T(8,128)(2,1)S(1)} all-to-all(bf16[32,32,512]{2,1,0:T(8,128)(2,1)S(1)} %shard_map.66), channel_id=1, replica_groups=mesh['member'=32,'domain'=16] {'member'}, dimensions={0} | all-to-all | bytes 2097152 | tf_op jit(solution)/shard_map/all_to_all | solution.py:297
  88.5 0.0 copy-done.1
  88.6 0.0 copy-done.2
  88.6 0.0 copy-done.3
  88.6 0.0 copy-done.4
  88.6 0.7 shard_map.67
  89.2 1.9 %collective-permute-start.2 = (bf16[1040,128]{1,0:T(8,128)(2,1)S(1)}, bf16[1040,128]{1,0:T(8,128)(2,1)S(1)}, u32[]{:S(2)}, u32[]{:S(2)}) collective-permute-start(bf16[1040,128]{1,0:T(8,128)(2,1)S(1)} %get-tuple-element.29), channel_id=1, source_target_pairs={{0,1},{1,0},{2,3},{3,2},{4,5},{5,4},{6,7},{7,6},{8,9},{9,8},{10,11... | collective-permute-start | bytes 798728 | tf_op jit(solution)/shard_map/ppermute | solution.py:306
  91.2 1.9 %collective-permute-start.3 = (bf16[1040,128]{1,0:T(8,128)(2,1)S(1)}, bf16[1040,128]{1,0:T(8,128)(2,1)S(1)}, u32[]{:S(2)}, u32[]{:S(2)}) collective-permute-start(bf16[1040,128]{1,0:T(8,128)(2,1)S(1)} %get-tuple-element.30), channel_id=1, source_target_pairs={{0,15},{1,2},{2,1},{3,4},{4,3},{5,6},{6,5},{7,8},{8,7},{9,10},{10,... | collective-permute-start | bytes 798728 | tf_op jit(solution)/shard_map/ppermute | solution.py:307
  93.1 0.0 copy-done.5
  93.1 1.0 shard_map.68
  94.1 0.0 collective-permute-done.2.pair_ref
  94.1 4.8 %collective-permute-done.3.cross_ref = bf16[1040,128]{1,0:T(8,128)(2,1)S(1)} collective-permute-done((bf16[1040,128]{1,0:T(8,128)(2,1)S(1)}, bf16[1040,128]{1,0:T(8,128)(2,1)S(1)}, u32[]{:S(2)}, u32[]{:S(2)}) %collective-permute-start.3) | collective-permute-done | bytes 266272 | tf_op jit(solution)/shard_map/ppermute | solution.py:307
  98.9 3.6 %shard_map.69 = bf16[1024,512]{1,0:T(8,128)(2,1)S(1)} custom-call(s32[1,1]{1,0:T(1,128)} %bitcast.even_ref, s32[1,4]{1,0:T(1,128)S(1)} %copy-done.5, bf16[1024,512]{1,0:T(8,128)(2,1)S(1)} %get-tuple-element.22.anomaly_ref, bf16[1024,256]{1,0:T(8,128)(2,1)S(1)} %get-tuple-element.20.y_ref, bf16[256,1024]{1,0:T(8,128)(2,1)S(1)} %get-tuple-element.23.yt_ref, ...), custom_call_target="tpu_custom_call" | custom-call | flops 2147483648 | bytes 3571732 | tf_op jit(solution)/shard_map/pallas_call | solution.py:22
  102.5 60.5 %all_to_all.11.in_ref = bf16[32,32,512]{2,1,0:T(8,128)(2,1)S(1)} all-to-all(bf16[32,32,512]{2,1,0:T(8,128)(2,1)S(1)} %bitcast.5), channel_id=1, replica_groups=mesh['member'=32,'domain'=16] {'member'}, dimensions={0} | all-to-all | bytes 2097152 | tf_op jit(solution)/shard_map/all_to_all | solution.py:337
  163.0 1.1 shard_map.70
Async XLA Ops:
  0.0 1.2 copy-start
  1.9 10.9 %collective-permute-start = (f32[8,512]{1,0:T(8,128)S(1)}, f32[8,512]{1,0:T(8,128)S(1)}, u32[]{:S(2)}, u32[]{:S(2)}) collective-permute-start(f32[8,512]{1,0:T(8,128)S(1)} %get-tuple-element.18), channel_id=1, source_target_pairs={{0,1},{1,0},{2,3},{3,2},{4,5},{5,4},{6,7},{7,6},{8,9},{9,8},{10,11... | collective-permute-start | bytes 49160 | tf_op jit(solution)/shard_map/ppermute | solution.py:287
  3.8 8.9 %collective-permute-start.1 = (f32[8,512]{1,0:T(8,128)S(1)}, f32[8,512]{1,0:T(8,128)S(1)}, u32[]{:S(2)}, u32[]{:S(2)}) collective-permute-start(f32[8,512]{1,0:T(8,128)S(1)} %get-tuple-element.19), channel_id=1, source_target_pairs={{0,15},{1,2},{2,1},{3,4},{4,3},{5,6},{6,5},{7,8},{8,7},{9,10},{10,... | collective-permute-start | bytes 49160 | tf_op jit(solution)/shard_map/ppermute | solution.py:288
  13.4 75.1 %copy-start.1 = (s32[1,256]{1,0:T(1,128)S(1)}, s32[1,256]{1,0:T(1,128)}, u32[]{:S(2)}) copy-start(s32[1,256]{1,0:T(1,128)} %row_ref.3) | copy-start | bytes 3076
  13.4 75.1 %copy-start.2 = (s32[1,256]{1,0:T(1,128)S(1)}, s32[1,256]{1,0:T(1,128)}, u32[]{:S(2)}) copy-start(s32[1,256]{1,0:T(1,128)} %col_ref.3) | copy-start | bytes 3076
  13.5 75.1 %copy-start.3 = (f32[1,256]{1,0:T(1,128)S(1)}, f32[1,256]{1,0:T(1,128)}, u32[]{:S(2)}) copy-start(f32[1,256]{1,0:T(1,128)} %value_ref.3) | copy-start | bytes 3076
  13.5 75.1 %copy-start.4 = (f32[1,256]{1,0:T(1,128)S(1)}, f32[1,256]{1,0:T(1,128)}, u32[]{:S(2)}) copy-start(f32[1,256]{1,0:T(1,128)} %prec_ref.3) | copy-start | bytes 3076
  13.5 79.6 %copy-start.5 = (s32[1,4]{1,0:T(1,128)S(1)}, s32[1,4]{1,0:T(1,128)}, u32[]{:S(2)}) copy-start(s32[1,4]{1,0:T(1,128)} %mask_ref.3) | copy-start | bytes 52
  89.2 4.8 %collective-permute-start.2 = (bf16[1040,128]{1,0:T(8,128)(2,1)S(1)}, bf16[1040,128]{1,0:T(8,128)(2,1)S(1)}, u32[]{:S(2)}, u32[]{:S(2)}) collective-permute-start(bf16[1040,128]{1,0:T(8,128)(2,1)S(1)} %get-tuple-element.29), channel_id=1, source_target_pairs={{0,1},{1,0},{2,3},{3,2},{4,5},{5,4},{6,7},{7,6},{8,9},{9,8},{10,11... | collective-permute-start | bytes 798728 | tf_op jit(solution)/shard_map/ppermute | solution.py:306
  91.2 7.7 %collective-permute-start.3 = (bf16[1040,128]{1,0:T(8,128)(2,1)S(1)}, bf16[1040,128]{1,0:T(8,128)(2,1)S(1)}, u32[]{:S(2)}, u32[]{:S(2)}) collective-permute-start(bf16[1040,128]{1,0:T(8,128)(2,1)S(1)} %get-tuple-element.30), channel_id=1, source_target_pairs={{0,15},{1,2},{2,1},{3,4},{4,3},{5,6},{6,5},{7,8},{8,7},{9,10},{10,... | collective-permute-start | bytes 798728 | tf_op jit(solution)/shard_map/ppermute | solution.py:307

commit v8 on v6

--- a/solution.py
+++ b/solution.py
@@ -14,10 +14,9 @@
 VMEM = pl.BlockSpec(memory_space=pltpu.VMEM)
 SMEM = pl.BlockSpec(memory_space=pltpu.SMEM)
 HBM = pl.BlockSpec(memory_space=pltpu.HBM)
-PARAMS = pltpu.CompilerParams(vmem_limit_bytes=40 * 1024 * 1024)
-
-
-def call(kernel, shapes, args, scratch=(), specs=None, flops=0, out=VMEM):
+
+
+def call(kernel, shapes, args, scratch=(), specs=None, flops=0, out=VMEM, limit=40):
     nbytes = sum(a.size * a.dtype.itemsize for a in args)
     return pl.pallas_call(
         kernel,
@@ -25,7 +24,7 @@
         in_specs=specs or [VMEM] * len(args),
         out_specs=jax.tree.map(lambda _: out, shapes),
         scratch_shapes=list(scratch),
-        compiler_params=PARAMS,
+        compiler_params=pltpu.CompilerParams(vmem_limit_bytes=limit * 1024 * 1024),
         cost_estimate=pl.CostEstimate(flops=flops, bytes_accessed=nbytes, transcendentals=0),
     )(*args)
 
@@ -44,19 +43,26 @@
     return jnp.sum(jnp.where(iota((n, n), 0) == iota((n, n), 1), col, 0.0), axis=0, keepdims=True)
 
 
-def write_edges(ens_ref, tail, edge_ref):
+def write_edges(ens_ref, tail, edge_ref, k):
     rows, cols = ens_ref.shape[2:]
     pick = (iota((8, cols), 1) == jnp.where(tail, cols - 1, 0)).astype(F32).astype(BF16)
     members = ens_ref.shape[0] // 8
+    lines = ens_ref[k * members : (k + 1) * members].reshape(-1, cols)
+    edges = lax.dot_general(pick, lines, (((1,), (1,)), ((), ())), preferred_element_type=F32)
+    edge_ref[k : k + 1, :] = edges[0:1]
+
+
+def edge_kernel(even_ref, ens_ref, pair_ref, cross_ref, here, sems):
+    n = here.shape[0] // 8
+    copies = [
+        pltpu.make_async_copy(ens_ref.at[pl.ds(k * n, n)], here.at[pl.ds(k * n, n)], sems.at[k]) for k in range(8)
+    ]
+    for copy in copies:
+        copy.start()
     for k in range(8):
-        lines = ens_ref[k * members : (k + 1) * members].reshape(-1, cols)
-        edges = lax.dot_general(pick, lines, (((1,), (1,)), ((), ())), preferred_element_type=F32)
-        edge_ref[k : k + 1, :] = edges[0:1]
-
-
-def edge_kernel(even_ref, ens_ref, pair_ref, cross_ref):
-    write_edges(ens_ref, even_ref[0, 0] == 0, cross_ref)
-    write_edges(ens_ref, even_ref[0, 0] == 1, pair_ref)
+        copies[k].wait()
+        write_edges(here, even_ref[0, 0] == 0, cross_ref, k)
+        write_edges(here, even_ref[0, 0] == 1, pair_ref, k)
 
 
 def inside_kernel(ens_ref, new_ref):
@@ -281,7 +287,14 @@
     even = (1 - lax.axis_index("domain") % 2).astype(jnp.int32).reshape(1, 1)
 
     edge = struct((8, members // 8 * fields * rows), F32)
-    pair_edge, cross_edge = call(edge_kernel, [edge, edge], [even, ensemble], specs=[SMEM, VMEM])
+    pair_edge, cross_edge = call(
+        edge_kernel,
+        [edge, edge],
+        [even, ensemble],
+        scratch=[pltpu.VMEM(ensemble.shape, BF16), pltpu.SemaphoreType.DMA((8,))],
+        specs=[SMEM, HBM],
+        limit=60,
+    )
     pair_edge = lax.ppermute(pair_edge, "domain", pairs)
     cross_edge = lax.ppermute(cross_edge, "domain", crosses)
     inside = call(inside_kernel, struct((fields, members * rows, cols), F32), [ensemble], flops=10**9)

time: 164 us -> 166 us (1.012)
  Pallas kernels: 8.9 us -> 11.3 us
    pallas_call x7, Pallas kernels: 8.9 us -> 11.3 us  [call(): pl.pallas_call(kernel, out_shape=shapes, in_specs=specs or [VMEM] * len(a...]
where the time goes in v8:
time: 166 us; the launch traced here: 165 us
  blocking collectives  136 us (82%)
  starting transfers between devices  13.3 us (8%)
  Pallas kernels  11.3 us (7%)
  waiting for transfers between devices  2.91 us (2%)
    all_to_all x1, blocking collectives, on_device(): lax.all_to_all(predicted, 'member', split_axis=0, concat_axis=0, tiled=True)  74 us
    all_to_all x1, blocking collectives, on_device(): lax.all_to_all(analysis.reshape(bands, members, cells), 'member', split_a...  62.3 us
    pallas_call x7, Pallas kernels, call(): pl.pallas_call(kernel, out_shape=shapes, in_specs=specs or [VMEM] * len(a...  11.3 us
    ppermute x1, starting transfers between devices, on_device(): cross_edge = lax.ppermute(cross_edge, 'domain', crosses)  7.49 us
  transfers between devices with their start and end apart: 4, of which 1 were waited for; matrix products, arithmetic and copies ran while one was open for 0% of the time, Pallas kernels for 1%

profile of v8, /device:TPU:32, one launch (start us, length us, event | category | flops | bytes accessed | tf_op | source)
XLA Modules:
  0.0 165.2 jit_solution(10944554787154214728)
XLA Ops:
  0.0 3.1 %shard_map.65 = (f32[8,512]{1,0:T(8,128)}, f32[8,512]{1,0:T(8,128)}) custom-call(s32[1,1]{1,0:T(1,128)} %bitcast.even_ref, bf16[32,2,64,128]{3,2,1,0:T(8,128)(2,1)} %ens_ref.5), custom_call_target="tpu_custom_call" | custom-call | bytes 1048580 | tf_op jit(solution)/shard_map/pallas_call | solution.py:21
  3.1 1.9 %collective-permute-start = (f32[8,512]{1,0:T(8,128)}, f32[8,512]{1,0:T(8,128)S(1)}, u32[]{:S(2)}, u32[]{:S(2)}) collective-permute-start(f32[8,512]{1,0:T(8,128)} %get-tuple-element.18), channel_id=1, source_target_pairs={{0,1},{1,0},{2,3},{3,2},{4,5},{5,4},{6,7},{7,6},{8,9},{9,8},{10,11... | collective-permute-start | bytes 49160 | tf_op jit(solution)/shard_map/ppermute | solution.py:298
  5.0 7.5 %collective-permute-start.1 = (f32[8,512]{1,0:T(8,128)}, f32[8,512]{1,0:T(8,128)S(1)}, u32[]{:S(2)}, u32[]{:S(2)}) collective-permute-start(f32[8,512]{1,0:T(8,128)} %get-tuple-element.19), channel_id=1, source_target_pairs={{0,15},{1,2},{2,1},{3,4},{4,3},{5,6},{6,5},{7,8},{8,7},{9,10},{10,... | collective-permute-start | bytes 49160 | tf_op jit(solution)/shard_map/ppermute | solution.py:299
  12.5 0.0 copy-start
  12.5 1.2 copy-done
  13.8 1.4 shard_map.64.new_ref
  15.2 0.0 collective-permute-done.pair_ref
  15.2 0.0 collective-permute-done.1.cross_ref
  15.2 0.7 shard_map.66
  15.9 0.0 copy-start.1
  15.9 0.0 copy-start.2
  15.9 0.0 copy-start.3
  15.9 0.0 copy-start.4
  15.9 0.0 copy-start.5
  15.9 74.0 %all_to_all.10 = bf16[32,32,512]{2,1,0:T(8,128)(2,1)S(1)} all-to-all(bf16[32,32,512]{2,1,0:T(8,128)(2,1)S(1)} %shard_map.66), channel_id=1, replica_groups=mesh['member'=32,'domain'=16] {'member'}, dimensions={0} | all-to-all | bytes 2097152 | tf_op jit(solution)/shard_map/all_to_all | solution.py:308
  89.9 0.0 copy-done.1
  89.9 0.0 copy-done.2
  89.9 0.0 copy-done.3
  89.9 0.0 copy-done.4
  89.9 0.5 shard_map.67
  90.4 1.9 %collective-permute-start.3 = (bf16[1040,128]{1,0:T(8,128)(2,1)S(1)}, bf16[1040,128]{1,0:T(8,128)(2,1)S(1)}, u32[]{:S(2)}, u32[]{:S(2)}) collective-permute-start(bf16[1040,128]{1,0:T(8,128)(2,1)S(1)} %get-tuple-element.30), channel_id=1, source_target_pairs={{0,15},{1,2},{2,1},{3,4},{4,3},{5,6},{6,5},{7,8},{8,7},{9,10},{10,... | collective-permute-start | bytes 798728 | tf_op jit(solution)/shard_map/ppermute | solution.py:317
  92.4 0.0 copy-done.5
  92.4 1.0 shard_map.68
  93.4 1.9 %collective-permute-start.2 = (bf16[1040,128]{1,0:T(8,128)(2,1)S(1)}, bf16[1040,128]{1,0:T(8,128)(2,1)S(1)}, u32[]{:S(2)}, u32[]{:S(2)}) collective-permute-start(bf16[1040,128]{1,0:T(8,128)(2,1)S(1)} %get-tuple-element.29), channel_id=1, source_target_pairs={{0,1},{1,0},{2,3},{3,2},{4,5},{5,4},{6,7},{7,6},{8,9},{9,8},{10,11... | collective-permute-start | bytes 798728 | tf_op jit(solution)/shard_map/ppermute | solution.py:335
  95.3 2.9 %collective-permute-done.3.cross_ref = bf16[1040,128]{1,0:T(8,128)(2,1)S(1)} collective-permute-done((bf16[1040,128]{1,0:T(8,128)(2,1)S(1)}, bf16[1040,128]{1,0:T(8,128)(2,1)S(1)}, u32[]{:S(2)}, u32[]{:S(2)}) %collective-permute-start.3) | collective-permute-done | bytes 266272 | tf_op jit(solution)/shard_map/ppermute | solution.py:317
  98.2 0.0 collective-permute-done.2.pair_ref
  98.2 3.6 %shard_map.69 = bf16[1024,512]{1,0:T(8,128)(2,1)S(1)} custom-call(s32[1,1]{1,0:T(1,128)} %bitcast.even_ref, s32[1,4]{1,0:T(1,128)S(1)} %copy-done.5, bf16[1024,512]{1,0:T(8,128)(2,1)S(1)} %get-tuple-element.22.anomaly_ref, bf16[1024,256]{1,0:T(8,128)(2,1)S(1)} %get-tuple-element.20.y_ref, bf16[256,1024]{1,0:T(8,128)(2,1)S(1)} %get-tuple-element.23.yt_ref, ...), custom_call_target="tpu_custom_call" | custom-call | flops 2147483648 | bytes 3571732 | tf_op jit(solution)/shard_map/pallas_call | solution.py:21
  101.8 62.3 %all_to_all.11.in_ref = bf16[32,32,512]{2,1,0:T(8,128)(2,1)S(1)} all-to-all(bf16[32,32,512]{2,1,0:T(8,128)(2,1)S(1)} %bitcast.5), channel_id=1, replica_groups=mesh['member'=32,'domain'=16] {'member'}, dimensions={0} | all-to-all | bytes 2097152 | tf_op jit(solution)/shard_map/all_to_all | solution.py:350
  164.1 1.1 shard_map.70
Async XLA Ops:
  3.1 12.1 %collective-permute-start = (f32[8,512]{1,0:T(8,128)}, f32[8,512]{1,0:T(8,128)S(1)}, u32[]{:S(2)}, u32[]{:S(2)}) collective-permute-start(f32[8,512]{1,0:T(8,128)} %get-tuple-element.18), channel_id=1, source_target_pairs={{0,1},{1,0},{2,3},{3,2},{4,5},{5,4},{6,7},{7,6},{8,9},{9,8},{10,11... | collective-permute-start | bytes 49160 | tf_op jit(solution)/shard_map/ppermute | solution.py:298
  5.0 10.2 %collective-permute-start.1 = (f32[8,512]{1,0:T(8,128)}, f32[8,512]{1,0:T(8,128)S(1)}, u32[]{:S(2)}, u32[]{:S(2)}) collective-permute-start(f32[8,512]{1,0:T(8,128)} %get-tuple-element.19), channel_id=1, source_target_pairs={{0,15},{1,2},{2,1},{3,4},{4,3},{5,6},{6,5},{7,8},{8,7},{9,10},{10,... | collective-permute-start | bytes 49160 | tf_op jit(solution)/shard_map/ppermute | solution.py:299
  12.5 1.2 copy-start
  15.9 74.0 %copy-start.1 = (s32[1,256]{1,0:T(1,128)S(1)}, s32[1,256]{1,0:T(1,128)}, u32[]{:S(2)}) copy-start(s32[1,256]{1,0:T(1,128)} %row_ref.3) | copy-start | bytes 3076
  15.9 74.0 %copy-start.2 = (s32[1,256]{1,0:T(1,128)S(1)}, s32[1,256]{1,0:T(1,128)}, u32[]{:S(2)}) copy-start(s32[1,256]{1,0:T(1,128)} %col_ref.3) | copy-start | bytes 3076
  15.9 74.0 %copy-start.3 = (f32[1,256]{1,0:T(1,128)S(1)}, f32[1,256]{1,0:T(1,128)}, u32[]{:S(2)}) copy-start(f32[1,256]{1,0:T(1,128)} %value_ref.3) | copy-start | bytes 3076
  15.9 74.0 %copy-start.4 = (f32[1,256]{1,0:T(1,128)S(1)}, f32[1,256]{1,0:T(1,128)}, u32[]{:S(2)}) copy-start(f32[1,256]{1,0:T(1,128)} %prec_ref.3) | copy-start | bytes 3076
  15.9 76.4 %copy-start.5 = (s32[1,4]{1,0:T(1,128)S(1)}, s32[1,4]{1,0:T(1,128)}, u32[]{:S(2)}) copy-start(s32[1,4]{1,0:T(1,128)} %mask_ref.3) | copy-start | bytes 52
  90.4 7.8 %collective-permute-start.3 = (bf16[1040,128]{1,0:T(8,128)(2,1)S(1)}, bf16[1040,128]{1,0:T(8,128)(2,1)S(1)}, u32[]{:S(2)}, u32[]{:S(2)}) collective-permute-start(bf16[1040,128]{1,0:T(8,128)(2,1)S(1)} %get-tuple-element.30), channel_id=1, source_target_pairs={{0,15},{1,2},{2,1},{3,4},{4,3},{5,6},{6,5},{7,8},{8,7},{9,10},{10,... | collective-permute-start | bytes 798728 | tf_op jit(solution)/shard_map/ppermute | solution.py:317
  93.4 4.8 %collective-permute-start.2 = (bf16[1040,128]{1,0:T(8,128)(2,1)S(1)}, bf16[1040,128]{1,0:T(8,128)(2,1)S(1)}, u32[]{:S(2)}, u32[]{:S(2)}) collective-permute-start(bf16[1040,128]{1,0:T(8,128)(2,1)S(1)} %get-tuple-element.29), channel_id=1, source_target_pairs={{0,1},{1,0},{2,3},{3,2},{4,5},{5,4},{6,7},{7,6},{8,9},{9,8},{10,11... | collective-permute-start | bytes 798728 | tf_op jit(solution)/shard_map/ppermute | solution.py:335

commit v9 on v5

--- a/solution.py
+++ b/solution.py
@@ -108,14 +108,14 @@
             out_ref[r // 2, :, at : at + cols] = part.astype(BF16)
 
 
-def restore_kernel(in_ref, out_ref, store, done, sems):
+def restore_kernel(wind_ref, tracer_ref, out_ref, store, done, sems):
     members, _, rows, cols = done.shape
     pitch = store.shape[1] // members
     half = members // 2
     copies = []
-    for f in range(2):
+    for f, in_ref in enumerate((wind_ref, tracer_ref)):
         for r in range(rows):
-            at = (f * 2 + r % 2) * cols
+            at = r % 2 * cols
             store[f, pl.ds(r, members, stride=pitch), :] = in_ref[r // 2, :, at : at + cols].astype(F32)
         for p in range(2):
             for m in range(p * half, (p + 1) * half):
@@ -180,7 +180,7 @@
 
 def analyse_kernel(
     even_ref, mask_ref, anomaly_ref, y_ref, yt_ref, mean_ref, gram_ref, cover_ref, row_ref, col_ref,
-    pair_ref, cross_ref, out_ref, z, zt, gram, cover, u,
+    pair_ref, cross_ref, wind_ref, tracer_ref, z, zt, gram, cover, u,
 ):
     members, cells = anomaly_ref.shape
     half = cells // 2
@@ -261,11 +261,13 @@
     keep = 0.5 * (1.0 + to_one)
     for i in range(members // step):
         at = pl.ds(i * step, step)
-        out_ref[at, :] = (
+        new = (
             shift
             + keep * anomaly_ref[at, :].astype(F32)
             + jnp.dot(z[at, :], gain, preferred_element_type=F32)
         ).astype(BF16)
+        wind_ref[at, :] = new[:, :half]
+        tracer_ref[at, :] = new[:, half:]
 
 
 def on_device(ensemble, obs_value, obs_prec, obs_row, obs_col, loc_mask):
@@ -328,7 +330,7 @@
     pair_rows = lax.ppermute(pair_rows, "domain", pairs)
     analysis = call(
         analyse_kernel,
-        struct((total, cells), BF16),
+        [struct((total, cells // 2), BF16)] * 2,
         [even, loc_mask, anomalies, y, yt, mean, gram, cover, row, col, pair_rows, cross_rows],
         scratch=[
             pltpu.VMEM((total, cells), BF16),
@@ -340,13 +342,16 @@
         specs=[SMEM] + [VMEM] * 11,
         flops=2 * total * total * cells * 2,
     )
-    back = lax.all_to_all(
-        analysis.reshape(bands, members, cells), "member", split_axis=0, concat_axis=0, tiled=True
-    )
+    back = [
+        lax.all_to_all(
+            field.reshape(bands, members, cells // 2), "member", split_axis=0, concat_axis=0, tiled=True
+        )
+        for field in analysis
+    ]
     return call(
         restore_kernel,
         struct(ensemble.shape, BF16),
-        [back],
+        back,
         scratch=[
             pltpu.VMEM((fields, members * (rows + SKEW), cols), F32),
             pltpu.VMEM(ensemble.shape, BF16),

time: 163 us -> 169 us (1.037)
  blocking collectives: 139 us -> 145 us
    all_to_all x1 -> x2, blocking collectives: 61.5 us -> 67.1 us  [on_device(): lax.all_to_all(field.reshape(bands, members, cells // 2), 'member', split...]
  transfers between devices with their start and end apart: 4 -> 4, of which waited for: 2 -> 2; matrix products, arithmetic and copies ran while one was open for 0% -> 0% of each run, Pallas kernels for 2% -> 1%
where the time goes in v9:
time: 169 us
  blocking collectives  145 us (86%)
  starting transfers between devices  9.7 us (6%)
  Pallas kernels  8.7 us (5%)
  waiting for transfers between devices  3.67 us (2%)
    all_to_all x1, blocking collectives, on_device(): lax.all_to_all(predicted, 'member', split_axis=0, concat_axis=0, tiled=True)  78 us
    all_to_all x2, blocking collectives, on_device(): lax.all_to_all(field.reshape(bands, members, cells // 2), 'member', split...  67.1 us
    pallas_call x7, Pallas kernels, call(): pl.pallas_call(kernel, out_shape=shapes, in_specs=specs or [VMEM] * len(a...  8.7 us
    ppermute x1, starting transfers between devices, on_device(): pair_edge = lax.ppermute(pair_edge, 'domain', pairs)  3.93 us
  transfers between devices with their start and end apart: 4, of which 2 were waited for; matrix products, arithmetic and copies ran while one was open for 0% of the time, Pallas kernels for 1%

profile of v9, /device:TPU:32, one launch (start us, length us, event | category | flops | bytes accessed | tf_op | source)
XLA Modules:
  0.0 168.5 jit_solution(17656576281971063806)
XLA Ops:
  0.0 0.0 copy-start
  0.0 1.2 copy-done
  1.2 0.4 shard_map.65
  1.6 1.9 %collective-permute-start.1 = (f32[8,512]{1,0:T(8,128)S(1)}, f32[8,512]{1,0:T(8,128)S(1)}, u32[]{:S(2)}, u32[]{:S(2)}) collective-permute-start(f32[8,512]{1,0:T(8,128)S(1)} %shard_map.65), channel_id=1, source_target_pairs={{0,15},{1,2},{2,1},{3,4},{4,3},{5,6},{6,5},{7,8},{8,7},{9,10},{10,... | collective-permute-start | bytes 49160 | tf_op jit(solution)/shard_map/ppermute | solution.py:287
  3.5 1.5 shard_map.64
  5.0 3.9 %collective-permute-start = (f32[8,512]{1,0:T(8,128)S(1)}, f32[8,512]{1,0:T(8,128)S(1)}, u32[]{:S(2)}, u32[]{:S(2)}) collective-permute-start(f32[8,512]{1,0:T(8,128)S(1)} %get-tuple-element.21), channel_id=1, source_target_pairs={{0,1},{1,0},{2,3},{3,2},{4,5},{5,4},{6,7},{7,6},{8,9},{9,8},{10,11... | collective-permute-start | bytes 49160 | tf_op jit(solution)/shard_map/ppermute | solution.py:295
  8.9 0.0 collective-permute-done.1.cross_ref
  8.9 0.8 collective-permute-done.pair_ref
  9.8 0.7 shard_map.66
  10.4 0.0 copy-start.1
  10.4 0.0 copy-start.2
  10.5 0.0 copy-start.3
  10.5 0.0 copy-start.4
  10.5 0.0 copy-start.5
  10.5 78.0 %all_to_all.15 = bf16[32,32,512]{2,1,0:T(8,128)(2,1)S(1)} all-to-all(bf16[32,32,512]{2,1,0:T(8,128)(2,1)S(1)} %shard_map.66), channel_id=1, replica_groups=mesh['member'=32,'domain'=16] {'member'}, dimensions={0} | all-to-all | bytes 2097152 | tf_op jit(solution)/shard_map/all_to_all | solution.py:303
  88.4 0.0 copy-done.1
  88.4 0.0 copy-done.2
  88.4 0.0 copy-done.3
  88.5 0.0 copy-done.4
  88.5 0.5 shard_map.67
  89.0 1.9 %collective-permute-start.3 = (bf16[1040,128]{1,0:T(8,128)(2,1)S(1)}, bf16[1040,128]{1,0:T(8,128)(2,1)S(1)}, u32[]{:S(2)}, u32[]{:S(2)}) collective-permute-start(bf16[1040,128]{1,0:T(8,128)(2,1)S(1)} %get-tuple-element.32), channel_id=1, source_target_pairs={{0,15},{1,2},{2,1},{3,4},{4,3},{5,6},{6,5},{7,8},{8,7},{9,10},{10,... | collective-permute-start | bytes 798728 | tf_op jit(solution)/shard_map/ppermute | solution.py:312
  90.9 0.0 copy-done.5
  90.9 1.0 shard_map.68
  91.9 1.9 %collective-permute-start.2 = (bf16[1040,128]{1,0:T(8,128)(2,1)S(1)}, bf16[1040,128]{1,0:T(8,128)(2,1)S(1)}, u32[]{:S(2)}, u32[]{:S(2)}) collective-permute-start(bf16[1040,128]{1,0:T(8,128)(2,1)S(1)} %get-tuple-element.31), channel_id=1, source_target_pairs={{0,1},{1,0},{2,3},{3,2},{4,5},{5,4},{6,7},{7,6},{8,9},{9,8},{10,11... | collective-permute-start | bytes 798728 | tf_op jit(solution)/shard_map/ppermute | solution.py:330
  93.8 2.9 %collective-permute-done.3.cross_ref = bf16[1040,128]{1,0:T(8,128)(2,1)S(1)} collective-permute-done((bf16[1040,128]{1,0:T(8,128)(2,1)S(1)}, bf16[1040,128]{1,0:T(8,128)(2,1)S(1)}, u32[]{:S(2)}, u32[]{:S(2)}) %collective-permute-start.3) | collective-permute-done | bytes 266272 | tf_op jit(solution)/shard_map/ppermute | solution.py:312
  96.7 0.0 collective-permute-done.2.pair_ref
  96.7 3.6 %shard_map.69 = (bf16[1024,256]{1,0:T(8,128)(2,1)S(1)}, bf16[1024,256]{1,0:T(8,128)(2,1)S(1)}) custom-call(s32[1,1]{1,0:T(1,128)} %bitcast.even_ref, s32[1,4]{1,0:T(1,128)S(1)} %copy-done.5, bf16[1024,512]{1,0:T(8,128)(2,1)S(1)} %get-tuple-element.24.anomaly_ref, bf16[1024,256]{1,0:T(8,128)(2,1)S(1)} %get-tuple-element.22.y_ref, ...), custom_call_target="tpu_custom_call" | custom-call | flops 2147483648 | bytes 3571732 | tf_op jit(solution)/shard_map/pallas_call | solution.py:22
  100.3 39.8 %all_to_all.16.tracer_ref = bf16[32,32,256]{2,1,0:T(8,128)(2,1)S(1)} all-to-all(bf16[32,32,256]{2,1,0:T(8,128)(2,1)S(1)} %bitcast.7), channel_id=1, replica_groups=mesh['member'=32,'domain'=16] {'member'}, dimensions={0} | all-to-all | bytes 1048576 | tf_op jit(solution)/shard_map/all_to_all | solution.py:346
  140.1 27.3 %all_to_all.17.wind_ref = bf16[32,32,256]{2,1,0:T(8,128)(2,1)S(1)} all-to-all(bf16[32,32,256]{2,1,0:T(8,128)(2,1)S(1)} %bitcast.6), channel_id=1, replica_groups=mesh['member'=32,'domain'=16] {'member'}, dimensions={0} | all-to-all | bytes 1048576 | tf_op jit(solution)/shard_map/all_to_all | solution.py:346
  167.4 1.1 shard_map.70
Async XLA Ops:
  0.0 1.2 copy-start
  1.6 7.3 %collective-permute-start.1 = (f32[8,512]{1,0:T(8,128)S(1)}, f32[8,512]{1,0:T(8,128)S(1)}, u32[]{:S(2)}, u32[]{:S(2)}) collective-permute-start(f32[8,512]{1,0:T(8,128)S(1)} %shard_map.65), channel_id=1, source_target_pairs={{0,15},{1,2},{2,1},{3,4},{4,3},{5,6},{6,5},{7,8},{8,7},{9,10},{10,... | collective-permute-start | bytes 49160 | tf_op jit(solution)/shard_map/ppermute | solution.py:287
  5.0 4.8 %collective-permute-start = (f32[8,512]{1,0:T(8,128)S(1)}, f32[8,512]{1,0:T(8,128)S(1)}, u32[]{:S(2)}, u32[]{:S(2)}) collective-permute-start(f32[8,512]{1,0:T(8,128)S(1)} %get-tuple-element.21), channel_id=1, source_target_pairs={{0,1},{1,0},{2,3},{3,2},{4,5},{5,4},{6,7},{7,6},{8,9},{9,8},{10,11... | collective-permute-start | bytes 49160 | tf_op jit(solution)/shard_map/ppermute | solution.py:295
  10.4 78.0 %copy-start.1 = (s32[1,256]{1,0:T(1,128)S(1)}, s32[1,256]{1,0:T(1,128)}, u32[]{:S(2)}) copy-start(s32[1,256]{1,0:T(1,128)} %row_ref.3) | copy-start | bytes 3076
  10.4 78.0 %copy-start.2 = (s32[1,256]{1,0:T(1,128)S(1)}, s32[1,256]{1,0:T(1,128)}, u32[]{:S(2)}) copy-start(s32[1,256]{1,0:T(1,128)} %col_ref.3) | copy-start | bytes 3076
  10.5 78.0 %copy-start.3 = (f32[1,256]{1,0:T(1,128)S(1)}, f32[1,256]{1,0:T(1,128)}, u32[]{:S(2)}) copy-start(f32[1,256]{1,0:T(1,128)} %value_ref.3) | copy-start | bytes 3076
  10.5 78.0 %copy-start.4 = (f32[1,256]{1,0:T(1,128)S(1)}, f32[1,256]{1,0:T(1,128)}, u32[]{:S(2)}) copy-start(f32[1,256]{1,0:T(1,128)} %prec_ref.3) | copy-start | bytes 3076
  10.5 80.4 %copy-start.5 = (s32[1,4]{1,0:T(1,128)S(1)}, s32[1,4]{1,0:T(1,128)}, u32[]{:S(2)}) copy-start(s32[1,4]{1,0:T(1,128)} %mask_ref.3) | copy-start | bytes 52
  89.0 7.7 %collective-permute-start.3 = (bf16[1040,128]{1,0:T(8,128)(2,1)S(1)}, bf16[1040,128]{1,0:T(8,128)(2,1)S(1)}, u32[]{:S(2)}, u32[]{:S(2)}) collective-permute-start(bf16[1040,128]{1,0:T(8,128)(2,1)S(1)} %get-tuple-element.32), channel_id=1, source_target_pairs={{0,15},{1,2},{2,1},{3,4},{4,3},{5,6},{6,5},{7,8},{8,7},{9,10},{10,... | collective-permute-start | bytes 798728 | tf_op jit(solution)/shard_map/ppermute | solution.py:312
  91.9 4.8 %collective-permute-start.2 = (bf16[1040,128]{1,0:T(8,128)(2,1)S(1)}, bf16[1040,128]{1,0:T(8,128)(2,1)S(1)}, u32[]{:S(2)}, u32[]{:S(2)}) collective-permute-start(bf16[1040,128]{1,0:T(8,128)(2,1)S(1)} %get-tuple-element.31), channel_id=1, source_target_pairs={{0,1},{1,0},{2,3},{3,2},{4,5},{5,4},{6,7},{7,6},{8,9},{9,8},{10,11... | collective-permute-start | bytes 798728 | tf_op jit(solution)/shard_map/ppermute | solution.py:330

commit v10 on v5

--- a/solution.py
+++ b/solution.py
@@ -149,18 +149,21 @@
     write_rows(1 - even_ref[0, 0], y_ref, mean, row_ref, col_ref, value_ref, prec_ref, cross_ref)
 
 
+def pair_kernel(even_ref, y_ref, observed_ref, row_ref, col_ref, value_ref, prec_ref, pair_ref, yt_ref):
+    write_rows(even_ref[0, 0], y_ref, observed_ref[0:1, :], row_ref, col_ref, value_ref, prec_ref, pair_ref)
+    yt_ref[...] = y_ref[...].T
+
+
 def own_kernel(
-    even_ref, mask_ref, local_ref, y_ref, observed_ref, row_ref, col_ref, value_ref, prec_ref,
-    pair_ref, anomaly_ref, yt_ref, mean_ref, gram_ref, cover_ref, across_ref, down_ref,
+    mask_ref, local_ref, y_ref, yt_ref, observed_ref, row_ref, col_ref, value_ref, prec_ref,
+    anomaly_ref, mean_ref, gram_ref, cover_ref, across_ref, down_ref,
 ):
-    write_rows(even_ref[0, 0], y_ref, observed_ref[0:1, :], row_ref, col_ref, value_ref, prec_ref, pair_ref)
     members, cells = local_ref.shape
     half = cells // 2
     local = local_ref[...].astype(F32)
     mean = jnp.sum(local, axis=0, keepdims=True) * (1.0 / members)
     mean_ref[...] = jnp.broadcast_to(mean, mean_ref.shape)
     anomaly_ref[...] = (local - mean).astype(BF16)
-    yt_ref[...] = y_ref[...].T
     gram_ref[...] = jnp.dot(yt_ref[...], y_ref[...], preferred_element_type=F32)
     cover_ref[...] = jnp.dot(yt_ref[...], anomaly_ref[...], preferred_element_type=F32)
 
@@ -308,24 +311,28 @@
         specs=[SMEM] + [VMEM] * 5,
     )
     cross_rows = lax.ppermute(cross_rows, "domain", crosses)
+    pair_rows, yt = call(
+        pair_kernel,
+        [rim, struct((cells // 2, total), BF16)],
+        [even, y, observed, obs_row, obs_col, obs_value, obs_prec],
+        specs=[SMEM] + [VMEM] * 6,
+        flops=10**9,
+    )
+    pair_rows = lax.ppermute(pair_rows, "domain", pairs)
     own = call(
         own_kernel,
         [
-            rim,
             struct((total, cells), BF16),
-            struct((cells // 2, total), BF16),
             struct((8, cells), F32),
             struct((cells // 2, cells // 2), F32),
             struct((cells // 2, cells), F32),
             struct((8, cells // 2), F32),
             struct((cells // 2, 128), F32),
         ],
-        [even, loc_mask, local, y, observed, obs_row, obs_col, obs_value, obs_prec],
-        specs=[SMEM] + [VMEM] * 8,
+        [loc_mask, local, y, yt, observed, obs_row, obs_col, obs_value, obs_prec],
         flops=2 * total * cells * cells * 3 // 4,
     )
-    pair_rows, anomalies, yt, mean, gram, cover, row, col = own
-    pair_rows = lax.ppermute(pair_rows, "domain", pairs)
+    anomalies, mean, gram, cover, row, col = own
     analysis = call(
         analyse_kernel,
         struct((total, cells), BF16),

time: 163 us -> 163 us (level)
    pallas_call x7 -> x8, Pallas kernels: 8.66 us -> 8.93 us  [call(): pl.pallas_call(kernel, out_shape=shapes, in_specs=specs or [VMEM] * len(a...]
where the time goes in v10:
time: 163 us; the launch traced here: 162 us
  blocking collectives  139 us (85%)
  starting transfers between devices  9.7 us (6%)
  Pallas kernels  8.93 us (5%)
  waiting for transfers between devices  3.38 us (2%)
    all_to_all x1, blocking collectives, on_device(): lax.all_to_all(predicted, 'member', split_axis=0, concat_axis=0, tiled=True)  78 us
    all_to_all x1, blocking collectives, on_device(): lax.all_to_all(analysis.reshape(bands, members, cells), 'member', split_a...  60.8 us
    pallas_call x8, Pallas kernels, call(): pl.pallas_call(kernel, out_shape=shapes, in_specs=specs or [VMEM] * len(a...  8.93 us
    ppermute x1, starting transfers between devices, on_device(): pair_edge = lax.ppermute(pair_edge, 'domain', pairs)  3.93 us
  transfers between devices with their start and end apart: 4, of which 2 were waited for; matrix products, arithmetic and copies ran while one was open for 0% of the time, Pallas kernels for 2%

profile of v10, /device:TPU:32, one launch (start us, length us, event | category | flops | bytes accessed | tf_op | source)
XLA Modules:
  0.0 162.2 jit_solution(11450882315378806584)
XLA Ops:
  0.0 0.0 copy-start
  0.0 1.2 copy-done
  1.2 0.4 shard_map.65
  1.6 1.9 %collective-permute-start.1 = (f32[8,512]{1,0:T(8,128)S(1)}, f32[8,512]{1,0:T(8,128)S(1)}, u32[]{:S(2)}, u32[]{:S(2)}) collective-permute-start(f32[8,512]{1,0:T(8,128)S(1)} %shard_map.65), channel_id=1, source_target_pairs={{0,15},{1,2},{2,1},{3,4},{4,3},{5,6},{6,5},{7,8},{8,7},{9,10},{10,... | collective-permute-start | bytes 49160 | tf_op jit(solution)/shard_map/ppermute | solution.py:288
  3.5 1.5 shard_map.64
  5.0 3.9 %collective-permute-start = (f32[8,512]{1,0:T(8,128)S(1)}, f32[8,512]{1,0:T(8,128)S(1)}, u32[]{:S(2)}, u32[]{:S(2)}) collective-permute-start(f32[8,512]{1,0:T(8,128)S(1)} %get-tuple-element.19), channel_id=1, source_target_pairs={{0,1},{1,0},{2,3},{3,2},{4,5},{5,4},{6,7},{7,6},{8,9},{9,8},{10,11... | collective-permute-start | bytes 49160 | tf_op jit(solution)/shard_map/ppermute | solution.py:296
  8.9 0.0 collective-permute-done.1.cross_ref
  8.9 0.8 collective-permute-done.pair_ref
  9.8 0.7 shard_map.66
  10.4 0.0 copy-start.1
  10.4 0.0 copy-start.2
  10.5 0.0 copy-start.3
  10.5 0.0 copy-start.4
  10.5 78.0 %all_to_all.10 = bf16[32,32,512]{2,1,0:T(8,128)(2,1)S(1)} all-to-all(bf16[32,32,512]{2,1,0:T(8,128)(2,1)S(1)} %shard_map.66), channel_id=1, replica_groups=mesh['member'=32,'domain'=16] {'member'}, dimensions={0} | all-to-all | bytes 2097152 | tf_op jit(solution)/shard_map/all_to_all | solution.py:304
  88.4 0.0 copy-done.1
  88.4 0.0 copy-done.2
  88.4 0.0 copy-done.3
  88.4 0.0 copy-done.4
  88.4 0.5 shard_map.67
  89.0 0.0 copy-start.5
  89.0 1.9 %collective-permute-start.3 = (bf16[1040,128]{1,0:T(8,128)(2,1)S(1)}, bf16[1040,128]{1,0:T(8,128)(2,1)S(1)}, u32[]{:S(2)}, u32[]{:S(2)}) collective-permute-start(bf16[1040,128]{1,0:T(8,128)(2,1)S(1)} %get-tuple-element.30), channel_id=1, source_target_pairs={{0,15},{1,2},{2,1},{3,4},{4,3},{5,6},{6,5},{7,8},{8,7},{9,10},{10,... | collective-permute-start | bytes 798728 | tf_op jit(solution)/shard_map/ppermute | solution.py:313
  90.9 0.3 shard_map.68
  91.2 1.9 %collective-permute-start.2 = (bf16[1040,128]{1,0:T(8,128)(2,1)S(1)}, bf16[1040,128]{1,0:T(8,128)(2,1)S(1)}, u32[]{:S(2)}, u32[]{:S(2)}) collective-permute-start(bf16[1040,128]{1,0:T(8,128)(2,1)S(1)} %get-tuple-element.29), channel_id=1, source_target_pairs={{0,1},{1,0},{2,3},{3,2},{4,5},{5,4},{6,7},{7,6},{8,9},{9,8},{10,11... | collective-permute-start | bytes 798728 | tf_op jit(solution)/shard_map/ppermute | solution.py:321
  93.2 0.0 copy-done.5
  93.2 1.0 shard_map.69
  94.1 2.6 %collective-permute-done.3.cross_ref = bf16[1040,128]{1,0:T(8,128)(2,1)S(1)} collective-permute-done((bf16[1040,128]{1,0:T(8,128)(2,1)S(1)}, bf16[1040,128]{1,0:T(8,128)(2,1)S(1)}, u32[]{:S(2)}, u32[]{:S(2)}) %collective-permute-start.3) | collective-permute-done | bytes 266272 | tf_op jit(solution)/shard_map/ppermute | solution.py:313
  96.7 0.0 collective-permute-done.2.pair_ref
  96.7 3.6 %shard_map.70 = bf16[1024,512]{1,0:T(8,128)(2,1)S(1)} custom-call(s32[1,1]{1,0:T(1,128)} %bitcast.even_ref, s32[1,4]{1,0:T(1,128)S(1)} %copy-done.5, bf16[1024,512]{1,0:T(8,128)(2,1)S(1)} %get-tuple-element.23.anomaly_ref, bf16[1024,256]{1,0:T(8,128)(2,1)S(1)} %get-tuple-element.20.y_ref, bf16[256,1024]{1,0:T(8,128)(2,1)S(1)} %get-tuple-element.22.yt_ref, ...), custom_call_target="tpu_custom_call" | custom-call | flops 2147483648 | bytes 3571732 | tf_op jit(solution)/shard_map/pallas_call | solution.py:22
  100.3 60.8 %all_to_all.11.in_ref = bf16[32,32,512]{2,1,0:T(8,128)(2,1)S(1)} all-to-all(bf16[32,32,512]{2,1,0:T(8,128)(2,1)S(1)} %bitcast.5), channel_id=1, replica_groups=mesh['member'=32,'domain'=16] {'member'}, dimensions={0} | all-to-all | bytes 2097152 | tf_op jit(solution)/shard_map/all_to_all | solution.py:350
  161.1 1.1 shard_map.71
Async XLA Ops:
  0.0 1.2 copy-start
  1.6 7.3 %collective-permute-start.1 = (f32[8,512]{1,0:T(8,128)S(1)}, f32[8,512]{1,0:T(8,128)S(1)}, u32[]{:S(2)}, u32[]{:S(2)}) collective-permute-start(f32[8,512]{1,0:T(8,128)S(1)} %shard_map.65), channel_id=1, source_target_pairs={{0,15},{1,2},{2,1},{3,4},{4,3},{5,6},{6,5},{7,8},{8,7},{9,10},{10,... | collective-permute-start | bytes 49160 | tf_op jit(solution)/shard_map/ppermute | solution.py:288
  5.0 4.8 %collective-permute-start = (f32[8,512]{1,0:T(8,128)S(1)}, f32[8,512]{1,0:T(8,128)S(1)}, u32[]{:S(2)}, u32[]{:S(2)}) collective-permute-start(f32[8,512]{1,0:T(8,128)S(1)} %get-tuple-element.19), channel_id=1, source_target_pairs={{0,1},{1,0},{2,3},{3,2},{4,5},{5,4},{6,7},{7,6},{8,9},{9,8},{10,11... | collective-permute-start | bytes 49160 | tf_op jit(solution)/shard_map/ppermute | solution.py:296
  10.4 78.0 %copy-start.1 = (s32[1,256]{1,0:T(1,128)S(1)}, s32[1,256]{1,0:T(1,128)}, u32[]{:S(2)}) copy-start(s32[1,256]{1,0:T(1,128)} %row_ref.5) | copy-start | bytes 3076
  10.4 78.0 %copy-start.2 = (s32[1,256]{1,0:T(1,128)S(1)}, s32[1,256]{1,0:T(1,128)}, u32[]{:S(2)}) copy-start(s32[1,256]{1,0:T(1,128)} %col_ref.5) | copy-start | bytes 3076
  10.5 78.0 %copy-start.3 = (f32[1,256]{1,0:T(1,128)S(1)}, f32[1,256]{1,0:T(1,128)}, u32[]{:S(2)}) copy-start(f32[1,256]{1,0:T(1,128)} %value_ref.5) | copy-start | bytes 3076
  10.5 78.0 %copy-start.4 = (f32[1,256]{1,0:T(1,128)S(1)}, f32[1,256]{1,0:T(1,128)}, u32[]{:S(2)}) copy-start(f32[1,256]{1,0:T(1,128)} %prec_ref.5) | copy-start | bytes 3076
  89.0 4.2 %copy-start.5 = (s32[1,4]{1,0:T(1,128)S(1)}, s32[1,4]{1,0:T(1,128)}, u32[]{:S(2)}) copy-start(s32[1,4]{1,0:T(1,128)} %mask_ref.3) | copy-start | bytes 52
  89.0 7.7 %collective-permute-start.3 = (bf16[1040,128]{1,0:T(8,128)(2,1)S(1)}, bf16[1040,128]{1,0:T(8,128)(2,1)S(1)}, u32[]{:S(2)}, u32[]{:S(2)}) collective-permute-start(bf16[1040,128]{1,0:T(8,128)(2,1)S(1)} %get-tuple-element.30), channel_id=1, source_target_pairs={{0,15},{1,2},{2,1},{3,4},{4,3},{5,6},{6,5},{7,8},{8,7},{9,10},{10,... | collective-permute-start | bytes 798728 | tf_op jit(solution)/shard_map/ppermute | solution.py:313
  91.2 5.5 %collective-permute-start.2 = (bf16[1040,128]{1,0:T(8,128)(2,1)S(1)}, bf16[1040,128]{1,0:T(8,128)(2,1)S(1)}, u32[]{:S(2)}, u32[]{:S(2)}) collective-permute-start(bf16[1040,128]{1,0:T(8,128)(2,1)S(1)} %get-tuple-element.29), channel_id=1, source_target_pairs={{0,1},{1,0},{2,3},{3,2},{4,5},{5,4},{6,7},{7,6},{8,9},{9,8},{10,11... | collective-permute-start | bytes 798728 | tf_op jit(solution)/shard_map/ppermute | solution.py:321
